TPU v7x, 512 devices: a whole 4x4x16 slice. The times are simulated.
512 devices in a mesh: section: 8 (over x, core), dp: 64 (over z, y).
Axes of the slice: x: 4, y: 4, z: 16, core: 2. Of those that a mesh axis runs over, the one named last changes fastest.
Arguments:
- teacher_hidden: bfloat16 [256, 8192], P('dp'), may hold values from -12 to 12
- student_hidden: bfloat16 [256, 3584], P('dp'), may hold values from -12 to 12
- teacher_gain: bfloat16 [8192], replicated, may hold values from 0.5 to 1.5
- student_gain: bfloat16 [3584], replicated, may hold values from 0.5 to 1.5
- teacher_head: bfloat16 [81920, 8192], P(('section', 'dp')), may hold values from -64 to 64
- student_head: bfloat16 [81920, 3584], P(('section', 'dp')), may hold values from -64 to 64
- labels: int32 [256], replicated, may hold values from 0 to 81919
- cotangent: float32 [256], replicated, may hold values from 2 to 20
Outputs:
- loss: float32 [], replicated
- student_grad: float32 [256, 3584], P('dp')
- gain_grad: float32 [3584], replicated
- head_grad: bfloat16 [81920, 3584], P(('section', 'dp'))
All inputs are finite; a program needn't handle non-finite values.
Results may differ from a plain program's by a relative error of at most 0.0079.
Values may be sent and summed in bfloat16 or wider, within the bound.
No kernel may reach another device: no remote copies, remote signals or barrier semaphores. Data moves between devices by JAX's collectives and lax.ppermute only.
A program may use at most 64 MiB of HBM per device.

v0:
```python
import functools

import jax
import jax.numpy as jnp
from jax import lax
from jax.sharding import Mesh
from jax.sharding import PartitionSpec as P

DP = ("dp_0", "dp_1")
SECTION_DP = ("section_0", "section_1", "dp_0", "dp_1")
SECTION = ("section_0", "section_1")


eps = 1e-06
ce_weight = 0.5


def side_by_side(arrays, axis, dim, along):
    both = jnp.concatenate(arrays, axis=along)
    out, at, gathered = (lax.all_gather(both, axis, axis=dim, tiled=True), 0, [])
    for a in arrays:
        gathered.append(lax.slice_in_dim(out, at, at + a.shape[along], axis=along))
        at += a.shape[along]
    return tuple(gathered)


def gathered_once(x, axis):
    leaves = jax.tree.leaves(x)
    turns = sorted(range(len(leaves)), key=lambda k: -leaves[k].size)
    width = (1, *leaves[turns[0]].shape)[-1]
    lines = [
        jnp.pad(leaves[k].reshape(-1), (0, -leaves[k].size % width)).reshape(-1, width)
        for k in turns
    ]
    both, at, found = (lax.all_gather(jnp.concatenate(lines), axis), 0, {})
    for k, line in zip(turns, lines):
        share = both[:, at : at + len(line)].reshape(len(both), -1)
        found[k] = share[:, : leaves[k].size].reshape(-1, *leaves[k].shape)
        at += len(line)
    numbers = iter(range(len(leaves)))
    return jax.tree.map(lambda _: found[next(numbers)], x)


def merged_by_axis(x, axes, combine):
    for axis in axes:
        pieces = gathered_once(x, axis)
        x = jax.tree.map(lambda part: part[0], pieces)
        for k in range(1, lax.axis_size(axis)):
            x = combine(x, jax.tree.map(lambda part: part[k], pieces))
    return x


def split_up(x, dim, length):
    before, after = (x.shape[:dim], x.shape[dim + 1 :])
    return jnp.moveaxis(x.reshape(*before, length, -1, *after), dim, 0)


def sent_and_summed(x, axis, dim):
    length = lax.axis_size(axis)
    tiles = lax.all_to_all(split_up(x, dim, length), axis, 0, 0, tiled=True)
    return jnp.sum(tiles.astype(jnp.float32), axis=0)


def sent_to_all(x, axis):
    length = lax.axis_size(axis)
    return lax.all_to_all(jnp.broadcast_to(x[None], (length, *x.shape)), axis, 0, 0, tiled=True)


def over_copies(x, axis):
    return sent_to_all(x, axis).sum(axis=0)


def by_axis(x, axes):
    return functools.reduce(lax.psum, axes, x)


def gather_turned(arrays, axis, dims):
    turned = [jnp.moveaxis(a, dim, 0) for a, dim in zip(arrays, dims)]
    widths = [t[0].size for t in turned]
    both = jnp.concatenate([t.reshape(-1, w) for t, w in zip(turned, widths)], axis=1)
    out = lax.all_gather(both, axis, axis=0, tiled=True)
    tiles = jnp.split(out, [sum(widths[:k]) for k in range(1, len(widths))], axis=1)
    return tuple(
        (
            jnp.moveaxis(b.reshape(-1, *t.shape[1:]), 0, dim)
            for b, t, dim in zip(tiles, turned, dims)
        )
    )


def normalize(hidden, gain):
    values = hidden.astype(jnp.float32)
    inverse = lax.rsqrt(jnp.mean(values * values, axis=-1, keepdims=True) + eps)
    scaled = values * inverse
    return (scaled, inverse, (scaled * gain.astype(jnp.float32)).astype(jnp.bfloat16))


def local_stats(teacher_logits, student_logits, picked_part):
    teacher_peak = jnp.max(teacher_logits, axis=1)
    student_peak = jnp.max(student_logits, axis=1)
    teacher_exp = jnp.exp(teacher_logits - teacher_peak[:, None])
    teacher_total = jnp.sum(teacher_exp, axis=1)
    cross = jnp.sum(teacher_exp * (teacher_logits - student_logits), axis=1)
    student_total = jnp.sum(jnp.exp(student_logits - student_peak[:, None]), axis=1)
    return (teacher_peak, teacher_total, cross, student_peak, student_total, picked_part)


def merge_stats(earlier, later):
    teacher_peak = jnp.maximum(earlier[0], later[0])
    first_scale = jnp.exp(earlier[0] - teacher_peak)
    second_scale = jnp.exp(later[0] - teacher_peak)
    student_peak = jnp.maximum(earlier[3], later[3])
    student_total = earlier[4] * jnp.exp(earlier[3] - student_peak) + later[4] * jnp.exp(
        later[3] - student_peak
    )
    return (
        teacher_peak,
        earlier[1] * first_scale + later[1] * second_scale,
        earlier[2] * first_scale + later[2] * second_scale,
        student_peak,
        student_total,
        earlier[5] + later[5],
    )


def on_device(
    teacher_hidden,
    student_hidden,
    teacher_gain,
    student_gain,
    teacher_head,
    student_head,
    labels,
    cotangent,
):
    _, _, teacher_normed = normalize(teacher_hidden, teacher_gain)
    scaled, inverse, student_normed = normalize(student_hidden, student_gain)
    teacher_rows, student_rows = side_by_side((teacher_normed, student_normed), DP, 0, 1)
    teacher_logits = lax.dot_general(
        teacher_rows, teacher_head, (((1,), (1,)), ((), ())), preferred_element_type=jnp.float32
    )
    student_logits = lax.dot_general(
        student_rows, student_head, (((1,), (1,)), ((), ())), preferred_element_type=jnp.float32
    )
    entries = student_head.shape[0]
    offset = lax.axis_index(SECTION_DP) * entries
    columns = lax.broadcasted_iota(jnp.int32, student_logits.shape, 1) + offset
    hits = columns == labels[:, None]
    picked_part = jnp.sum(jnp.where(hits, student_logits, 0.0), axis=1)
    stats = merged_by_axis(
        local_stats(teacher_logits, student_logits, picked_part), SECTION_DP, merge_stats
    )
    teacher_peak, teacher_total, cross, student_peak, student_total, picked = stats
    teacher_log = teacher_peak + jnp.log(teacher_total)
    student_log = student_peak + jnp.log(student_total)
    token_loss = (
        cross / teacher_total - teacher_log + student_log + ce_weight * (student_log - picked)
    )
    loss = jnp.mean(token_loss)
    student_prob = jnp.exp(student_logits - student_log[:, None])
    teacher_prob = jnp.exp(teacher_logits - teacher_log[:, None])
    onehot = jnp.where(hits, 1.0, 0.0).astype(jnp.float32)
    slope = (
        cotangent[:, None] * ((1.0 + ce_weight) * student_prob - teacher_prob - ce_weight * onehot)
    ).astype(jnp.bfloat16)
    head_grad = lax.dot_general(
        slope, student_rows, (((0,), (0,)), ((), ())), preferred_element_type=jnp.float32
    ).astype(jnp.bfloat16)
    grad_terms = jnp.dot(slope, student_head, preferred_element_type=jnp.float32)
    gain_values = student_gain.astype(jnp.float32)
    column_part = sent_and_summed(grad_terms.astype(jnp.bfloat16), SECTION, 1)
    normed_cols = sent_and_summed(column_part.astype(jnp.bfloat16), DP, 0)
    share = normed_cols.shape[1]
    start = lax.axis_index(SECTION) * share
    scaled_cols = lax.dynamic_slice_in_dim(scaled, start, share, 1)
    gain_cols = lax.dynamic_slice_in_dim(gain_values, start, share, 0)
    weighted = normed_cols * gain_cols
    inner = over_copies(jnp.sum(weighted * scaled_cols, axis=1), SECTION)
    grad_cols = inverse * (weighted - scaled_cols * (inner / scaled.shape[1])[:, None])
    gain_part = by_axis(jnp.sum(normed_cols * scaled_cols, axis=0), DP)
    student_grad, gain_grad = gather_turned((grad_cols, gain_part), SECTION, (1, 0))
    return (loss, student_grad, gain_grad, head_grad)


def solution(mesh):
    finer = Mesh(mesh.devices.reshape(4, 2, 16, 4), ("section_0", "section_1", "dp_0", "dp_1"))
    placed = (
        P(DP, None),
        P(DP, None),
        P(),
        P(),
        P(SECTION_DP, None),
        P(SECTION_DP, None),
        P(),
        P(),
    )
    return jax.shard_map(
        on_device,
        mesh=finer,
        in_specs=placed,
        out_specs=(P(), P(DP, None), P(), P(SECTION_DP, None)),
        check_vma=False,
    )
```

profile of v0, /device:TPU:1, one launch (start us, length us, event | category | flops | bytes accessed | tf_op | source)
XLA Modules:
  0.0 376.8 jit_solution(194016077905394936)
XLA Ops:
  7.2 0.0 copy-start
  7.2 0.0 all-gather.12.cloned.1.call-start
  7.2 1.0 fusion.14
  8.3 0.7 convert_element_type.37
  9.0 0.7 convert_element_type.34
  9.7 1.0 fusion.11
  10.7 0.8 convert_multiply_fusion.2
  11.6 0.9 fusion.13
  12.5 0.7 maximum_bitcast_fusion
  13.2 0.0 all-gather.12.cloned.1.call-update
  13.3 148.4 %all-gather.12.cloned.1.call-done = bf16[64,4,11776]{2,1,0:T(4,128)(2,1)} async-done(((bf16[1,4,11776]{2,1,0:T(4,128)(2,1)}), bf16[64,4,11776]{2,1,0:T(4,128)(2,1)}) %all-gather.12.cloned.1.call-update) | async-done | bytes 6029328 | tf_op jit(solution)/shard_map/all_gather | solution.py:20
  161.7 10.3 %reshape.3256 = bf16[256,11776]{1,0:T(8,128)(2,1)} reshape(bf16[64,4,11776]{2,1,0:T(4,128)(2,1)} %all-gather.12.cloned.1.call-done) | data formatting | bytes 12058624
  171.9 0.0 copy-done
  171.9 0.0 copy-start.1
  171.9 3.8 %fusion.247 = (f32[256]{0:T(256)S(1)}, f32[256,160]{0,1:T(8,128)S(1)}) fusion(bf16[160,8192]{1,0:T(8,128)(2,1)S(1)} %copy-done, bf16[256,11776]{1,0:T(8,128)(2,1)} %reshape.3256), kind=kOutput, calls=%fused_computation.443 | convolution fusion | flops 671129344 | bytes 6980608 | tf_op jit(solution)/shard_map/dot_general | solution.py:139
  175.8 0.0 copy-done.1
  175.8 0.0 copy-start.2
  175.8 0.0 copy-start.3
  175.8 2.3 fusion.248
  178.1 0.0 copy-done.2
  178.1 0.1 fusion.5
  178.2 9.3 %all-gather.5 = f32[4,6,256]{2,1,0:T(8,128)S(1)} all-gather(f32[1,6,256]{2,1,0:T(8,128)S(1)} %bitcast.1185), channel_id=2, replica_groups=mesh['section_0'=4,'section_1'=2,'dp_0'=16,'dp_1'=4] {'section_0'}, dimensions={0}, use_global_device_ids=true | all-gather | bytes 30720 | tf_op jit(solution)/shard_map/all_gather | solution.py:35
  187.7 13.4 %all-gather.6 = f32[2,6,256]{2,1,0:T(8,128)S(1)} all-gather(f32[1,6,256]{2,1,0:T(8,128)S(1)} %bitcast.1186), channel_id=3, replica_groups=mesh['section_0'=4,'section_1'=2,'dp_0'=16,'dp_1'=4] {'section_1'}, dimensions={0}, use_global_device_ids=true | all-gather | bytes 18432 | tf_op jit(solution)/shard_map/all_gather | solution.py:35
  201.2 21.6 %all-gather.7 = f32[16,6,256]{2,1,0:T(8,128)S(1)} all-gather(f32[1,6,256]{2,1,0:T(8,128)S(1)} %bitcast.1187), channel_id=4, replica_groups=mesh['section_0'=4,'section_1'=2,'dp_0'=16,'dp_1'=4] {'dp_0'}, dimensions={0}, use_global_device_ids=true | all-gather | bytes 104448 | tf_op jit(solution)/shard_map/all_gather | solution.py:35
  222.7 0.1 fusion.62
  222.8 0.1 fusion.17
  222.9 0.1 fusion.107
  223.0 9.0 %all-gather.8 = f32[4,6,256]{2,1,0:T(8,128)S(1)} all-gather(f32[1,6,256]{2,1,0:T(8,128)S(1)} %bitcast.1188), channel_id=5, replica_groups=mesh['section_0'=4,'section_1'=2,'dp_0'=16,'dp_1'=4] {'dp_1'}, dimensions={0}, use_global_device_ids=true | all-gather | bytes 30720 | tf_op jit(solution)/shard_map/all_gather | solution.py:35
  232.1 0.6 add_reduce_fusion
  232.7 0.0 copy-done.3
  232.7 0.1 fusion.9
  232.8 3.2 convolution_convert_fusion
  236.1 3.8 %copy.23 = bf16[256,3584]{0,1:T(8,128)(2,1)} copy(bf16[256,3584]{1,0:T(8,128)(2,1)} %convolution_convert_fusion) | data formatting | bytes 3670016 | tf_op jit(solution)/shard_map/convert_element_type | solution.py:171
  239.8 38.4 %all_to_all.16 = bf16[8,256,448]{1,2,0:T(8,128)(2,1)} all-to-all(bf16[8,256,448]{1,2,0:T(8,128)(2,1)} %bitcast.1184), channel_id=1, replica_groups=mesh['section_0'=4,'section_1'=2,'dp_0'=16,'dp_1'=4] {'section_0','secti..., dimensions={0} | all-to-all | bytes 3670016 | tf_op jit(solution)/shard_map/all_to_all | solution.py:60
  278.2 1.8 reduce_sum.118
  280.0 0.1 copy.24
  280.2 0.8 reshape.3240
  281.0 8.2 %all-to-all-start.1 = ((bf16[64,4,448]{2,1,0:T(4,128)(2,1)}), bf16[64,4,448]{2,1,0:T(4,128)(2,1)S(1)}, u32[]{:S(2)}, u32[]{:S(2)}) async-start(bf16[64,4,448]{2,1,0:T(4,128)(2,1)} %reshape.3240), calls=%async_computation.1 | async-start | bytes 524288 | tf_op jit(solution)/shard_map/all_to_all | solution.py:60
  289.2 0.8 dynamic_slice.6
  290.6 3.0 convolution_convert_fusion.1
  293.6 14.5 %all-to-all-done.1 = bf16[64,4,448]{2,1,0:T(4,128)(2,1)S(1)} async-done(((bf16[64,4,448]{2,1,0:T(4,128)(2,1)}), bf16[64,4,448]{2,1,0:T(4,128)(2,1)S(1)}, u32[]{:S(2)}, u32[]{:S(2)}) %all-to-all-start.1) | async-done | bytes 229408 | tf_op jit(solution)/shard_map/all_to_all | solution.py:60
  308.1 0.1 convert_reduce_fusion
  308.3 0.2 multiply_reduce_fusion.2
  308.5 21.6 %psum.14 = f32[448]{0:T(512)S(1)} all-reduce(f32[448]{0:T(512)S(1)} %get-tuple-element.11), channel_id=1, replica_groups=mesh['section_0'=4,'section_1'=2,'dp_0'=16,'dp_1'=4] {'dp_0'}, use_global_device_ids=true, to_apply=%region_14.15 | all-reduce | flops 448 | bytes 3584 | tf_op jit(solution)/shard_map/psum | solution.py:74
  330.1 0.6 broadcast_in_dim.12
  330.6 14.2 %all-to-all-start.2 = ((f32[8,1,4]{2,1,0:T(1,128)}), f32[8,1,4]{2,1,0:T(1,128)S(1)}, u32[]{:S(2)}, u32[]{:S(2)}) async-start(f32[8,1,4]{2,1,0:T(1,128)} %broadcast_in_dim.12), calls=%async_computation.2 | async-start | bytes 8192 | tf_op jit(solution)/shard_map/all_to_all | solution.py:66
  344.8 6.9 %psum.15 = f32[448,1]{0,1:T(1,128)S(1)} all-reduce(f32[448,1]{0,1:T(1,128)S(1)} %bitcast.1205), channel_id=1, replica_groups=mesh['section_0'=4,'section_1'=2,'dp_0'=16,'dp_1'=4] {'dp_1'}, use_global_device_ids=true, to_apply=%region_15.16 | all-reduce | flops 448 | bytes 3584 | tf_op jit(solution)/shard_map/psum | solution.py:74
  351.8 0.0 all-to-all-done.2
  351.8 0.1 multiply_bitcast_fusion
  351.9 15.5 %all-gather.9 = f32[8,448,5]{1,2,0:T(8,128)S(1)} all-gather(f32[1,448,5]{1,2,0:T(8,128)S(1)} %maximum_bitcast_fusion.1), channel_id=1, replica_groups=mesh['section_0'=4,'section_1'=2,'dp_0'=16,'dp_1'=4] {'section_0','secti..., dimensions={0}, use_global_device_ids=true | all-gather | bytes 80640 | tf_op jit(solution)/shard_map/all_gather | solution.py:81
  367.4 0.1 copy.26
  367.4 0.1 reshape.3266
  367.5 0.6 slice_bitcast_fusion
  368.1 0.6 slice_reduce_fusion
  (20 shorter events, 0.3 us)
Async XLA Ops:
  7.2 164.8 %copy-start = (bf16[160,8192]{1,0:T(8,128)(2,1)S(1)}, bf16[160,8192]{1,0:T(8,128)(2,1)}, u32[]{:S(2)}) copy-start(bf16[160,8192]{1,0:T(8,128)(2,1)} %param.12) | copy-start | bytes 7864324
  7.2 154.5 %all-gather.12.cloned.1.call-start = ((), (), s32[]{:S(2)}) async-start(), calls=%async_computation.3 | async-start | bytes 6123520 | tf_op jit(solution)/shard_map/all_gather | solution.py:20
  171.9 3.8 %copy-start.1 = (bf16[160,3584]{1,0:T(8,128)(2,1)S(1)}, bf16[160,3584]{1,0:T(8,128)(2,1)}, u32[]{:S(2)}) copy-start(bf16[160,3584]{1,0:T(8,128)(2,1)} %param.13) | copy-start | bytes 3440644
  175.8 2.3 copy-start.2
  175.8 56.9 %copy-start.3 = (f32[256]{0:T(256)S(1)}, f32[256]{0:T(256)}, u32[]{:S(2)}) copy-start(f32[256]{0:T(256)} %param.15) | copy-start | bytes 3076
  281.0 27.2 %all-to-all-start.1 = ((bf16[64,4,448]{2,1,0:T(4,128)(2,1)}), bf16[64,4,448]{2,1,0:T(4,128)(2,1)S(1)}, u32[]{:S(2)}, u32[]{:S(2)}) async-start(bf16[64,4,448]{2,1,0:T(4,128)(2,1)} %reshape.3240), calls=%async_computation.1 | async-start | bytes 524288 | tf_op jit(solution)/shard_map/all_to_all | solution.py:60
  330.6 21.1 %all-to-all-start.2 = ((f32[8,1,4]{2,1,0:T(1,128)}), f32[8,1,4]{2,1,0:T(1,128)S(1)}, u32[]{:S(2)}, u32[]{:S(2)}) async-start(f32[8,1,4]{2,1,0:T(1,128)} %broadcast_in_dim.12), calls=%async_computation.2 | async-start | bytes 8192 | tf_op jit(solution)/shard_map/all_to_all | solution.py:66
Sparse Core Ops, SparseCore 0:
  13.3 148.2 all-gather.11
where the time goes:
time: 378 us; the launch traced here: 377 us
  waiting for transfers between devices  163 us (43%)
  blocking collectives  136 us (36%)
  starting transfers between devices  22.4 us (6%)
  local copies, waits for them, and re-layouts  17.9 us (5%)
  between operations  16 us (4%)
  matrix products  12.3 us (3%)
  other arithmetic  9.46 us (3%)
    all_gather x1, waiting for transfers between devices, side_by_side(): lax.all_gather(both, axis, axis=dim, tiled=True)  148 us
    all_gather x4, blocking collectives, gathered_once(): both, at, found = (lax.all_gather(jnp.concatenate(lines), axis), 0, {})  53.3 us
    all_to_all x1, blocking collectives, sent_and_summed(): tiles = lax.all_to_all(split_up(x, dim, length), axis, 0, 0, tiled=True)  38.4 us
    psum x2, blocking collectives, by_axis(): return functools.reduce(lax.psum, axes, x)  28.5 us
    all_gather x1, blocking collectives, gather_turned(): out = lax.all_gather(both, axis, axis=0, tiled=True)  15.5 us
    all_to_all x1, waiting for transfers between devices, sent_and_summed(): tiles = lax.all_to_all(split_up(x, dim, length), axis, 0, 0, tiled=True)  14.5 us
    all_to_all x1, starting transfers between devices, sent_to_all(): lax.all_to_all(jnp.broadcast_to(x[None], (length, *x.shape)), axis, 0, 0,...  14.2 us
    unnamed x10, local copies, waits for them, and re-layouts  10.4 us
  transfers between devices with their start and end apart: 3, of which 2 were waited for; matrix products, arithmetic and copies ran while one was open for 1% of the time, Pallas kernels for 0%

commit v1 on v0

v1 whole, which is shorter than its diff:
```python
import jax
import jax.numpy as jnp
from jax import lax
from jax.sharding import Mesh
from jax.sharding import PartitionSpec as P

X, C, Z, Y = ("section_0", "section_1", "dp_0", "dp_1")
DP = (Z, Y)
SECTION_DP = (X, C, Z, Y)
PLANE = (X, Y)

eps = 1e-06
ce_weight = 0.5
f32 = jnp.float32
bf16 = jnp.bfloat16


def to_all(x, axes):
    length = lax.axis_size(axes)
    return lax.all_to_all(jnp.broadcast_to(x[None], (length, *x.shape)), axes, 0, 0, tiled=True)


def swapped(x):
    return lax.ppermute(x, C, [(0, 1), (1, 0)])


def normalize(hidden):
    values = hidden.astype(f32)
    inverse = lax.rsqrt(jnp.mean(values * values, axis=-1, keepdims=True) + eps)
    return (values * inverse, inverse)


def merged(logs):
    peak = jnp.max(logs, axis=0)
    return peak + jnp.log(jnp.sum(jnp.exp(logs - peak[None]), axis=0))


def high_low(x):
    high = x.astype(bf16)
    return (high, (x - high.astype(f32)).astype(bf16))


def dot(a, b, along_a, along_b):
    return lax.dot_general(a, b, (((along_a,), (along_b,)), ((), ())), preferred_element_type=f32)


def on_device(
    teacher_hidden,
    student_hidden,
    teacher_gain,
    student_gain,
    teacher_head,
    student_head,
    labels,
    cotangent,
):
    nx, nc, nz, ny = (lax.axis_size(a) for a in SECTION_DP)
    ix, ic, iz, iy = (lax.axis_index(a) for a in SECTION_DP)
    rows, dt = teacher_head.shape
    ds = student_head.shape[1]
    own = teacher_hidden.shape[0]
    half = own // nc
    qt, qs = (dt // nx, ds // nx)
    held = nz * half
    tokens = ny * held

    teacher_other, student_other = (swapped(teacher_head), swapped(student_head))

    t_scaled, _ = normalize(lax.dynamic_slice_in_dim(teacher_hidden, ic * half, half, 0))
    scaled, inverse = normalize(student_hidden)
    s_scaled = lax.dynamic_slice_in_dim(scaled, ic * half, half, 0)
    t_part = lax.dynamic_slice_in_dim(t_scaled, ix * qt, qt, 1)
    s_part = lax.dynamic_slice_in_dim(s_scaled, ix * qs, qs, 1)
    t_gain = lax.dynamic_slice_in_dim(teacher_gain, ix * qt, qt, 0).astype(f32)
    s_gain = lax.dynamic_slice_in_dim(student_gain, ix * qs, qs, 0).astype(f32)
    piece = jnp.concatenate(
        [(t_part * t_gain).astype(bf16), (s_part * s_gain).astype(bf16)], axis=1
    )
    line = to_all(piece, Z).reshape(held, qt + qs)
    plane = to_all(line, PLANE).reshape(nx, tokens, qt + qs)
    teacher_rows = jnp.concatenate([plane[k, :, :qt] for k in range(nx)], axis=1)
    student_rows = jnp.concatenate([plane[k, :, qt:] for k in range(nx)], axis=1)
    student_rows_other = swapped(student_rows)

    t_logits = jnp.concatenate(
        [dot(teacher_head, teacher_rows, 1, 1), dot(teacher_other, teacher_rows, 1, 1)], axis=0
    )
    s_logits = jnp.concatenate(
        [dot(student_head, student_rows, 1, 1), dot(student_other, student_rows, 1, 1)], axis=0
    )

    def local_log(logits):
        peak = jnp.max(logits, axis=0)
        return peak + jnp.log(jnp.sum(jnp.exp(logits - peak[None]), axis=0))

    logs = jnp.stack([local_log(t_logits), local_log(s_logits)])
    logs = merged(to_all(logs, PLANE))
    logs = merged(to_all(logs, Z))
    teacher_log, student_log = (logs[0], logs[1])

    def of_tokens(a):
        mine = lax.dynamic_index_in_dim(a.reshape(nz, ny, nc, half), ic, 2, keepdims=False)
        return mine.transpose(1, 0, 2).reshape(tokens)

    label, cot = (of_tokens(labels), of_tokens(cotangent))

    def start_of(core):
        return (((ix * nc + core) * nz + iz) * ny + iy) * rows

    first = lax.broadcasted_iota(jnp.int32, (rows, tokens), 0)
    entry = jnp.concatenate([first + start_of(ic), first + start_of(1 - ic)], axis=0)
    hits = entry == label[None, :]
    student_prob = jnp.exp(s_logits - student_log[None])
    teacher_prob = jnp.exp(t_logits - teacher_log[None])
    onehot = jnp.where(hits, 1.0, 0.0).astype(f32)
    slope = (
        cot[None] * ((1.0 + ce_weight) * student_prob - teacher_prob - ce_weight * onehot)
    ).astype(bf16)
    loss_part = jnp.sum(
        teacher_prob * (t_logits - s_logits) - ce_weight * jnp.where(hits, s_logits, 0.0)
    )
    loss_common = jnp.sum((1.0 + ce_weight) * student_log - teacher_log)

    slope_other = swapped(slope[rows:])

    terms = dot(slope[:rows], student_head, 0, 0) + dot(slope[rows:], student_other, 0, 0)
    gain_terms = jnp.sum(terms * student_rows.astype(f32), axis=0)
    gain_high, gain_low = (g.reshape(nx, 1, 1, qs) for g in high_low(gain_terms))
    loss_high, loss_low = high_low(loss_part)
    lane = lax.broadcasted_iota(jnp.int32, (nx, 1, 1, qs), 3)
    loss_row = jnp.where(lane == 0, loss_high, jnp.where(lane == 1, loss_low, 0)).astype(bf16)
    extra = jnp.concatenate([gain_high, gain_low, loss_row, jnp.zeros((nx, 1, 5, qs), bf16)], axis=2)
    extra = jnp.broadcast_to(extra, (nx, ny, 8, qs))
    sent = terms.astype(bf16).reshape(ny, held, nx, qs).transpose(2, 0, 1, 3)
    sent = jnp.concatenate([sent, extra], axis=2).reshape(nx * ny, held + 8, qs)
    got = lax.all_to_all(sent, PLANE, 0, 0, tiled=True).astype(f32).sum(axis=0)

    head_grad = (
        dot(slope[:rows], student_rows, 1, 0) + dot(slope_other, student_rows_other, 1, 0)
    ).astype(bf16)

    gain_row = got[held] + got[held + 1]
    loss_sum = got[held + 2, 0] + got[held + 2, 1]
    lane = lax.broadcasted_iota(jnp.int32, (qs,), 0)
    tail = jnp.stack([gain_row, jnp.where(lane == 0, loss_sum, 0.0)])
    tail = jnp.broadcast_to(tail[None], (nz, 2, qs))
    sent = jnp.concatenate([got[:held].reshape(nz, half, qs), tail], axis=1)
    got = lax.all_to_all(sent, Z, 0, 0, tiled=True).sum(axis=0)

    lane = lax.broadcasted_iota(jnp.int32, got.shape, 1)
    line_no = lax.broadcasted_iota(jnp.int32, got.shape, 0)
    got = jnp.where((lane == 0) & (line_no == half + 1), got + loss_common, got)
    whole = to_all(got, (X, C)).reshape(nx, nc, half + 2, qs)
    normed_grad = whole[:, :, :half].transpose(1, 2, 0, 3).reshape(own, ds)
    gain_values = student_gain.astype(f32)
    gain_grad = whole[:, :, half].sum(axis=1).reshape(ds) / gain_values
    loss = jnp.sum(whole[0, :, half + 1, 0]) / (tokens * nc)
    weighted = normed_grad * gain_values
    inner = jnp.mean(weighted * scaled, axis=1, keepdims=True)
    student_grad = inverse * (weighted - scaled * inner)
    return (loss, student_grad, gain_grad, head_grad)


def solution(mesh):
    finer = Mesh(mesh.devices.reshape(4, 2, 16, 4), SECTION_DP)
    placed = (
        P(DP, None),
        P(DP, None),
        P(),
        P(),
        P(SECTION_DP, None),
        P(SECTION_DP, None),
        P(),
        P(),
    )
    return jax.shard_map(
        on_device,
        mesh=finer,
        in_specs=placed,
        out_specs=(P(), P(DP, None), P(), P(SECTION_DP, None)),
        check_vma=False,
    )
```

time: 378 us -> 189 us (0.50)
  waiting for transfers between devices: 163 us -> 44.3 us
  blocking collectives: 136 us -> 43.3 us
  starting transfers between devices: 22.4 us -> 61.9 us
  between operations: 16 us -> 5.49 us
  local copies, waits for them, and re-layouts: 17.9 us -> 9.7 us
    all_gather x1 -> x0, waiting for transfers between devices: 148 us -> none  [side_by_side(): lax.all_gather(both, axis, axis=dim, tiled=True)]
    all_gather x5 -> x0, blocking collectives: 68.8 us -> none  [the longest x4 53.3 us: gathered_once(): both, at, found = (lax.all_gather(jnp.concatenate(lines), axis), 0, {})]
    all_to_all x2 -> x5, waiting for transfers between devices: 14.5 us -> 44.3 us  [the longest x4 44 us: to_all(): lax.all_to_all(jnp.broadcast_to(x[None], (length, *x.shape)), axes, 0, 0,...]
    psum x2 -> x0, blocking collectives: 28.5 us -> none  [by_axis(): return functools.reduce(lax.psum, axes, x)]
    all_to_all x2 -> x5, starting transfers between devices: 22.4 us -> 42.8 us  [the longest x4 39.3 us: to_all(): lax.all_to_all(jnp.broadcast_to(x[None], (length, *x.shape)), axes, 0, 0,...]
    ppermute x0 -> x4, starting transfers between devices: none -> 19.1 us  [swapped(): return lax.ppermute(x, C, [(0, 1), (1, 0)])]
    unnamed x10 -> x15, local copies, waits for them, and re-layouts: 10.4 us -> 2.58 us
    all_to_all x1 -> x2, blocking collectives: 38.4 us -> 43.3 us  [the longest x1 28 us: to_all(): lax.all_to_all(jnp.broadcast_to(x[None], (length, *x.shape)), axes, 0, 0,...]
  transfers between devices with their start and end apart: 3 -> 9, of which waited for: 2 -> 5; matrix products, arithmetic and copies ran while one was open for 1% -> 7% of each run, Pallas kernels for 0% -> 0%
where the time goes in v1:
time: 189 us; the launch traced here: 188 us
  starting transfers between devices  61.9 us (33%)
  waiting for transfers between devices  44.3 us (23%)
  blocking collectives  43.3 us (23%)
  other arithmetic  12.4 us (7%)
  matrix products  11 us (6%)
  local copies, waits for them, and re-layouts  9.7 us (5%)
  between operations  5.49 us (3%)
    all_to_all x4, waiting for transfers between devices, to_all(): lax.all_to_all(jnp.broadcast_to(x[None], (length, *x.shape)), axes, 0, 0,...  44 us
    all_to_all x4, starting transfers between devices, to_all(): lax.all_to_all(jnp.broadcast_to(x[None], (length, *x.shape)), axes, 0, 0,...  39.3 us
    all_to_all x1, blocking collectives, to_all(): lax.all_to_all(jnp.broadcast_to(x[None], (length, *x.shape)), axes, 0, 0,...  28 us
    ppermute x4, starting transfers between devices, swapped(): return lax.ppermute(x, C, [(0, 1), (1, 0)])  19.1 us
    all_to_all x1, blocking collectives, on_device(): got = lax.all_to_all(sent, PLANE, 0, 0, tiled=True).astype(f32).sum(axis=0)  15.3 us
    dot_general x8, matrix products, dot(): lax.dot_general(a, b, (((along_a,), (along_b,)), ((), ())), preferred_ele...  11 us
    broadcast_in_dim x6, local copies, waits for them, and re-layouts, to_all(): jnp.broadcast_to(x[None], (length, *x.shape))  3.89 us
  transfers between devices with their start and end apart: 9, of which 5 were waited for; matrix products, arithmetic and copies ran while one was open for 7% of the time, Pallas kernels for 0%

profile of v1, /device:TPU:1, one launch (start us, length us, event | category | flops | bytes accessed | tf_op | source)
XLA Modules:
  0.0 188.1 jit_solution(14398986537496734143)
XLA Ops:
  0.6 0.9 dynamic-slice_convert_fusion
  1.5 1.0 multiply_reduce_fusion.1
  2.6 0.8 dynamic-slice_convert_fusion.2
  3.3 0.9 fusion.10
  4.2 0.8 convert_multiply_fusion
  5.1 0.7 dynamic-slice_convert_fusion.1
  5.8 0.1 fusion.16
  5.8 0.1 multiply_convert_fusion
  5.9 0.1 broadcast_in_dim.50
  6.0 28.0 %all_to_all.35 = bf16[16,2,2944]{2,1,0:T(2,128)(2,1)S(1)} all-to-all(bf16[16,2,2944]{2,1,0:T(2,128)(2,1)S(1)} %broadcast_in_dim.50), channel_id=1, replica_groups=mesh['section_0'=4,'section_1'=2,'dp_0'=16,'dp_1'=4] {'dp_0'}, dimensions={0} | all-to-all | bytes 376832 | tf_op jit(solution)/shard_map/all_to_all | solution.py:20
  34.1 1.8 broadcast_in_dim.52
  35.9 6.9 %all-to-all-start.1 = ((bf16[16,32,2944]{2,1,0:T(8,128)(2,1)}), bf16[16,32,2944]{2,1,0:T(8,128)(2,1)S(1)}, u32[]{:S(2)}, u32[]{:S(2)}) async-start(bf16[16,32,2944]{2,1,0:T(8,128)(2,1)} %broadcast_in_dim.52), calls=%async_computation.1 | async-start | bytes 6029312 | tf_op jit(solution)/shard_map/all_to_all | solution.py:20
  42.8 6.9 %collective-permute-start.1 = (bf16[160,8192]{1,0:T(8,128)(2,1)}, bf16[160,8192]{1,0:T(8,128)(2,1)}, u32[]{:S(2)}, u32[]{:S(2)}) collective-permute-start(bf16[160,8192]{1,0:T(8,128)(2,1)} %param.12), channel_id=1, source_target_pairs={{0,64},{64,0},{1,65},{65,1},{2,66},{66,2},{3,67},{67,3},{4,68},{68... | collective-permute-start | bytes 7864328 | tf_op jit(solution)/shard_map/ppermute | solution.py:24
  49.7 1.9 %collective-permute-start = (bf16[160,3584]{1,0:T(8,128)(2,1)}, bf16[160,3584]{1,0:T(8,128)(2,1)}, u32[]{:S(2)}, u32[]{:S(2)}) collective-permute-start(bf16[160,3584]{1,0:T(8,128)(2,1)} %param.13), channel_id=1, source_target_pairs={{0,64},{64,0},{1,65},{65,1},{2,66},{66,2},{3,67},{67,3},{4,68},{68... | collective-permute-start | bytes 3440648 | tf_op jit(solution)/shard_map/ppermute | solution.py:24
  51.7 0.2 reshape.235
  51.8 0.2 reshape.233
  52.1 24.6 %all-to-all-done.1 = bf16[16,32,2944]{2,1,0:T(8,128)(2,1)S(1)} async-done(((bf16[16,32,2944]{2,1,0:T(8,128)(2,1)}), bf16[16,32,2944]{2,1,0:T(8,128)(2,1)S(1)}, u32[]{:S(2)}, u32[]{:S(2)}) %all-to-all-start.1) | async-done | bytes 3014688 | tf_op jit(solution)/shard_map/all_to_all | solution.py:20
  76.7 0.3 slice_bitcast_fusion.3
  77.0 1.5 copy-done.6
  78.4 0.8 fusion.30
  79.3 2.6 %fusion.31 = (f32[128]{0:T(128)S(1)}, f32[128,160]{0,1:T(8,128)S(1)}) fusion(bf16[160,8192]{1,0:T(8,128)(2,1)} %collective-permute-done.1, bf16[128,2048]{1,0:T(8,128)(2,1)S(1)} %get-tuple-element.9, bf16[128,2048]{1,0:T(8,128)(2,1)S(1)} %get-tuple-element.10, bf16[128,2048]{1,0:T(8,128)(2,1)S(1)} %get-tuple-element.11, ...), kind=kOutput, calls=%fused_computation.98 | convolution fusion | flops 343953280 | bytes 4801024 | tf_op jit(solution)/shard_map/dot_general | solution.py:44
  82.1 1.1 copy-done
  83.2 0.5 fusion.28
  83.6 1.8 fusion.29
  85.6 0.6 broadcast_in_dim.90
  86.3 8.7 %all-to-all-start.2 = ((f32[16,2,128]{2,1,0:T(2,128)}), f32[16,2,128]{2,1,0:T(2,128)S(1)}, u32[]{:S(2)}, u32[]{:S(2)}) async-start(f32[16,2,128]{2,1,0:T(2,128)} %broadcast_in_dim.90), calls=%async_computation.2 | async-start | bytes 32768 | tf_op jit(solution)/shard_map/all_to_all | solution.py:20
  95.0 0.1 copy.55
  95.1 0.1 copy.56
  95.2 0.1 eq.53
  95.4 0.1 copy.49
  95.5 0.1 copy.50
  95.6 0.1 mul.131
  95.8 5.6 %all-to-all-done.2 = f32[16,2,128]{2,1,0:T(2,128)S(1)} async-done(((f32[16,2,128]{2,1,0:T(2,128)}), f32[16,2,128]{2,1,0:T(2,128)S(1)}, u32[]{:S(2)}, u32[]{:S(2)}) %all-to-all-start.2) | async-done | bytes 16416 | tf_op jit(solution)/shard_map/all_to_all | solution.py:20
  101.4 0.6 broadcast_in_dim.91
  102.1 12.9 %all-to-all-start.3 = ((f32[16,2,128]{2,1,0:T(2,128)}), f32[16,2,128]{2,1,0:T(2,128)S(1)}, u32[]{:S(2)}, u32[]{:S(2)}) async-start(f32[16,2,128]{2,1,0:T(2,128)} %broadcast_in_dim.91), calls=%async_computation.3 | async-start | bytes 32768 | tf_op jit(solution)/shard_map/all_to_all | solution.py:20
  115.0 11.4 %all-to-all-done.3 = f32[16,2,128]{2,1,0:T(2,128)S(1)} async-done(((f32[16,2,128]{2,1,0:T(2,128)}), f32[16,2,128]{2,1,0:T(2,128)S(1)}, u32[]{:S(2)}, u32[]{:S(2)}) %all-to-all-start.3) | async-done | bytes 16416 | tf_op jit(solution)/shard_map/all_to_all | solution.py:20
  126.5 0.7 fusion.6
  127.2 0.4 fusion.13
  127.6 1.8 fusion.25
  129.4 0.2 reshape.236
  129.6 0.1 copy.75
  131.1 0.1 maximum_bitcast_fusion
  131.2 0.1 pad_maximum_fusion.1
  131.4 15.3 %all_to_all.36 = bf16[16,40,896]{2,1,0:T(8,128)(2,1)S(1)} all-to-all(bf16[16,40,896]{2,1,0:T(8,128)(2,1)S(1)} %bitcast.65), channel_id=1, replica_groups=mesh['section_0'=4,'section_1'=2,'dp_0'=16,'dp_1'=4] {'section_0','dp_1'}, dimensions={0} | all-to-all | bytes 2293760 | tf_op jit(solution)/shard_map/all_to_all | solution.py:136
  146.7 0.2 convert_reduce_fusion
  146.9 0.6 fusion.26
  148.9 0.8 pad_maximum_fusion.5
  149.7 3.5 %all-to-all-start.5 = ((f32[16,4,896]{2,1,0:T(4,128)}), f32[16,4,896]{2,1,0:T(4,128)S(1)}, u32[]{:S(2)}, u32[]{:S(2)}) async-start(f32[16,4,896]{2,1,0:T(4,128)} %pad_maximum_fusion.5), calls=%async_computation.5 | async-start | bytes 458752 | tf_op jit(solution)/shard_map/all_to_all | solution.py:148
  153.2 8.4 %collective-permute-start.3 = (bf16[128,3584]{1,0:T(8,128)(2,1)S(1)}, bf16[128,3584]{1,0:T(8,128)(2,1)}, u32[]{:S(2)}, u32[]{:S(2)}) collective-permute-start(bf16[128,3584]{1,0:T(8,128)(2,1)S(1)} %pad_maximum_fusion.2), channel_id=1, source_target_pairs={{0,64},{64,0},{1,65},{65,1},{2,66},{66,2},{3,67},{67,3},{4,68},{68... | collective-permute-start | bytes 2752520 | tf_op jit(solution)/shard_map/ppermute | solution.py:24
  161.6 0.5 iota_compare_fusion.2
  162.2 0.6 slice.91
  162.8 1.9 %collective-permute-start.2 = (bf16[160,128]{1,0:T(8,128)(2,1)}, bf16[160,128]{1,0:T(8,128)(2,1)}, u32[]{:S(2)}, u32[]{:S(2)}) collective-permute-start(bf16[160,128]{1,0:T(8,128)(2,1)} %slice.91), channel_id=1, source_target_pairs={{0,64},{64,0},{1,65},{65,1},{2,66},{66,2},{3,67},{67,3},{4,68},{68... | collective-permute-start | bytes 122888 | tf_op jit(solution)/shard_map/ppermute | solution.py:24
  164.7 0.6 subtract_reduce_fusion
  165.3 0.4 fusion.11
  165.7 0.2 all-to-all-done.5
  166.0 1.4 add_select_fusion
  167.4 0.7 broadcast_in_dim.103
  168.1 10.8 %all-to-all-start.6 = ((f32[8,4,896]{2,1,0:T(4,128)}), f32[8,4,896]{2,1,0:T(4,128)S(1)}, u32[]{:S(2)}, u32[]{:S(2)}) async-start(f32[8,4,896]{2,1,0:T(4,128)} %broadcast_in_dim.103), calls=%async_computation.6 | async-start | bytes 229376 | tf_op jit(solution)/shard_map/all_to_all | solution.py:20
  178.9 2.7 %fusion = bf16[160,3584]{1,0:T(8,128)(2,1)} fusion(f32[160,3584]{1,0:T(8,128)S(1)} %fusion.11, bf16[160,128]{1,0:T(8,128)(2,1)} %collective-permute-done.2, bf16[128,3584]{1,0:T(8,128)(2,1)} %collective-permute-done.3), kind=kOutput, calls=%fused_computation.2 | convolution fusion | flops 147947520 | bytes 4399104 | tf_op jit(solution)/shard_map/dot_general | solution.py:44
  181.5 2.5 %all-to-all-done.6 = f32[8,4,896]{2,1,0:T(4,128)S(1)} async-done(((f32[8,4,896]{2,1,0:T(4,128)}), f32[8,4,896]{2,1,0:T(4,128)S(1)}, u32[]{:S(2)}, u32[]{:S(2)}) %all-to-all-start.6) | async-done | bytes 114720 | tf_op jit(solution)/shard_map/all_to_all | solution.py:20
  184.1 0.6 slice_reduce_fusion.1
  184.8 0.2 multiply_reduce_fusion.2
  185.0 0.7 subtract_multiply_fusion
  185.7 0.6 convert_divide_fusion
  (61 shorter events, 1.2 us)
Async XLA Ops:
  35.9 15.7 %copy-start.4 = (s32[256]{0:T(256)S(1)}, s32[256]{0:T(256)}, u32[]{:S(2)}) copy-start(s32[256]{0:T(256)} %param.14) | copy-start | bytes 3076
  35.9 15.9 %copy-start.5 = (f32[256]{0:T(256)S(1)}, f32[256]{0:T(256)}, u32[]{:S(2)}) copy-start(f32[256]{0:T(256)} %param.15) | copy-start | bytes 3076
  35.9 40.8 %all-to-all-start.1 = ((bf16[16,32,2944]{2,1,0:T(8,128)(2,1)}), bf16[16,32,2944]{2,1,0:T(8,128)(2,1)S(1)}, u32[]{:S(2)}, u32[]{:S(2)}) async-start(bf16[16,32,2944]{2,1,0:T(8,128)(2,1)} %broadcast_in_dim.52), calls=%async_computation.1 | async-start | bytes 6029312 | tf_op jit(solution)/shard_map/all_to_all | solution.py:20
  42.8 36.5 %collective-permute-start.1 = (bf16[160,8192]{1,0:T(8,128)(2,1)}, bf16[160,8192]{1,0:T(8,128)(2,1)}, u32[]{:S(2)}, u32[]{:S(2)}) collective-permute-start(bf16[160,8192]{1,0:T(8,128)(2,1)} %param.12), channel_id=1, source_target_pairs={{0,64},{64,0},{1,65},{65,1},{2,66},{66,2},{3,67},{67,3},{4,68},{68... | collective-permute-start | bytes 7864328 | tf_op jit(solution)/shard_map/ppermute | solution.py:24
  49.7 33.9 %collective-permute-start = (bf16[160,3584]{1,0:T(8,128)(2,1)}, bf16[160,3584]{1,0:T(8,128)(2,1)}, u32[]{:S(2)}, u32[]{:S(2)}) collective-permute-start(bf16[160,3584]{1,0:T(8,128)(2,1)} %param.13), channel_id=1, source_target_pairs={{0,64},{64,0},{1,65},{65,1},{2,66},{66,2},{3,67},{67,3},{4,68},{68... | collective-permute-start | bytes 3440648 | tf_op jit(solution)/shard_map/ppermute | solution.py:24
  76.7 1.7 copy-start.6
  81.9 1.3 copy-start
  83.6 43.6 %copy-start.1 = (bf16[160,3584]{1,0:T(8,128)(2,1)S(1)}, bf16[160,3584]{1,0:T(8,128)(2,1)}, u32[]{:S(2)}) copy-start(bf16[160,3584]{1,0:T(8,128)(2,1)} %param.13) | copy-start | bytes 3440644
  86.3 15.1 %all-to-all-start.2 = ((f32[16,2,128]{2,1,0:T(2,128)}), f32[16,2,128]{2,1,0:T(2,128)S(1)}, u32[]{:S(2)}, u32[]{:S(2)}) async-start(f32[16,2,128]{2,1,0:T(2,128)} %broadcast_in_dim.90), calls=%async_computation.2 | async-start | bytes 32768 | tf_op jit(solution)/shard_map/all_to_all | solution.py:20
  102.1 24.3 %all-to-all-start.3 = ((f32[16,2,128]{2,1,0:T(2,128)}), f32[16,2,128]{2,1,0:T(2,128)S(1)}, u32[]{:S(2)}, u32[]{:S(2)}) async-start(f32[16,2,128]{2,1,0:T(2,128)} %broadcast_in_dim.91), calls=%async_computation.3 | async-start | bytes 32768 | tf_op jit(solution)/shard_map/all_to_all | solution.py:20
  131.4 30.3 %copy-start.3 = (bf16[3584]{0:T(1024)(128)(2,1)S(1)}, bf16[3584]{0:T(1024)(128)(2,1)}, u32[]{:S(2)}) copy-start(bf16[3584]{0:T(1024)(128)(2,1)} %param.11) | copy-start | bytes 21508
  149.7 16.3 %all-to-all-start.5 = ((f32[16,4,896]{2,1,0:T(4,128)}), f32[16,4,896]{2,1,0:T(4,128)S(1)}, u32[]{:S(2)}, u32[]{:S(2)}) async-start(f32[16,4,896]{2,1,0:T(4,128)} %pad_maximum_fusion.5), calls=%async_computation.5 | async-start | bytes 458752 | tf_op jit(solution)/shard_map/all_to_all | solution.py:148
  153.2 25.6 %collective-permute-start.3 = (bf16[128,3584]{1,0:T(8,128)(2,1)S(1)}, bf16[128,3584]{1,0:T(8,128)(2,1)}, u32[]{:S(2)}, u32[]{:S(2)}) collective-permute-start(bf16[128,3584]{1,0:T(8,128)(2,1)S(1)} %pad_maximum_fusion.2), channel_id=1, source_target_pairs={{0,64},{64,0},{1,65},{65,1},{2,66},{66,2},{3,67},{67,3},{4,68},{68... | collective-permute-start | bytes 2752520 | tf_op jit(solution)/shard_map/ppermute | solution.py:24
  162.8 16.1 %collective-permute-start.2 = (bf16[160,128]{1,0:T(8,128)(2,1)}, bf16[160,128]{1,0:T(8,128)(2,1)}, u32[]{:S(2)}, u32[]{:S(2)}) collective-permute-start(bf16[160,128]{1,0:T(8,128)(2,1)} %slice.91), channel_id=1, source_target_pairs={{0,64},{64,0},{1,65},{65,1},{2,66},{66,2},{3,67},{67,3},{4,68},{68... | collective-permute-start | bytes 122888 | tf_op jit(solution)/shard_map/ppermute | solution.py:24
  168.1 15.9 %all-to-all-start.6 = ((f32[8,4,896]{2,1,0:T(4,128)}), f32[8,4,896]{2,1,0:T(4,128)S(1)}, u32[]{:S(2)}, u32[]{:S(2)}) async-start(f32[8,4,896]{2,1,0:T(4,128)} %broadcast_in_dim.103), calls=%async_computation.6 | async-start | bytes 229376 | tf_op jit(solution)/shard_map/all_to_all | solution.py:20
  178.9 5.9 %copy-start.2 = (bf16[4,3584]{1,0:T(4,128)(2,1)S(1)}, bf16[4,3584]{1,0:T(4,128)(2,1)}, u32[]{:S(2)}) copy-start(bf16[4,3584]{1,0:T(4,128)(2,1)} %param.9) | copy-start | bytes 86020

commit v2 on v1

v2 whole, which is shorter than its diff:
```python
import jax
import jax.numpy as jnp
from jax import lax
from jax.experimental import pallas as pl
from jax.experimental.pallas import tpu as pltpu
from jax.sharding import Mesh
from jax.sharding import PartitionSpec as P

X, C, Z, Y = ("section_0", "section_1", "dp_0", "dp_1")
DP = (Z, Y)
SECTION_DP = (X, C, Z, Y)
PLANE = (X, Y)

eps = 1e-06
ce_weight = 0.5
f32 = jnp.float32
bf16 = jnp.bfloat16


def to_all(x, axes):
    length = lax.axis_size(axes)
    return lax.all_to_all(jnp.broadcast_to(x[None], (length, *x.shape)), axes, 0, 0, tiled=True)


def swapped(x):
    return lax.ppermute(x, C, [(0, 1), (1, 0)])


def shifted(x, k):
    length = lax.axis_size(X)
    return lax.ppermute(x, X, [(i, (i + k) % length) for i in range(length)])


def normalize(hidden):
    values = hidden.astype(f32)
    inverse = lax.rsqrt(jnp.mean(values * values, axis=-1, keepdims=True) + eps)
    return (values * inverse, inverse)


def merged(logs):
    peak = jnp.max(logs, axis=0)
    return peak + jnp.log(jnp.sum(jnp.exp(logs - peak[None]), axis=0))


def dot(a, b, along_a, along_b):
    return lax.dot_general(a, b, (((along_a,), (along_b,)), ((), ())), preferred_element_type=f32)


VMEM = pl.BlockSpec(memory_space=pltpu.VMEM)
SMEM = pl.BlockSpec(memory_space=pltpu.SMEM)
HBM = pl.BlockSpec(memory_space=pltpu.HBM)
MIB = 2**20


def column_log(logits):
    peak = jnp.max(logits, axis=0, keepdims=True)
    return peak + jnp.log(jnp.sum(jnp.exp(logits - peak), axis=0, keepdims=True))


def logits_kernel(
    place, a0, a1, a2, a3, b, t_own, t_other, s_own, s_other,
    t_logits, s_logits, logs, student_rows, teacher_rows, t0, t1, s0, s1, sems,
):
    copies = [
        pltpu.make_async_copy(src, dst, sems.at[k])
        for k, (src, dst) in enumerate(((t_own, t0), (t_other, t1), (s_own, s0), (s_other, s1)))
    ]
    for copy in copies:
        copy.start()
    nx = b.shape[1]
    qt = teacher_rows.shape[1] // nx
    qs = student_rows.shape[1] // nx
    half = a0.shape[0]
    for k, a in enumerate((a0, a1, a2, a3)):
        part = lax.rem(place[0] + (nx - k), nx)
        t_at = pl.ds(pl.multiple_of(part * qt, 128), qt)
        s_at = pl.ds(pl.multiple_of(part * qs, 128), qs)
        teacher_rows[0:half, t_at] = a[:, 0:qt]
        student_rows[0:half, s_at] = a[:, qt:]
        step = b.shape[2]
        for y in range(b.shape[0]):
            rows = slice(half + y * step, half + (y + 1) * step)
            teacher_rows[rows, t_at] = b[y, k, :, 0:qt]
            student_rows[rows, s_at] = b[y, k, :, qt:]
    rows = t0.shape[0]
    for k, head in enumerate((t0, t1)):
        copies[k].wait()
        total = 0.0
        for at in range(0, head.shape[1], 1024):
            total += dot(head[:, at : at + 1024], teacher_rows[:, at : at + 1024], 1, 1)
        t_logits[k * rows : (k + 1) * rows] = total
    for k, head in enumerate((s0, s1)):
        copies[2 + k].wait()
        total = 0.0
        for at in range(0, head.shape[1], 896):
            total += dot(head[:, at : at + 896], student_rows[:, at : at + 896], 1, 1)
        s_logits[k * rows : (k + 1) * rows] = total
    logs[0:1] = column_log(t_logits[...])
    logs[1:2] = column_log(s_logits[...])


def terms_kernel(
    place, got, t_logits, s_logits, label, cot, student_rows, s_own, s_other,
    slope, sent, common, s0, s1, sems,
):
    copies = [
        pltpu.make_async_copy(src, dst, sems.at[k])
        for k, (src, dst) in enumerate(((s_own, s0), (s_other, s1)))
    ]
    for copy in copies:
        copy.start()
    rows = s0.shape[0]
    nx, ny, held, _ = sent.shape
    step = held // 2
    qs = student_rows.shape[1] // nx
    half = ny * step
    teacher_log = column_log(got[:, 0, :])
    student_log = column_log(got[:, 1, :])
    common[...] = (1.0 + ce_weight) * student_log - teacher_log
    slopes = []
    loss_terms = 0.0
    for k in range(2):
        at = slice(k * rows, (k + 1) * rows)
        s_part, t_part = (s_logits[at], t_logits[at])
        entry = lax.broadcasted_iota(jnp.int32, s_part.shape, 0) + place[k]
        hits = entry == label[...]
        s_prob = jnp.exp(s_part - student_log)
        t_prob = jnp.exp(t_part - teacher_log)
        onehot = jnp.where(hits, 1.0, 0.0)
        value = cot[...] * ((1.0 + ce_weight) * s_prob - t_prob - ce_weight * onehot)
        slopes.append(value.astype(bf16))
        slope[at] = slopes[k]
        lost = t_prob * (t_part - s_part) - ce_weight * jnp.where(hits, s_part, 0.0)
        loss_terms += jnp.sum(lost, axis=0, keepdims=True)
    for copy in copies:
        copy.wait()
    line = lax.broadcasted_iota(jnp.int32, (step, 128), 0)
    loss_high = loss_terms.astype(bf16).astype(f32)
    for x in range(nx):
        at = slice(x * qs, (x + 1) * qs)
        terms = dot(slopes[0], s0[:, at], 0, 0) + dot(slopes[1], s1[:, at], 0, 0)
        gain = jnp.sum(terms * student_rows[:, at].astype(f32), axis=0, keepdims=True)
        high = gain.astype(bf16).astype(f32)
        tail = jnp.where(line == 14, loss_high, jnp.where(line == 15, loss_terms - loss_high, 0.0))
        for k in range(qs // 128):
            chunk = slice(k * 128, (k + 1) * 128)
            tail = jnp.where(line == k, high[:, chunk], tail)
            tail = jnp.where(line == 7 + k, (gain - high)[:, chunk], tail)
        terms = terms.astype(bf16)
        for y in range(ny):
            for k in range(2):
                sent[x, y, k * step : (k + 1) * step, 0:qs] = terms[
                    k * half + y * step : k * half + (y + 1) * step
                ]
            sent[x, y, 0:step, qs:] = tail.astype(bf16)
            sent[x, y, step:held, qs:] = jnp.zeros((held - step, 128), bf16)


def on_device(
    teacher_hidden,
    student_hidden,
    teacher_gain,
    student_gain,
    teacher_head,
    student_head,
    labels,
    cotangent,
):
    nx, nc, nz, ny = (lax.axis_size(a) for a in SECTION_DP)
    ix, ic, iz, iy = (lax.axis_index(a) for a in SECTION_DP)
    rows, dt = teacher_head.shape
    ds = student_head.shape[1]
    own = teacher_hidden.shape[0]
    half = own // nc
    qt, qs = (dt // nx, ds // nx)
    held = nz * half
    tokens = ny * held

    teacher_other, student_other = (swapped(teacher_head), swapped(student_head))

    t_scaled, _ = normalize(lax.dynamic_slice_in_dim(teacher_hidden, ic * half, half, 0))
    scaled, inverse = normalize(student_hidden)
    s_scaled = lax.dynamic_slice_in_dim(scaled, ic * half, half, 0)
    t_part = lax.dynamic_slice_in_dim(t_scaled, ix * qt, qt, 1)
    s_part = lax.dynamic_slice_in_dim(s_scaled, ix * qs, qs, 1)
    t_gain = lax.dynamic_slice_in_dim(teacher_gain, ix * qt, qt, 0).astype(f32)
    s_gain = lax.dynamic_slice_in_dim(student_gain, ix * qs, qs, 0).astype(f32)
    piece = jnp.concatenate(
        [(t_part * t_gain).astype(bf16), (s_part * s_gain).astype(bf16)], axis=1
    )
    line = to_all(piece, Z).reshape(held, qt + qs)

    first, second = (line[: held // 2], line[held // 2 :])
    second = jnp.stack([second] + [shifted(second, k) for k in range(1, nx)])
    first = to_all(first, Y).reshape(tokens // 2, qt + qs)
    first = [first] + [shifted(first, k) for k in range(1, nx)]
    second = to_all(second, Y)

    def of_tokens(a):
        mine = lax.dynamic_index_in_dim(a.reshape(2, nz // 2, ny, nc, half), ic, 3, keepdims=False)
        return mine.transpose(0, 2, 1, 3).reshape(1, tokens)

    def start_of(core):
        return (((ix * nc + core) * nz + iz) * ny + iy) * rows

    second, label, cot = lax.optimization_barrier((second, of_tokens(labels), of_tokens(cotangent)))

    shape = jax.ShapeDtypeStruct
    t_logits, s_logits, logs, student_rows = pl.pallas_call(
        logits_kernel,
        in_specs=[SMEM] + [VMEM] * 5 + [HBM] * 4,
        out_specs=[VMEM] * 4,
        out_shape=[
            shape((2 * rows, tokens), f32),
            shape((2 * rows, tokens), f32),
            shape((2, tokens), f32),
            shape((tokens, ds), bf16),
        ],
        scratch_shapes=[
            pltpu.VMEM((tokens, dt), bf16),
            pltpu.VMEM((rows, dt), bf16),
            pltpu.VMEM((rows, dt), bf16),
            pltpu.VMEM((rows, ds), bf16),
            pltpu.VMEM((rows, ds), bf16),
            pltpu.SemaphoreType.DMA((4,)),
        ],
        compiler_params=pltpu.CompilerParams(vmem_limit_bytes=20 * MIB),
    )(ix[None], *first, second, teacher_head, teacher_other, student_head, student_other)

    logs = merged(to_all(logs, PLANE))
    logs = to_all(logs, Z)

    slope, sent, common = pl.pallas_call(
        terms_kernel,
        in_specs=[SMEM] + [VMEM] * 6 + [HBM] * 2,
        out_specs=[VMEM] * 3,
        out_shape=[
            shape((2 * rows, tokens), bf16),
            shape((nx, ny, held, qs + 128), bf16),
            shape((1, tokens), f32),
        ],
        scratch_shapes=[
            pltpu.VMEM((rows, ds), bf16),
            pltpu.VMEM((rows, ds), bf16),
            pltpu.SemaphoreType.DMA((2,)),
        ],
        compiler_params=pltpu.CompilerParams(vmem_limit_bytes=12 * MIB),
    )(
        jnp.stack([start_of(ic), start_of(1 - ic)]),
        logs, t_logits, s_logits, label, cot, student_rows, student_head, student_other,
    )
    sent = sent.reshape(nx * ny, held, qs + 128)
    got = lax.all_to_all(sent, PLANE, 0, 0, tiled=True).astype(f32).sum(axis=0)

    student_rows, slope = lax.optimization_barrier((student_rows, slope))
    head_grad = (
        dot(slope[:rows], student_rows, 1, 0)
        + dot(swapped(slope[rows:]), swapped(student_rows), 1, 0)
    ).astype(bf16)

    tail = got[:16, qs:]
    tail = jnp.concatenate([tail[0:7] + tail[7:14], tail[14:15] + tail[15:16]]).reshape(2, 512)
    tail = jnp.broadcast_to(tail[None], (nz, half, 512))
    sent = jnp.concatenate([got[:, :qs].reshape(nz, half, qs), tail], axis=2)
    got = lax.all_to_all(sent, Z, 0, 0, tiled=True).sum(axis=0)

    whole = to_all(got, (X, C)).reshape(nx, nc, half, qs + 512)
    normed_grad = whole[:, :, :, :qs].transpose(1, 2, 0, 3).reshape(own, ds)
    tails = whole[:, :, :, qs:].sum(axis=1).reshape(nx, 8, 128)
    gain_values = student_gain.astype(f32)
    gain_grad = tails[:, :7].reshape(ds) / gain_values
    commons = common + swapped(common)
    loss = jnp.sum(tails[0, 7] + commons[0]) / (tokens * nc)
    weighted = normed_grad * gain_values
    inner = jnp.mean(weighted * scaled, axis=1, keepdims=True)
    student_grad = inverse * (weighted - scaled * inner)
    return (loss, student_grad, gain_grad, head_grad)


def solution(mesh):
    finer = Mesh(mesh.devices.reshape(4, 2, 16, 4), SECTION_DP)
    placed = (
        P(DP, None),
        P(DP, None),
        P(),
        P(),
        P(SECTION_DP, None),
        P(SECTION_DP, None),
        P(),
        P(),
    )
    return jax.shard_map(
        on_device,
        mesh=finer,
        in_specs=placed,
        out_specs=(P(), P(DP, None), P(), P(SECTION_DP, None)),
        check_vma=False,
    )
```

time: 189 us -> 195 us (1.032)
  blocking collectives: 43.3 us -> 0 us
  starting transfers between devices: 61.9 us -> 94.8 us
  waiting for transfers between devices: 44.3 us -> 59.3 us
  Pallas kernels: 0 us -> 9.51 us
  matrix products: 11 us -> 4.96 us
  other arithmetic: 12.4 us -> 8.67 us
  local copies, waits for them, and re-layouts: 9.7 us -> 13.3 us
  between operations: 5.49 us -> 2.9 us
    all_to_all x2 -> x0, blocking collectives: 43.3 us -> none  [the longest x1 28 us: to_all(): lax.all_to_all(jnp.broadcast_to(x[None], (length, *x.shape)), axes, 0, 0,...]
    ppermute x0 -> x6, starting transfers between devices: none -> 19 us  [shifted(): return lax.ppermute(x, X, [(i, (i + k) % length) for i in range(length)])]
    pallas_call x0 -> x2, Pallas kernels: none -> 9.51 us  [the longest x1 5.78 us: on_device(): pl.pallas_call(logits_kernel, in_specs=[SMEM] + [VMEM] * 5 + [HBM] * 4, o...]
    all_to_all x0 -> x1, waiting for transfers between devices: none -> 8.2 us  [on_device(): got = lax.all_to_all(sent, PLANE, 0, 0, tiled=True).astype(f32).sum(axis=0)]
    dot_general x8 -> x2, matrix products: 11 us -> 4.96 us  [dot(): lax.dot_general(a, b, (((along_a,), (along_b,)), ((), ())), preferred_ele...]
    all_to_all x4 -> x6, starting transfers between devices: 39.3 us -> 44.7 us  [to_all(): lax.all_to_all(jnp.broadcast_to(x[None], (length, *x.shape)), axes, 0, 0,...]
    ppermute x4 -> x5, starting transfers between devices: 19.1 us -> 24 us  [swapped(): return lax.ppermute(x, C, [(0, 1), (1, 0)])]
    unnamed x15 -> x27, local copies, waits for them, and re-layouts: 2.58 us -> 7.04 us
  transfers between devices with their start and end apart: 9 -> 19, of which waited for: 5 -> 10; matrix products, arithmetic and copies ran while one was open for 7% -> 6% of each run, Pallas kernels for 0% -> 0%
where the time goes in v2:
time: 195 us; the launch traced here: 193 us
  starting transfers between devices  94.8 us (49%)
  waiting for transfers between devices  59.3 us (30%)
  local copies, waits for them, and re-layouts  13.3 us (7%)
  Pallas kernels  9.51 us (5%)
  other arithmetic  8.67 us (4%)
  matrix products  4.96 us (3%)
  between operations  2.9 us (1%)
    all_to_all x6, waiting for transfers between devices, to_all(): lax.all_to_all(jnp.broadcast_to(x[None], (length, *x.shape)), axes, 0, 0,...  44.8 us
    all_to_all x6, starting transfers between devices, to_all(): lax.all_to_all(jnp.broadcast_to(x[None], (length, *x.shape)), axes, 0, 0,...  44.7 us
    ppermute x5, starting transfers between devices, swapped(): return lax.ppermute(x, C, [(0, 1), (1, 0)])  24 us
    ppermute x6, starting transfers between devices, shifted(): return lax.ppermute(x, X, [(i, (i + k) % length) for i in range(length)])  19 us
    all_to_all x1, waiting for transfers between devices, on_device(): got = lax.all_to_all(sent, PLANE, 0, 0, tiled=True).astype(f32).sum(axis=0)  8.2 us
    unnamed x27, local copies, waits for them, and re-layouts  7.04 us
    pallas_call x1, Pallas kernels, on_device(): pl.pallas_call(logits_kernel, in_specs=[SMEM] + [VMEM] * 5 + [HBM] * 4, o...  5.78 us
    dot_general x2, matrix products, dot(): lax.dot_general(a, b, (((along_a,), (along_b,)), ((), ())), preferred_ele...  4.96 us
  transfers between devices with their start and end apart: 19, of which 10 were waited for; matrix products, arithmetic and copies ran while one was open for 6% of the time, Pallas kernels for 0%

profile of v2, /device:TPU:1, one launch (start us, length us, event | category | flops | bytes accessed | tf_op | source)
XLA Modules:
  0.0 193.4 jit_solution(17246139667079881484)
XLA Ops:
  0.6 0.9 dynamic-slice_convert_fusion
  1.5 1.0 multiply_reduce_fusion
  2.5 0.9 fusion.1
  3.4 0.8 convert_multiply_fusion
  4.3 0.8 dynamic-slice_convert_fusion.2
  5.0 0.7 dynamic-slice_convert_fusion.1
  5.9 0.8 broadcast_in_dim.21
  6.7 15.7 %all-to-all-start = ((bf16[16,2,2944]{2,1,0:T(2,128)(2,1)}), bf16[16,2,2944]{2,1,0:T(2,128)(2,1)S(1)}, u32[]{:S(2)}, u32[]{:S(2)}) async-start(bf16[16,2,2944]{2,1,0:T(2,128)(2,1)} %broadcast_in_dim.21), calls=%async_computation | async-start | bytes 376832 | tf_op jit(solution)/shard_map/all_to_all | solution.py:22
  22.5 2.9 %collective-permute-start.6 = (bf16[160,8192]{1,0:T(8,128)(2,1)}, bf16[160,8192]{1,0:T(8,128)(2,1)}, u32[]{:S(2)}, u32[]{:S(2)}) collective-permute-start(bf16[160,8192]{1,0:T(8,128)(2,1)} %t_own.1), channel_id=1, source_target_pairs={{0,64},{64,0},{1,65},{65,1},{2,66},{66,2},{3,67},{67,3},{4,68},{68... | collective-permute-start | bytes 7864328 | tf_op jit(solution)/shard_map/ppermute | solution.py:26
  25.3 9.6 %all-to-all-done = bf16[16,2,2944]{2,1,0:T(2,128)(2,1)S(1)} async-done(((bf16[16,2,2944]{2,1,0:T(2,128)(2,1)}), bf16[16,2,2944]{2,1,0:T(2,128)(2,1)S(1)}, u32[]{:S(2)}, u32[]{:S(2)}) %all-to-all-start) | async-done | bytes 188448 | tf_op jit(solution)/shard_map/all_to_all | solution.py:22
  34.9 0.1 fusion.10
  35.1 4.4 %collective-permute-start.5 = (bf16[16,2944]{1,0:T(8,128)(2,1)S(1)}, bf16[16,2944]{1,0:T(8,128)(2,1)S(1)}, u32[]{:S(2)}, u32[]{:S(2)}) collective-permute-start(bf16[16,2944]{1,0:T(8,128)(2,1)S(1)} %slice.50), channel_id=1, source_target_pairs={{0,384},{128,0},{256,128},{384,256},{1,385},{129,1},{257,129},{385... | collective-permute-start | bytes 282632 | tf_op jit(solution)/shard_map/ppermute | solution.py:31
  39.5 2.4 %collective-permute-start.4 = (bf16[16,2944]{1,0:T(8,128)(2,1)S(1)}, bf16[16,2944]{1,0:T(8,128)(2,1)S(1)}, u32[]{:S(2)}, u32[]{:S(2)}) collective-permute-start(bf16[16,2944]{1,0:T(8,128)(2,1)S(1)} %slice.50), channel_id=1, source_target_pairs={{0,256},{128,384},{256,0},{384,128},{1,257},{129,385},{257,1},{385... | collective-permute-start | bytes 282632 | tf_op jit(solution)/shard_map/ppermute | solution.py:31
  41.9 2.5 %collective-permute-start.3 = (bf16[16,2944]{1,0:T(8,128)(2,1)S(1)}, bf16[16,2944]{1,0:T(8,128)(2,1)S(1)}, u32[]{:S(2)}, u32[]{:S(2)}) collective-permute-start(bf16[16,2944]{1,0:T(8,128)(2,1)S(1)} %slice.50), channel_id=1, source_target_pairs={{0,128},{128,256},{256,384},{384,0},{1,129},{129,257},{257,385},{3... | collective-permute-start | bytes 282632 | tf_op jit(solution)/shard_map/ppermute | solution.py:31
  44.4 7.4 %collective-permute-start.7 = (bf16[160,3584]{1,0:T(8,128)(2,1)}, bf16[160,3584]{1,0:T(8,128)(2,1)}, u32[]{:S(2)}, u32[]{:S(2)}) collective-permute-start(bf16[160,3584]{1,0:T(8,128)(2,1)} %s_own.3), channel_id=1, source_target_pairs={{0,64},{64,0},{1,65},{65,1},{2,66},{66,2},{3,67},{67,3},{4,68},{68... | collective-permute-start | bytes 3440648 | tf_op jit(solution)/shard_map/ppermute | solution.py:26
  52.0 0.8 broadcast_in_dim.23
  52.7 4.2 %all-to-all-start.1 = ((bf16[4,16,2944]{2,1,0:T(8,128)(2,1)}), bf16[4,16,2944]{2,1,0:T(8,128)(2,1)S(1)}, u32[]{:S(2)}, u32[]{:S(2)}) async-start(bf16[4,16,2944]{2,1,0:T(8,128)(2,1)} %broadcast_in_dim.23), calls=%async_computation.1 | async-start | bytes 753664 | tf_op jit(solution)/shard_map/all_to_all | solution.py:22
  57.0 7.6 %all-to-all-done.1 = bf16[4,16,2944]{2,1,0:T(8,128)(2,1)S(1)} async-done(((bf16[4,16,2944]{2,1,0:T(8,128)(2,1)}), bf16[4,16,2944]{2,1,0:T(8,128)(2,1)S(1)}, u32[]{:S(2)}, u32[]{:S(2)}) %all-to-all-start.1) | async-done | bytes 376864 | tf_op jit(solution)/shard_map/all_to_all | solution.py:22
  64.6 1.2 broadcast_in_dim.24
  65.9 3.6 %all-to-all-start.2 = ((bf16[4,4,16,2944]{3,2,1,0:T(8,128)(2,1)}), bf16[4,4,16,2944]{3,2,1,0:T(8,128)(2,1)S(1)}, u32[]{:S(2)}, u32[]{:S(2)}) async-start(bf16[4,4,16,2944]{3,2,1,0:T(8,128)(2,1)} %broadcast_in_dim.24), calls=%async_computation.2 | async-start | bytes 3014656 | tf_op jit(solution)/shard_map/all_to_all | solution.py:22
  69.5 3.4 %collective-permute-start = (bf16[64,2944]{1,0:T(8,128)(2,1)S(1)}, bf16[64,2944]{1,0:T(8,128)(2,1)S(1)}, u32[]{:S(2)}, u32[]{:S(2)}) collective-permute-start(bf16[64,2944]{1,0:T(8,128)(2,1)S(1)} %bitcast.36), channel_id=1, source_target_pairs={{0,128},{128,256},{256,384},{384,0},{1,129},{129,257},{257,385},{3... | collective-permute-start | bytes 1130504 | tf_op jit(solution)/shard_map/ppermute | solution.py:31
  72.9 3.6 %collective-permute-start.1 = (bf16[64,2944]{1,0:T(8,128)(2,1)S(1)}, bf16[64,2944]{1,0:T(8,128)(2,1)}, u32[]{:S(2)}, u32[]{:S(2)}) collective-permute-start(bf16[64,2944]{1,0:T(8,128)(2,1)S(1)} %bitcast.37), channel_id=1, source_target_pairs={{0,256},{128,384},{256,0},{384,128},{1,257},{129,385},{257,1},{385... | collective-permute-start | bytes 1130504 | tf_op jit(solution)/shard_map/ppermute | solution.py:31
  76.5 2.6 %collective-permute-start.2 = (bf16[64,2944]{1,0:T(8,128)(2,1)S(1)}, bf16[64,2944]{1,0:T(8,128)(2,1)}, u32[]{:S(2)}, u32[]{:S(2)}) collective-permute-start(bf16[64,2944]{1,0:T(8,128)(2,1)S(1)} %bitcast.38), channel_id=1, source_target_pairs={{0,384},{128,0},{256,128},{384,256},{1,385},{129,1},{257,129},{385... | collective-permute-start | bytes 1130504 | tf_op jit(solution)/shard_map/ppermute | solution.py:31
  79.1 0.2 reshape.83
  79.4 0.1 copy.42
  79.6 0.1 reshape.84.label
  79.8 0.2 reshape.85
  80.2 0.1 reshape.86.cot
  80.4 8.1 %all-to-all-done.2.b = bf16[4,4,16,2944]{3,2,1,0:T(8,128)(2,1)S(1)} async-done(((bf16[4,4,16,2944]{3,2,1,0:T(8,128)(2,1)}), bf16[4,4,16,2944]{3,2,1,0:T(8,128)(2,1)S(1)}, u32[]{:S(2)}, u32[]{:S(2)}) %all-to-all-start.2) | async-done | bytes 1507360 | tf_op jit(solution)/shard_map/all_to_all | solution.py:22
  88.5 2.0 %collective-permute-done.1.a2 = bf16[64,2944]{1,0:T(8,128)(2,1)} collective-permute-done((bf16[64,2944]{1,0:T(8,128)(2,1)S(1)}, bf16[64,2944]{1,0:T(8,128)(2,1)}, u32[]{:S(2)}, u32[]{:S(2)}) %collective-permute-start.1) | collective-permute-done | bytes 376864 | tf_op jit(solution)/shard_map/ppermute | solution.py:31
  90.5 2.3 %collective-permute-done.2.a3 = bf16[64,2944]{1,0:T(8,128)(2,1)} collective-permute-done((bf16[64,2944]{1,0:T(8,128)(2,1)S(1)}, bf16[64,2944]{1,0:T(8,128)(2,1)}, u32[]{:S(2)}, u32[]{:S(2)}) %collective-permute-start.2) | collective-permute-done | bytes 376864 | tf_op jit(solution)/shard_map/ppermute | solution.py:31
  92.8 1.7 copy-done.4
  94.5 5.8 %shard_map.111 = (f32[320,128]{1,0:T(8,128)S(1)}, f32[320,128]{1,0:T(8,128)S(1)}, f32[2,128]{1,0:T(2,128)S(1)}, bf16[128,3584]{1,0:T(8,128)(2,1)S(1)}) custom-call(s32[1]{0:T(128)} %bitcast.2.place, bf16[64,2944]{1,0:T(8,128)(2,1)S(1)} %bitcast.39, bf16[64,2944]{1,0:T(8,128)(2,1)S(1)} %collective-permute-done.a1, ...), custom_call_target="tpu_custom_call" | custom-call | tf_op jit(solution)/shard_map/pallas_call | solution.py:209
  100.3 0.9 copy-done.1
  101.3 0.7 copy-done.5
  101.9 0.7 copy-done.7
  102.6 0.6 broadcast_in_dim.25
  103.2 7.5 %all-to-all-start.3 = ((f32[16,2,128]{2,1,0:T(2,128)}), f32[16,2,128]{2,1,0:T(2,128)S(1)}, u32[]{:S(2)}, u32[]{:S(2)}) async-start(f32[16,2,128]{2,1,0:T(2,128)} %broadcast_in_dim.25), calls=%async_computation.3 | async-start | bytes 32768 | tf_op jit(solution)/shard_map/all_to_all | solution.py:22
  110.8 6.4 %all-to-all-done.3 = f32[16,2,128]{2,1,0:T(2,128)S(1)} async-done(((f32[16,2,128]{2,1,0:T(2,128)}), f32[16,2,128]{2,1,0:T(2,128)S(1)}, u32[]{:S(2)}, u32[]{:S(2)}) %all-to-all-start.3) | async-done | bytes 16416 | tf_op jit(solution)/shard_map/all_to_all | solution.py:22
  117.2 0.6 broadcast_in_dim.26
  117.9 4.5 %all-to-all-start.4 = ((f32[16,2,128]{2,1,0:T(2,128)}), f32[16,2,128]{2,1,0:T(2,128)S(1)}, u32[]{:S(2)}, u32[]{:S(2)}) async-start(f32[16,2,128]{2,1,0:T(2,128)} %broadcast_in_dim.26), calls=%async_computation.4 | async-start | bytes 32768 | tf_op jit(solution)/shard_map/all_to_all | solution.py:22
  122.5 11.3 %all-to-all-done.4.got = f32[16,2,128]{2,1,0:T(2,128)S(1)} async-done(((f32[16,2,128]{2,1,0:T(2,128)}), f32[16,2,128]{2,1,0:T(2,128)S(1)}, u32[]{:S(2)}, u32[]{:S(2)}) %all-to-all-start.4) | async-done | bytes 16416 | tf_op jit(solution)/shard_map/all_to_all | solution.py:22
  133.8 1.2 copy-done.2
  135.0 0.9 copy-done.6
  135.9 0.9 copy-done.8
  136.8 3.7 %shard_map.112 = (bf16[320,128]{1,0:T(8,128)(2,1)S(1)}, bf16[4,4,32,1024]{3,2,1,0:T(8,128)(2,1)}, f32[1,128]{1,0:T(1,128)S(1)}) custom-call(s32[2]{0:T(128)S(1)} %pad_add_fusion.place, f32[16,2,128]{2,1,0:T(2,128)S(1)} %all-to-all-done.4.got, f32[320,128]{1,0:T(8,128)S(1)} %copy-done.6, f32[320,128]{1,0:T(8,128)S(1)} %copy-done.8, ...), custom_call_target="tpu_custom_call" | custom-call | tf_op jit(solution)/shard_map/pallas_call | solution.py:233
  140.6 3.7 %all-to-all-start.5 = ((bf16[16,32,1024]{2,1,0:T(8,128)(2,1)}), bf16[16,32,1024]{2,1,0:T(8,128)(2,1)S(1)}, u32[]{:S(2)}, u32[]{:S(2)}) async-start(bf16[16,32,1024]{2,1,0:T(8,128)(2,1)} %bitcast.11), calls=%async_computation.5 | async-start | bytes 2097152 | tf_op jit(solution)/shard_map/all_to_all | solution.py:253
  144.3 5.3 %collective-permute-start.10 = (bf16[128,3584]{1,0:T(8,128)(2,1)S(1)}, bf16[128,3584]{1,0:T(8,128)(2,1)S(1)}, u32[]{:S(2)}, u32[]{:S(2)}) collective-permute-start(bf16[128,3584]{1,0:T(8,128)(2,1)S(1)} %copy-done.3), channel_id=1, source_target_pairs={{0,64},{64,0},{1,65},{65,1},{2,66},{66,2},{3,67},{67,3},{4,68},{68... | collective-permute-start | bytes 2752520 | tf_op jit(solution)/shard_map/ppermute | solution.py:26
  149.5 8.2 %all-to-all-done.5 = bf16[16,32,1024]{2,1,0:T(8,128)(2,1)S(1)} async-done(((bf16[16,32,1024]{2,1,0:T(8,128)(2,1)}), bf16[16,32,1024]{2,1,0:T(8,128)(2,1)S(1)}, u32[]{:S(2)}, u32[]{:S(2)}) %all-to-all-start.5) | async-done | bytes 1048608 | tf_op jit(solution)/shard_map/all_to_all | solution.py:253
  157.7 0.2 convert_reduce_fusion
  158.1 0.8 pad_maximum_fusion.1
  158.8 3.5 %all-to-all-start.6 = ((f32[16,2,1408]{2,1,0:T(2,128)}), f32[16,2,1408]{2,1,0:T(2,128)S(1)}, u32[]{:S(2)}, u32[]{:S(2)}) async-start(f32[16,2,1408]{2,1,0:T(2,128)} %pad_maximum_fusion.1), calls=%async_computation.6 | async-start | bytes 360448 | tf_op jit(solution)/shard_map/all_to_all | solution.py:265
  162.4 6.5 %collective-permute-start.9 = (bf16[160,128]{1,0:T(8,128)(2,1)S(1)}, bf16[160,128]{1,0:T(8,128)(2,1)S(1)}, u32[]{:S(2)}, u32[]{:S(2)}) collective-permute-start(bf16[160,128]{1,0:T(8,128)(2,1)S(1)} %slice.61), channel_id=1, source_target_pairs={{0,64},{64,0},{1,65},{65,1},{2,66},{66,2},{3,67},{67,3},{4,68},{68... | collective-permute-start | bytes 122888 | tf_op jit(solution)/shard_map/ppermute | solution.py:26
  168.9 1.8 fusion.2
  170.8 1.9 collective-permute-start.8
  172.7 1.9 all-to-all-done.6
  174.6 0.7 broadcast_in_dim.29
  175.3 9.1 %all-to-all-start.7 = ((f32[8,2,1408]{2,1,0:T(2,128)}), f32[8,2,1408]{2,1,0:T(2,128)S(1)}, u32[]{:S(2)}, u32[]{:S(2)}) async-start(f32[8,2,1408]{2,1,0:T(2,128)} %broadcast_in_dim.29), calls=%async_computation.7 | async-start | bytes 180224 | tf_op jit(solution)/shard_map/all_to_all | solution.py:22
  184.4 3.1 %fusion = bf16[160,3584]{1,0:T(8,128)(2,1)} fusion(f32[160,3584]{1,0:T(8,128)} %fusion.2, bf16[160,128]{1,0:T(8,128)(2,1)S(1)} %collective-permute-done.9, bf16[128,3584]{1,0:T(8,128)(2,1)S(1)} %collective-permute-done.10), kind=kOutput, calls=%fused_computation.1 | convolution fusion | flops 147947520 | bytes 4399104 | tf_op jit(solution)/shard_map/dot_general | solution.py:46
  187.5 1.8 all-to-all-done.7
  189.5 0.2 multiply_reduce_fusion.1
  189.7 0.7 subtract_multiply_fusion
  190.4 0.6 convert_divide_fusion
  191.0 0.6 fusion.9
  (63 shorter events, 1.3 us)
Async XLA Ops:
  6.7 28.2 %all-to-all-start = ((bf16[16,2,2944]{2,1,0:T(2,128)(2,1)}), bf16[16,2,2944]{2,1,0:T(2,128)(2,1)S(1)}, u32[]{:S(2)}, u32[]{:S(2)}) async-start(bf16[16,2,2944]{2,1,0:T(2,128)(2,1)} %broadcast_in_dim.21), calls=%async_computation | async-start | bytes 376832 | tf_op jit(solution)/shard_map/all_to_all | solution.py:22
  22.5 70.3 %collective-permute-start.6 = (bf16[160,8192]{1,0:T(8,128)(2,1)}, bf16[160,8192]{1,0:T(8,128)(2,1)}, u32[]{:S(2)}, u32[]{:S(2)}) collective-permute-start(bf16[160,8192]{1,0:T(8,128)(2,1)} %t_own.1), channel_id=1, source_target_pairs={{0,64},{64,0},{1,65},{65,1},{2,66},{66,2},{3,67},{67,3},{4,68},{68... | collective-permute-start | bytes 7864328 | tf_op jit(solution)/shard_map/ppermute | solution.py:26
  35.1 21.9 %collective-permute-start.5 = (bf16[16,2944]{1,0:T(8,128)(2,1)S(1)}, bf16[16,2944]{1,0:T(8,128)(2,1)S(1)}, u32[]{:S(2)}, u32[]{:S(2)}) collective-permute-start(bf16[16,2944]{1,0:T(8,128)(2,1)S(1)} %slice.50), channel_id=1, source_target_pairs={{0,384},{128,0},{256,128},{384,256},{1,385},{129,1},{257,129},{385... | collective-permute-start | bytes 282632 | tf_op jit(solution)/shard_map/ppermute | solution.py:31
  39.5 17.5 %collective-permute-start.4 = (bf16[16,2944]{1,0:T(8,128)(2,1)S(1)}, bf16[16,2944]{1,0:T(8,128)(2,1)S(1)}, u32[]{:S(2)}, u32[]{:S(2)}) collective-permute-start(bf16[16,2944]{1,0:T(8,128)(2,1)S(1)} %slice.50), channel_id=1, source_target_pairs={{0,256},{128,384},{256,0},{384,128},{1,257},{129,385},{257,1},{385... | collective-permute-start | bytes 282632 | tf_op jit(solution)/shard_map/ppermute | solution.py:31
  41.9 15.0 %collective-permute-start.3 = (bf16[16,2944]{1,0:T(8,128)(2,1)S(1)}, bf16[16,2944]{1,0:T(8,128)(2,1)S(1)}, u32[]{:S(2)}, u32[]{:S(2)}) collective-permute-start(bf16[16,2944]{1,0:T(8,128)(2,1)S(1)} %slice.50), channel_id=1, source_target_pairs={{0,128},{128,256},{256,384},{384,0},{1,129},{129,257},{257,385},{3... | collective-permute-start | bytes 282632 | tf_op jit(solution)/shard_map/ppermute | solution.py:31
  44.4 44.0 %collective-permute-start.7 = (bf16[160,3584]{1,0:T(8,128)(2,1)}, bf16[160,3584]{1,0:T(8,128)(2,1)}, u32[]{:S(2)}, u32[]{:S(2)}) collective-permute-start(bf16[160,3584]{1,0:T(8,128)(2,1)} %s_own.3), channel_id=1, source_target_pairs={{0,64},{64,0},{1,65},{65,1},{2,66},{66,2},{3,67},{67,3},{4,68},{68... | collective-permute-start | bytes 3440648 | tf_op jit(solution)/shard_map/ppermute | solution.py:26
  52.7 11.9 %all-to-all-start.1 = ((bf16[4,16,2944]{2,1,0:T(8,128)(2,1)}), bf16[4,16,2944]{2,1,0:T(8,128)(2,1)S(1)}, u32[]{:S(2)}, u32[]{:S(2)}) async-start(bf16[4,16,2944]{2,1,0:T(8,128)(2,1)} %broadcast_in_dim.23), calls=%async_computation.1 | async-start | bytes 753664 | tf_op jit(solution)/shard_map/all_to_all | solution.py:22
  57.0 22.1 %copy-start.11 = (s32[256]{0:T(256)S(1)}, s32[256]{0:T(256)}, u32[]{:S(2)}) copy-start(s32[256]{0:T(256)} %param.14) | copy-start | bytes 3076
  57.0 22.7 %copy-start.12 = (f32[256]{0:T(256)S(1)}, f32[256]{0:T(256)}, u32[]{:S(2)}) copy-start(f32[256]{0:T(256)} %param.15) | copy-start | bytes 3076
  57.0 35.8 %copy-start = (bf16[160,3584]{1,0:T(8,128)(2,1)S(1)}, bf16[160,3584]{1,0:T(8,128)(2,1)}, u32[]{:S(2)}) copy-start(bf16[160,3584]{1,0:T(8,128)(2,1)} %s_own.3) | copy-start | bytes 3440644
  65.9 22.6 %all-to-all-start.2 = ((bf16[4,4,16,2944]{3,2,1,0:T(8,128)(2,1)}), bf16[4,4,16,2944]{3,2,1,0:T(8,128)(2,1)S(1)}, u32[]{:S(2)}, u32[]{:S(2)}) async-start(bf16[4,4,16,2944]{3,2,1,0:T(8,128)(2,1)} %broadcast_in_dim.24), calls=%async_computation.2 | async-start | bytes 3014656 | tf_op jit(solution)/shard_map/all_to_all | solution.py:22
  69.5 19.0 %collective-permute-start = (bf16[64,2944]{1,0:T(8,128)(2,1)S(1)}, bf16[64,2944]{1,0:T(8,128)(2,1)S(1)}, u32[]{:S(2)}, u32[]{:S(2)}) collective-permute-start(bf16[64,2944]{1,0:T(8,128)(2,1)S(1)} %bitcast.36), channel_id=1, source_target_pairs={{0,128},{128,256},{256,384},{384,0},{1,129},{129,257},{257,385},{3... | collective-permute-start | bytes 1130504 | tf_op jit(solution)/shard_map/ppermute | solution.py:31
  72.9 17.6 %collective-permute-start.1 = (bf16[64,2944]{1,0:T(8,128)(2,1)S(1)}, bf16[64,2944]{1,0:T(8,128)(2,1)}, u32[]{:S(2)}, u32[]{:S(2)}) collective-permute-start(bf16[64,2944]{1,0:T(8,128)(2,1)S(1)} %bitcast.37), channel_id=1, source_target_pairs={{0,256},{128,384},{256,0},{384,128},{1,257},{129,385},{257,1},{385... | collective-permute-start | bytes 1130504 | tf_op jit(solution)/shard_map/ppermute | solution.py:31
  76.5 16.3 %collective-permute-start.2 = (bf16[64,2944]{1,0:T(8,128)(2,1)S(1)}, bf16[64,2944]{1,0:T(8,128)(2,1)}, u32[]{:S(2)}, u32[]{:S(2)}) collective-permute-start(bf16[64,2944]{1,0:T(8,128)(2,1)S(1)} %bitcast.38), channel_id=1, source_target_pairs={{0,384},{128,0},{256,128},{384,256},{1,385},{129,1},{257,129},{385... | collective-permute-start | bytes 1130504 | tf_op jit(solution)/shard_map/ppermute | solution.py:31
  92.8 1.7 copy-start.4
  100.3 0.9 copy-start.1
  101.3 0.7 copy-start.5
  101.9 0.7 copy-start.7
  103.2 14.0 %all-to-all-start.3 = ((f32[16,2,128]{2,1,0:T(2,128)}), f32[16,2,128]{2,1,0:T(2,128)S(1)}, u32[]{:S(2)}, u32[]{:S(2)}) async-start(f32[16,2,128]{2,1,0:T(2,128)} %broadcast_in_dim.25), calls=%async_computation.3 | async-start | bytes 32768 | tf_op jit(solution)/shard_map/all_to_all | solution.py:22
  117.9 15.9 %all-to-all-start.4 = ((f32[16,2,128]{2,1,0:T(2,128)}), f32[16,2,128]{2,1,0:T(2,128)S(1)}, u32[]{:S(2)}, u32[]{:S(2)}) async-start(f32[16,2,128]{2,1,0:T(2,128)} %broadcast_in_dim.26), calls=%async_computation.4 | async-start | bytes 32768 | tf_op jit(solution)/shard_map/all_to_all | solution.py:22
  133.8 1.2 copy-start.2
  135.0 0.9 copy-start.6
  135.9 0.9 copy-start.8
  136.8 7.4 %copy-start.3 = (bf16[128,3584]{1,0:T(8,128)(2,1)S(1)}, bf16[128,3584]{1,0:T(8,128)(2,1)}, u32[]{:S(2)}) copy-start(bf16[128,3584]{1,0:T(8,128)(2,1)} %copy-done.1) | copy-start | bytes 2752516
  140.6 21.8 %copy-start.10 = (bf16[3584]{0:T(1024)(128)(2,1)S(1)}, bf16[3584]{0:T(1024)(128)(2,1)}, u32[]{:S(2)}) copy-start(bf16[3584]{0:T(1024)(128)(2,1)} %param.11) | copy-start | bytes 21508
  140.6 17.2 %all-to-all-start.5 = ((bf16[16,32,1024]{2,1,0:T(8,128)(2,1)}), bf16[16,32,1024]{2,1,0:T(8,128)(2,1)S(1)}, u32[]{:S(2)}, u32[]{:S(2)}) async-start(bf16[16,32,1024]{2,1,0:T(8,128)(2,1)} %bitcast.11), calls=%async_computation.5 | async-start | bytes 2097152 | tf_op jit(solution)/shard_map/all_to_all | solution.py:253
  144.3 40.1 %collective-permute-start.10 = (bf16[128,3584]{1,0:T(8,128)(2,1)S(1)}, bf16[128,3584]{1,0:T(8,128)(2,1)S(1)}, u32[]{:S(2)}, u32[]{:S(2)}) collective-permute-start(bf16[128,3584]{1,0:T(8,128)(2,1)S(1)} %copy-done.3), channel_id=1, source_target_pairs={{0,64},{64,0},{1,65},{65,1},{2,66},{66,2},{3,67},{67,3},{4,68},{68... | collective-permute-start | bytes 2752520 | tf_op jit(solution)/shard_map/ppermute | solution.py:26
  158.8 15.7 %all-to-all-start.6 = ((f32[16,2,1408]{2,1,0:T(2,128)}), f32[16,2,1408]{2,1,0:T(2,128)S(1)}, u32[]{:S(2)}, u32[]{:S(2)}) async-start(f32[16,2,1408]{2,1,0:T(2,128)} %pad_maximum_fusion.1), calls=%async_computation.6 | async-start | bytes 360448 | tf_op jit(solution)/shard_map/all_to_all | solution.py:265
  162.4 22.0 %collective-permute-start.9 = (bf16[160,128]{1,0:T(8,128)(2,1)S(1)}, bf16[160,128]{1,0:T(8,128)(2,1)S(1)}, u32[]{:S(2)}, u32[]{:S(2)}) collective-permute-start(bf16[160,128]{1,0:T(8,128)(2,1)S(1)} %slice.61), channel_id=1, source_target_pairs={{0,64},{64,0},{1,65},{65,1},{2,66},{66,2},{3,67},{67,3},{4,68},{68... | collective-permute-start | bytes 122888 | tf_op jit(solution)/shard_map/ppermute | solution.py:26
  170.8 20.3 %collective-permute-start.8 = (f32[1,128]{1,0:T(1,128)S(1)}, f32[1,128]{1,0:T(1,128)S(1)}, u32[]{:S(2)}, u32[]{:S(2)}) collective-permute-start(f32[1,128]{1,0:T(1,128)S(1)} %get-tuple-element.24), channel_id=1, source_target_pairs={{0,64},{64,0},{1,65},{65,1},{2,66},{66,2},{3,67},{67,3},{4,68},{68... | collective-permute-start | bytes 1544 | tf_op jit(solution)/shard_map/ppermute | solution.py:26
  175.3 14.1 %all-to-all-start.7 = ((f32[8,2,1408]{2,1,0:T(2,128)}), f32[8,2,1408]{2,1,0:T(2,128)S(1)}, u32[]{:S(2)}, u32[]{:S(2)}) async-start(f32[8,2,1408]{2,1,0:T(2,128)} %broadcast_in_dim.29), calls=%async_computation.7 | async-start | bytes 180224 | tf_op jit(solution)/shard_map/all_to_all | solution.py:22
  184.4 5.1 %copy-start.9 = (bf16[4,3584]{1,0:T(4,128)(2,1)S(1)}, bf16[4,3584]{1,0:T(4,128)(2,1)}, u32[]{:S(2)}) copy-start(bf16[4,3584]{1,0:T(4,128)(2,1)} %param.9) | copy-start | bytes 86020

commit v3 on v1

v3 whole, which is shorter than its diff:
```python
import jax
import jax.numpy as jnp
from jax import lax
from jax.experimental import pallas as pl
from jax.experimental.pallas import tpu as pltpu
from jax.sharding import Mesh
from jax.sharding import PartitionSpec as P

X, C, Z, Y = ("section_0", "section_1", "dp_0", "dp_1")
DP = (Z, Y)
SECTION_DP = (X, C, Z, Y)
PLANE = (X, Y)

eps = 1e-06
ce_weight = 0.5
f32 = jnp.float32
bf16 = jnp.bfloat16

VMEM = pl.BlockSpec(memory_space=pltpu.VMEM)
SMEM = pl.BlockSpec(memory_space=pltpu.SMEM)
ANY = pl.BlockSpec(memory_space=pl.ANY)
MIB = 2**20
BIG = 52
shape = jax.ShapeDtypeStruct


def to_all(x, axes):
    length = lax.axis_size(axes)
    return exchanged(jnp.broadcast_to(x[None], (length, *x.shape)), axes)


def exchanged(x, axes):
    return lax.all_to_all(x, axes, 0, 0, tiled=True)


def swapped(x):
    return lax.ppermute(x, C, [(0, 1), (1, 0)])


def dot(a, b, along_a, along_b):
    return lax.dot_general(a, b, (((along_a,), (along_b,)), ((), ())), preferred_element_type=f32)


def column_log(logits):
    peak = jnp.max(logits, axis=0, keepdims=True)
    return peak + jnp.log(jnp.sum(jnp.exp(logits - peak), axis=0, keepdims=True))


def chunk(k):
    return slice(k * 128, (k + 1) * 128)


def called(kernel, in_specs, out_specs, out_shape, mib, scratch=()):
    return pl.pallas_call(
        kernel,
        in_specs=in_specs,
        out_specs=out_specs,
        out_shape=out_shape,
        scratch_shapes=list(scratch),
        compiler_params=pltpu.CompilerParams(vmem_limit_bytes=mib * MIB),
    )


def norm_kernel(
    place, teacher_at, student_at, t_gain_at, s_gain_at, out,
    teacher, student, t_gain, s_gain, t_scaled, s_scaled, gains, sems,
):
    pairs = (
        (teacher_at, teacher),
        (t_gain_at, t_gain),
        (student_at, student),
        (s_gain_at, s_gain),
    )
    copies = [pltpu.make_async_copy(a, b, sems.at[k]) for k, (a, b) in enumerate(pairs)]
    for copy in copies:
        copy.start()
    ix, ic = (place[0], place[1])
    half = out.shape[1]
    at = 0
    for n, (hidden, gain, scaled) in enumerate(
        ((teacher, t_gain, t_scaled), (student, s_gain, s_scaled))
    ):
        copies[2 * n].wait()
        copies[2 * n + 1].wait()
        values = hidden[...].astype(f32)
        inverse = lax.rsqrt(jnp.mean(values * values, axis=-1, keepdims=True) + eps)
        scaled[...] = values * inverse
        lines = gain.shape[0]
        gains[0:lines] = gain[...].astype(f32)
        width = scaled.shape[1] // 4
        part = scaled[:, pl.ds(pl.multiple_of(ix * width, 128), width)]
        mine = jnp.where(ic == 0, part[0:half], part[half : 2 * half])
        for k in range(width // 128):
            line = gains[pl.ds(ix * (width // 128) + k, 1)]
            normed = (mine[:, chunk(k)] * line).astype(bf16)
            for z in range(out.shape[0]):
                out[z, :, at : at + 128] = normed
            at += 128


def logits_kernel(
    plane, t_own, t_other, s_own, s_other,
    t_logits, s_logits, logs, student_rows,
    t_rows, s_rows, t_heads, s_heads, t_out, s_out, sems, out_sems,
):
    nx = plane.shape[0]
    qt = t_rows.shape[1] // nx
    qs = s_rows.shape[1] // nx
    rows = t_own.shape[0]
    parts = []
    for k in range(nx):
        at = slice(k * qt, (k + 1) * qt)
        parts.append(
            [
                (plane.at[k, :, 0:qt], t_rows.at[:, at]),
                (t_own.at[:, at], t_heads.at[0:rows, at]),
                (t_other.at[:, at], t_heads.at[rows:, at]),
            ]
        )
    parts.append(
        [(plane.at[k, :, qt:], s_rows.at[:, k * qs : (k + 1) * qs]) for k in range(nx)]
        + [(s_own, s_heads.at[0:rows]), (s_other, s_heads.at[rows:])]
    )
    copies, number = ([], 0)
    for part in parts:
        copies.append([])
        for source, target in part:
            copies[-1].append(pltpu.make_async_copy(source, target, sems.at[number]))
            copies[-1][-1].start()
            number += 1
    total = 0.0
    for k in range(nx):
        for copy in copies[k]:
            copy.wait()
        at = slice(k * qt, (k + 1) * qt)
        total += dot(t_heads[:, at], t_rows[:, at], 1, 1)
    t_out[...] = total
    back = [pltpu.make_async_copy(t_out, t_logits, out_sems.at[0])]
    back[0].start()
    for copy in copies[nx]:
        copy.wait()
    back.append(pltpu.make_async_copy(s_rows, student_rows, out_sems.at[1]))
    back[1].start()
    s_out[...] = dot(s_heads[...], s_rows[...], 1, 1)
    back.append(pltpu.make_async_copy(s_out, s_logits, out_sems.at[2]))
    back[2].start()
    t_log = column_log(t_out[...])
    s_log = column_log(s_out[...])
    for k in range(logs.shape[0]):
        logs[k, 0:1] = t_log
        logs[k, 1:2] = s_log
    for copy in back:
        copy.wait()


def merge_kernel(got, out):
    t_log = column_log(got[:, 0, :])
    s_log = column_log(got[:, 1, :])
    for k in range(out.shape[0]):
        out[k, 0:1] = t_log
        out[k, 1:2] = s_log


def terms_kernel(
    place, got, label, cot, t_logits, s_logits, student_rows, s_own, s_other,
    slope, sent, common, t_in, s_in, s_rows, s_heads, sems,
):
    rows = s_own.shape[0]
    pairs = (
        (t_logits, t_in),
        (s_logits, s_in),
        (s_own, s_heads.at[0:rows]),
        (s_other, s_heads.at[rows:]),
        (student_rows, s_rows),
    )
    copies = [pltpu.make_async_copy(a, b, sems.at[k]) for k, (a, b) in enumerate(pairs)]
    for copy in copies:
        copy.start()
    nx, ny, held, _ = sent.shape
    qs = s_rows.shape[1] // nx
    teacher_log = column_log(got[:, 0, :])
    student_log = column_log(got[:, 1, :])
    common[...] = (1.0 + ce_weight) * student_log - teacher_log
    loss_terms = 0.0
    copies[0].wait()
    copies[1].wait()
    for k in range(2):
        at = slice(k * rows, (k + 1) * rows)
        s_part, t_part = (s_in[at], t_in[at])
        entry = lax.broadcasted_iota(jnp.int32, s_part.shape, 0) + place[2 + k]
        hits = entry == label[...]
        s_prob = jnp.exp(s_part - student_log)
        t_prob = jnp.exp(t_part - teacher_log)
        onehot = jnp.where(hits, 1.0, 0.0)
        value = cot[...] * ((1.0 + ce_weight) * s_prob - t_prob - ce_weight * onehot)
        slope[at] = value.astype(bf16)
        lost = t_prob * (t_part - s_part) - ce_weight * jnp.where(hits, s_part, 0.0)
        loss_terms += jnp.sum(lost, axis=0, keepdims=True)
    for copy in copies[2:]:
        copy.wait()
    line = lax.broadcasted_iota(jnp.int32, (16, 128), 0)
    loss_high = loss_terms.astype(bf16).astype(f32)
    slopes = slope[...]
    for x in range(nx):
        at = slice(x * qs, (x + 1) * qs)
        terms = dot(slopes, s_heads[:, at], 0, 0)
        gain = jnp.sum(terms * s_rows[:, at].astype(f32), axis=0, keepdims=True)
        high = gain.astype(bf16).astype(f32)
        tail = jnp.where(line == 14, loss_high, jnp.where(line == 15, loss_terms - loss_high, 0.0))
        for k in range(qs // 128):
            tail = jnp.where(line == k, high[:, chunk(k)], tail)
            tail = jnp.where(line == 7 + k, (gain - high)[:, chunk(k)], tail)
        terms = terms.astype(bf16)
        for y in range(ny):
            sent[x, y, :, 0:qs] = terms[y * held : (y + 1) * held]
            sent[x, y, 0:16, qs:] = tail.astype(bf16)
            sent[x, y, 16:held, qs:] = jnp.zeros((held - 16, 128), bf16)


def repack_kernel(got, out):
    total = got[0].astype(f32)
    for k in range(1, got.shape[0]):
        total += got[k].astype(f32)
    nz, half, _ = out.shape
    qs = got.shape[2] - 128
    tail = total[0:16, qs:]
    lines = [tail[k : k + 1] + tail[7 + k : 8 + k] for k in range(7)]
    lines.append(tail[14:15] + tail[15:16])
    pairs = [jnp.concatenate([lines[k], lines[4 + k]], axis=0) for k in range(4)]
    for z in range(nz):
        out[z, :, 0:qs] = total[z * half : (z + 1) * half, 0:qs]
        for k in range(4):
            out[z, :, qs + k * 128 : qs + (k + 1) * 128] = pairs[k]


def share_kernel(got, common, out):
    total = got[0]
    for k in range(1, got.shape[0]):
        total += got[k]
    width = out.shape[2] - 128
    for k in range(out.shape[0]):
        out[k] = total
        out[k, 1:2, width:] = total[1:2, width:] + common[...]


def final_kernel(got, hidden, gain, student_grad, gain_grad, loss, gains):
    values = hidden[...].astype(f32)
    own, ds = values.shape
    inverse = lax.rsqrt(jnp.mean(values * values, axis=-1, keepdims=True) + eps)
    scaled = values * inverse
    gains[...] = gain[...].astype(f32)
    each = gain.shape[0] // 4
    qs = each * 128
    inner = 0.0
    weighted = []
    for x in range(4):
        pair = (got[2 * x], got[2 * x + 1])
        for k in range(each):
            line = x * each + k
            grad = jnp.concatenate([p[:, chunk(k)] for p in pair], axis=0)
            weighted.append(grad * gains[line : line + 1])
            inner += jnp.sum(weighted[-1] * scaled[:, chunk(line)], axis=1, keepdims=True)
            row, at = (k // 4, qs + (k % 4) * 128)
            both = sum(p[row : row + 1, at : at + 128] for p in pair)
            gain_grad[line : line + 1] = both / gains[line : line + 1]
    inner = inner * (1.0 / ds)
    for k in range(4 * each):
        student_grad[:, chunk(k)] = inverse * (weighted[k] - scaled[:, chunk(k)] * inner)
    at = qs + 384
    lost = got[0][1:2, at:] + got[1][1:2, at:]
    loss[...] = jnp.sum(lost, axis=1, keepdims=True) * (1.0 / 256)


def on_device(
    teacher_hidden,
    student_hidden,
    teacher_gain,
    student_gain,
    teacher_head,
    student_head,
    labels,
    cotangent,
):
    nx, nc, nz, ny = (lax.axis_size(a) for a in SECTION_DP)
    ix, ic, iz, iy = (lax.axis_index(a) for a in SECTION_DP)
    rows, dt = teacher_head.shape
    own, ds = student_hidden.shape
    half = own // nc
    qt, qs = (dt // nx, ds // nx)
    held = nz * half
    tokens = ny * held

    def start_of(core):
        return (((ix * nc + core) * nz + iz) * ny + iy) * rows

    place = jnp.stack([ix, ic, start_of(ic), start_of(1 - ic)])
    t_gain, s_gain = (g.reshape(-1, 128) for g in (teacher_gain, student_gain))
    pieces = called(
        norm_kernel,
        [SMEM] + [ANY] * 4,
        VMEM,
        shape((nz, half, qt + qs), bf16),
        BIG,
        [
            pltpu.VMEM((own, dt), bf16),
            pltpu.VMEM((own, ds), bf16),
            pltpu.VMEM((dt // 128, 128), bf16),
            pltpu.VMEM((ds // 128, 128), bf16),
            pltpu.VMEM((own, dt), f32),
            pltpu.VMEM((own, ds), f32),
            pltpu.VMEM((dt // 128, 128), f32),
            pltpu.SemaphoreType.DMA((4,)),
        ],
    )(place, teacher_hidden, student_hidden, t_gain, s_gain)

    pieces, teacher_head, student_head = lax.optimization_barrier(
        (pieces, teacher_head, student_head)
    )
    teacher_other, student_other = (swapped(teacher_head), swapped(student_head))

    def of_tokens(a):
        mine = lax.dynamic_index_in_dim(a.reshape(nz, ny, nc, half), ic, 2, keepdims=False)
        return mine.transpose(1, 0, 2).reshape(1, tokens)

    line = exchanged(pieces, Z).reshape(held, qt + qs)
    line, teacher_other, student_other, label, cot = lax.optimization_barrier(
        (line, teacher_other, student_other, of_tokens(labels), of_tokens(cotangent))
    )
    plane = to_all(line, PLANE).reshape(nx, tokens, qt + qs)

    t_logits, s_logits, logs, student_rows = called(
        logits_kernel,
        [ANY] * 5,
        [ANY, ANY, VMEM, ANY],
        [
            shape((2 * rows, tokens), f32),
            shape((2 * rows, tokens), f32),
            shape((nx * ny, 2, tokens), f32),
            shape((tokens, ds), bf16),
        ],
        BIG,
        [
            pltpu.VMEM((tokens, dt), bf16),
            pltpu.VMEM((tokens, ds), bf16),
            pltpu.VMEM((2 * rows, dt), bf16),
            pltpu.VMEM((2 * rows, ds), bf16),
            pltpu.VMEM((2 * rows, tokens), f32),
            pltpu.VMEM((2 * rows, tokens), f32),
            pltpu.SemaphoreType.DMA((4 * nx + 2,)),
            pltpu.SemaphoreType.DMA((3,)),
        ],
    )(plane, teacher_head, teacher_other, student_head, student_other)
    logs = exchanged(logs, PLANE)
    logs = called(merge_kernel, [VMEM], VMEM, shape((nz, 2, tokens), f32), 4)(logs)
    logs = exchanged(logs, Z)

    slope, sent, common = called(
        terms_kernel,
        [SMEM] + [VMEM] * 3 + [ANY] * 5,
        [VMEM] * 3,
        [
            shape((2 * rows, tokens), bf16),
            shape((nx, ny, held, qs + 128), bf16),
            shape((1, tokens), f32),
        ],
        BIG,
        [
            pltpu.VMEM((2 * rows, tokens), f32),
            pltpu.VMEM((2 * rows, tokens), f32),
            pltpu.VMEM((tokens, ds), bf16),
            pltpu.VMEM((2 * rows, ds), bf16),
            pltpu.SemaphoreType.DMA((5,)),
        ],
    )(place, logs, label, cot, t_logits, s_logits, student_rows, student_head, student_other)
    got = exchanged(sent.reshape(nx * ny, held, qs + 128), PLANE)
    got, student_rows, slope = lax.optimization_barrier((got, student_rows, slope))
    got = called(repack_kernel, [VMEM], VMEM, shape((nz, half, qs + 512), f32), 8)(got)
    got = exchanged(got, Z)

    head_grad = (
        dot(slope[:rows], student_rows, 1, 0)
        + dot(swapped(slope[rows:]), swapped(student_rows), 1, 0)
    ).astype(bf16)

    got = called(share_kernel, [VMEM] * 2, VMEM, shape((nx * nc, half, qs + 512), f32), 4)(
        got, common
    )
    got, head_grad = lax.optimization_barrier((exchanged(got, (X, C)), head_grad))
    student_grad, gain_grad, loss = called(
        final_kernel,
        [VMEM] * 3,
        [VMEM] * 3,
        [shape((own, ds), f32), shape((ds // 128, 128), f32), shape((1, 1), f32)],
        4,
        [pltpu.VMEM((ds // 128, 128), f32)],
    )(got, student_hidden, s_gain)
    return (loss.reshape(()), student_grad, gain_grad.reshape(ds), head_grad)


def solution(mesh):
    finer = Mesh(mesh.devices.reshape(4, 2, 16, 4), SECTION_DP)
    placed = (
        P(DP, None),
        P(DP, None),
        P(),
        P(),
        P(SECTION_DP, None),
        P(SECTION_DP, None),
        P(),
        P(),
    )
    return jax.shard_map(
        on_device,
        mesh=finer,
        in_specs=placed,
        out_specs=(P(), P(DP, None), P(), P(SECTION_DP, None)),
        check_vma=False,
    )
```

time: 189 us -> 178 us (0.942)
  blocking collectives: 43.3 us -> 89.2 us
  starting transfers between devices: 61.9 us -> 39.6 us
  waiting for transfers between devices: 44.3 us -> 22.4 us
  Pallas kernels: 0 us -> 15.2 us
  other arithmetic: 12.4 us -> 0.08 us
  matrix products: 11 us -> 3.09 us
  between operations: 5.49 us -> 0.81 us
  local copies, waits for them, and re-layouts: 9.7 us -> 6.36 us
    all_to_all x2 -> x4, blocking collectives: 43.3 us -> 89.2 us  [exchanged(): return lax.all_to_all(x, axes, 0, 0, tiled=True)]
    all_to_all x5 -> x3, starting transfers between devices: 42.8 us -> 19.1 us  [exchanged(): return lax.all_to_all(x, axes, 0, 0, tiled=True)]
    all_to_all x5 -> x3, waiting for transfers between devices: 44.3 us -> 22.4 us  [exchanged(): return lax.all_to_all(x, axes, 0, 0, tiled=True)]
    pallas_call x0 -> x7, Pallas kernels: none -> 15.2 us  [the longest x1 6.7 us: on_device(): called(logits_kernel, [ANY] * 5, [ANY, ANY, VMEM, ANY], [shape((2 * rows,...]
    dot_general x8 -> x2, matrix products: 11 us -> 3.09 us  [dot(): lax.dot_general(a, b, (((along_a,), (along_b,)), ((), ())), preferred_ele...]
    reduce_sum x12 -> x0, other arithmetic: 3.8 us -> none  [the longest x2 1.92 us: normalize(): inverse = lax.rsqrt(jnp.mean(values * values, axis=-1, keepdims=True) + eps)]
    broadcast_in_dim x9 -> x1, local copies, waits for them, and re-layouts: 3.94 us -> 0.2 us  [to_all(): return exchanged(jnp.broadcast_to(x[None], (length, *x.shape)), axes)]
    convert_element_type x8 -> x0, other arithmetic: 3.24 us -> none  [the longest x1 0.88 us: normalize(): values = hidden.astype(f32)]
  transfers between devices with their start and end apart: 9 -> 7, of which waited for: 5 -> 3; matrix products, arithmetic and copies ran while one was open for 7% -> 4% of each run, Pallas kernels for 0% -> 1%
where the time goes in v3:
time: 178 us; the launch traced here: 177 us
  blocking collectives  89.2 us (50%)
  starting transfers between devices  39.6 us (22%)
  waiting for transfers between devices  22.4 us (13%)
  Pallas kernels  15.2 us (9%)
  local copies, waits for them, and re-layouts  6.36 us (4%)
  matrix products  3.09 us (2%)
    all_to_all x4, blocking collectives, exchanged(): return lax.all_to_all(x, axes, 0, 0, tiled=True)  89.2 us
    all_to_all x3, waiting for transfers between devices, exchanged(): return lax.all_to_all(x, axes, 0, 0, tiled=True)  22.4 us
    ppermute x4, starting transfers between devices, swapped(): return lax.ppermute(x, C, [(0, 1), (1, 0)])  20.6 us
    all_to_all x3, starting transfers between devices, exchanged(): return lax.all_to_all(x, axes, 0, 0, tiled=True)  19.1 us
    pallas_call x1, Pallas kernels, on_device(): called(logits_kernel, [ANY] * 5, [ANY, ANY, VMEM, ANY], [shape((2 * rows,...  6.7 us
    pallas_call x1, Pallas kernels, on_device(): called(terms_kernel, [SMEM] + [VMEM] * 3 + [ANY] * 5, [VMEM] * 3, [shape(...  4.35 us
  transfers between devices with their start and end apart: 7, of which 3 were waited for; matrix products, arithmetic and copies ran while one was open for 4% of the time, Pallas kernels for 1%

profile of v3, /device:TPU:1, one launch (start us, length us, event | category | flops | bytes accessed | tf_op | source)
XLA Modules:
  0.0 176.8 jit_solution(3851129817687866526)
XLA Ops:
  0.6 0.1 pad_add_fusion.place
  0.7 0.0 copy-start
  0.7 0.7 copy-done
  1.5 0.0 copy-start.2
  1.5 0.8 copy-done.2
  2.3 0.0 copy-start.3
  2.3 0.7 copy-done.3
  3.0 0.0 copy-start.5
  3.0 0.7 copy-done.5
  3.7 1.8 %shard_map.111 = bf16[16,2,2944]{2,1,0:T(2,128)(2,1)} custom-call(s32[4]{0:T(128)S(1)} %pad_add_fusion.place, bf16[4,8192]{1,0:T(4,128)(2,1)S(1)} %copy-done.2, bf16[4,3584]{1,0:T(4,128)(2,1)S(1)} %copy-done, bf16[64,128]{1,0:T(8,128)(2,1)S(1)} %bitcast.21, bf16[28,128]{1,0:T(8,128)(2,1)S(1)} %bitcast.19), custom_call_target="tpu_custom_call" | custom-call | tf_op jit(solution)/shard_map/pallas_call | solution.py:298
  5.5 8.8 %collective-permute-start = (bf16[160,8192]{1,0:T(8,128)(2,1)}, bf16[160,8192]{1,0:T(8,128)(2,1)}, u32[]{:S(2)}, u32[]{:S(2)}) collective-permute-start(bf16[160,8192]{1,0:T(8,128)(2,1)} %t_own), channel_id=1, source_target_pairs={{0,64},{64,0},{1,65},{65,1},{2,66},{66,2},{3,67},{67,3},{4,68},{68... | collective-permute-start | bytes 7864328 | tf_op jit(solution)/shard_map/ppermute | solution.py:37
  14.3 1.9 %collective-permute-start.1 = (bf16[160,3584]{1,0:T(8,128)(2,1)}, bf16[160,3584]{1,0:T(8,128)(2,1)S(1)}, u32[]{:S(2)}, u32[]{:S(2)}) collective-permute-start(bf16[160,3584]{1,0:T(8,128)(2,1)} %s_own.1), channel_id=1, source_target_pairs={{0,64},{64,0},{1,65},{65,1},{2,66},{66,2},{3,67},{67,3},{4,68},{68... | collective-permute-start | bytes 3440648 | tf_op jit(solution)/shard_map/ppermute | solution.py:37
  16.3 9.6 %all-to-all-start = ((bf16[16,2,2944]{2,1,0:T(2,128)(2,1)}), bf16[16,2,2944]{2,1,0:T(2,128)(2,1)S(1)}, u32[]{:S(2)}, u32[]{:S(2)}) async-start(bf16[16,2,2944]{2,1,0:T(2,128)(2,1)} %shard_map.111), calls=%async_computation | async-start | bytes 376832 | tf_op jit(solution)/shard_map/all_to_all | solution.py:33
  25.8 0.8 reshape.45
  26.7 0.1 copy.14
  26.8 0.1 copy.15
  26.9 0.1 reshape.46.label
  27.1 0.8 reshape.47
  28.0 0.1 copy.16
  28.1 0.1 copy.17
  28.2 0.1 reshape.48.cot
  28.3 10.0 %all-to-all-done = bf16[16,2,2944]{2,1,0:T(2,128)(2,1)S(1)} async-done(((bf16[16,2,2944]{2,1,0:T(2,128)(2,1)}), bf16[16,2,2944]{2,1,0:T(2,128)(2,1)S(1)}, u32[]{:S(2)}, u32[]{:S(2)}) %all-to-all-start) | async-done | bytes 188448 | tf_op jit(solution)/shard_map/all_to_all | solution.py:33
  38.3 0.1 reshape.44
  38.4 0.0 collective-permute-done.1.s_other
  38.4 0.0 copy-start.6
  38.4 0.0 collective-permute-done.t_other
  38.4 0.2 broadcast_in_dim.2
  38.7 39.0 %all_to_all.35 = bf16[16,32,2944]{2,1,0:T(8,128)(2,1)} all-to-all(bf16[16,32,2944]{2,1,0:T(8,128)(2,1)S(1)} %broadcast_in_dim.2), channel_id=1, replica_groups=mesh['section_0'=4,'section_1'=2,'dp_0'=16,'dp_1'=4] {'section_0','dp_1'}, dimensions={0} | all-to-all | bytes 6029312 | tf_op jit(solution)/shard_map/all_to_all | solution.py:33
  77.7 0.0 copy-done.6
  77.7 6.7 %shard_map.112 = (f32[320,128]{1,0:T(8,128)S(1)}, f32[320,128]{1,0:T(8,128)S(1)}, f32[16,2,128]{2,1,0:T(2,128)S(1)}, bf16[128,3584]{1,0:T(8,128)(2,1)S(1)}) custom-call(bf16[4,128,2944]{2,1,0:T(8,128)(2,1)} %bitcast.22, bf16[160,8192]{1,0:T(8,128)(2,1)} %t_own, bf16[160,8192]{1,0:T(8,128)(2,1)} %collective-permute-done.t_other, bf16[160,3584]{1,0:T(8,128)(2,1)} %s_own.1, ...), custom_call_target="tpu_custom_call" | custom-call | tf_op jit(solution)/shard_map/pallas_call | solution.py:331
  84.4 10.5 %all_to_all.36.got = f32[16,2,128]{2,1,0:T(2,128)S(1)} all-to-all(f32[16,2,128]{2,1,0:T(2,128)S(1)} %get-tuple-element.33), channel_id=1, replica_groups=mesh['section_0'=4,'section_1'=2,'dp_0'=16,'dp_1'=4] {'section_0','dp_1'}, dimensions={0} | all-to-all | bytes 32768 | tf_op jit(solution)/shard_map/all_to_all | solution.py:33
  95.0 24.0 %all_to_all.37.got = f32[16,2,128]{2,1,0:T(2,128)S(1)} all-to-all(f32[16,2,128]{2,1,0:T(2,128)S(1)} %shard_map.113), channel_id=1, replica_groups=mesh['section_0'=4,'section_1'=2,'dp_0'=16,'dp_1'=4] {'dp_0'}, dimensions={0} | all-to-all | bytes 32768 | tf_op jit(solution)/shard_map/all_to_all | solution.py:33
  118.9 4.4 %shard_map.114 = (bf16[320,128]{1,0:T(8,128)(2,1)S(1)}, bf16[4,4,32,1024]{3,2,1,0:T(8,128)(2,1)}, f32[1,128]{1,0:T(1,128)S(1)}) custom-call(s32[4]{0:T(128)S(1)} %pad_add_fusion.place, f32[16,2,128]{2,1,0:T(2,128)S(1)} %all_to_all.37.got, s32[1,128]{1,0:T(1,128)S(1)} %reshape.46.label, f32[1,128]{1,0:T(1,128)S(1)} %reshape.48.cot, ...), custom_call_target="tpu_custom_call" | custom-call | tf_op jit(solution)/shard_map/pallas_call | solution.py:357
  123.3 15.6 %all_to_all.38.got = bf16[16,32,1024]{2,1,0:T(8,128)(2,1)S(1)} all-to-all(bf16[16,32,1024]{2,1,0:T(8,128)(2,1)} %bitcast.23), channel_id=1, replica_groups=mesh['section_0'=4,'section_1'=2,'dp_0'=16,'dp_1'=4] {'section_0','dp_1'}, dimensions={0} | all-to-all | bytes 2097152 | tf_op jit(solution)/shard_map/all_to_all | solution.py:33
  138.9 7.9 %collective-permute-start.3 = (bf16[128,3584]{1,0:T(8,128)(2,1)S(1)}, bf16[128,3584]{1,0:T(8,128)(2,1)}, u32[]{:S(2)}, u32[]{:S(2)}) collective-permute-start(bf16[128,3584]{1,0:T(8,128)(2,1)S(1)} %get-tuple-element.44.student_rows), channel_id=1, source_target_pairs={{0,64},{64,0},{1,65},{65,1},{2,66},{66,2},{3,67},{67,3},{4,68},{68... | collective-permute-start | bytes 2752520 | tf_op jit(solution)/shard_map/ppermute | solution.py:37
  146.9 0.8 shard_map.115
  147.7 3.5 %all-to-all-start.5 = ((f32[16,2,1408]{2,1,0:T(2,128)}), f32[16,2,1408]{2,1,0:T(2,128)S(1)}, u32[]{:S(2)}, u32[]{:S(2)}) async-start(f32[16,2,1408]{2,1,0:T(2,128)} %shard_map.115), calls=%async_computation.5 | async-start | bytes 360448 | tf_op jit(solution)/shard_map/all_to_all | solution.py:33
  151.2 0.6 slice.7
  151.9 1.9 %collective-permute-start.2 = (bf16[160,128]{1,0:T(8,128)(2,1)}, bf16[160,128]{1,0:T(8,128)(2,1)S(1)}, u32[]{:S(2)}, u32[]{:S(2)}) collective-permute-start(bf16[160,128]{1,0:T(8,128)(2,1)} %slice.7), channel_id=1, source_target_pairs={{0,64},{64,0},{1,65},{65,1},{2,66},{66,2},{3,67},{67,3},{4,68},{68... | collective-permute-start | bytes 122888 | tf_op jit(solution)/shard_map/ppermute | solution.py:37
  153.8 0.4 fusion.1
  154.2 10.0 %all-to-all-done.5.got = f32[16,2,1408]{2,1,0:T(2,128)S(1)} async-done(((f32[16,2,1408]{2,1,0:T(2,128)}), f32[16,2,1408]{2,1,0:T(2,128)S(1)}, u32[]{:S(2)}, u32[]{:S(2)}) %all-to-all-start.5) | async-done | bytes 180256 | tf_op jit(solution)/shard_map/all_to_all | solution.py:33
  164.3 0.7 shard_map.116
  164.9 0.0 copy-start.1
  164.9 0.0 copy-start.4
  164.9 6.0 %all-to-all-start.6 = ((f32[8,2,1408]{2,1,0:T(2,128)}), f32[8,2,1408]{2,1,0:T(2,128)S(1)}, u32[]{:S(2)}, u32[]{:S(2)}) async-start(f32[8,2,1408]{2,1,0:T(2,128)} %shard_map.116), calls=%async_computation.6 | async-start | bytes 180224 | tf_op jit(solution)/shard_map/all_to_all | solution.py:33
  170.9 0.0 collective-permute-done.2
  170.9 0.0 collective-permute-done.3
  171.0 2.6 %fusion = bf16[160,3584]{1,0:T(8,128)(2,1)} fusion(f32[160,3584]{1,0:T(8,128)S(1)} %fusion.1, bf16[160,128]{1,0:T(8,128)(2,1)S(1)} %collective-permute-done.2, bf16[128,3584]{1,0:T(8,128)(2,1)} %collective-permute-done.3), kind=kOutput, calls=%fused_computation.1 | convolution fusion | flops 147947520 | bytes 4399104 | tf_op jit(solution)/shard_map/dot_general | solution.py:41
  173.6 2.3 %all-to-all-done.6.got = f32[8,2,1408]{2,1,0:T(2,128)S(1)} async-done(((f32[8,2,1408]{2,1,0:T(2,128)}), f32[8,2,1408]{2,1,0:T(2,128)S(1)}, u32[]{:S(2)}, u32[]{:S(2)}) %all-to-all-start.6) | async-done | bytes 90144 | tf_op jit(solution)/shard_map/all_to_all | solution.py:33
  175.9 0.0 copy-done.1
  175.9 0.0 copy-done.4
  175.9 0.9 shard_map.117
  (3 shorter events, 0.1 us)
Async XLA Ops:
  0.7 0.8 copy-start
  1.5 0.8 copy-start.2
  2.3 0.7 copy-start.3
  3.0 0.7 copy-start.5
  5.5 32.9 %collective-permute-start = (bf16[160,8192]{1,0:T(8,128)(2,1)}, bf16[160,8192]{1,0:T(8,128)(2,1)}, u32[]{:S(2)}, u32[]{:S(2)}) collective-permute-start(bf16[160,8192]{1,0:T(8,128)(2,1)} %t_own), channel_id=1, source_target_pairs={{0,64},{64,0},{1,65},{65,1},{2,66},{66,2},{3,67},{67,3},{4,68},{68... | collective-permute-start | bytes 7864328 | tf_op jit(solution)/shard_map/ppermute | solution.py:37
  14.3 24.1 %collective-permute-start.1 = (bf16[160,3584]{1,0:T(8,128)(2,1)}, bf16[160,3584]{1,0:T(8,128)(2,1)S(1)}, u32[]{:S(2)}, u32[]{:S(2)}) collective-permute-start(bf16[160,3584]{1,0:T(8,128)(2,1)} %s_own.1), channel_id=1, source_target_pairs={{0,64},{64,0},{1,65},{65,1},{2,66},{66,2},{3,67},{67,3},{4,68},{68... | collective-permute-start | bytes 3440648 | tf_op jit(solution)/shard_map/ppermute | solution.py:37
  16.3 22.1 %all-to-all-start = ((bf16[16,2,2944]{2,1,0:T(2,128)(2,1)}), bf16[16,2,2944]{2,1,0:T(2,128)(2,1)S(1)}, u32[]{:S(2)}, u32[]{:S(2)}) async-start(bf16[16,2,2944]{2,1,0:T(2,128)(2,1)} %shard_map.111), calls=%async_computation | async-start | bytes 376832 | tf_op jit(solution)/shard_map/all_to_all | solution.py:33
  38.4 39.3 %copy-start.6 = (bf16[160,3584]{1,0:T(8,128)(2,1)}, bf16[160,3584]{1,0:T(8,128)(2,1)S(1)}, u32[]{:S(2)}) copy-start(bf16[160,3584]{1,0:T(8,128)(2,1)S(1)} %collective-permute-done.1.s_other) | copy-start | bytes 3440644
  138.9 32.0 %collective-permute-start.3 = (bf16[128,3584]{1,0:T(8,128)(2,1)S(1)}, bf16[128,3584]{1,0:T(8,128)(2,1)}, u32[]{:S(2)}, u32[]{:S(2)}) collective-permute-start(bf16[128,3584]{1,0:T(8,128)(2,1)S(1)} %get-tuple-element.44.student_rows), channel_id=1, source_target_pairs={{0,64},{64,0},{1,65},{65,1},{2,66},{66,2},{3,67},{67,3},{4,68},{68... | collective-permute-start | bytes 2752520 | tf_op jit(solution)/shard_map/ppermute | solution.py:37
  147.7 16.6 %all-to-all-start.5 = ((f32[16,2,1408]{2,1,0:T(2,128)}), f32[16,2,1408]{2,1,0:T(2,128)S(1)}, u32[]{:S(2)}, u32[]{:S(2)}) async-start(f32[16,2,1408]{2,1,0:T(2,128)} %shard_map.115), calls=%async_computation.5 | async-start | bytes 360448 | tf_op jit(solution)/shard_map/all_to_all | solution.py:33
  151.9 19.1 %collective-permute-start.2 = (bf16[160,128]{1,0:T(8,128)(2,1)}, bf16[160,128]{1,0:T(8,128)(2,1)S(1)}, u32[]{:S(2)}, u32[]{:S(2)}) collective-permute-start(bf16[160,128]{1,0:T(8,128)(2,1)} %slice.7), channel_id=1, source_target_pairs={{0,64},{64,0},{1,65},{65,1},{2,66},{66,2},{3,67},{67,3},{4,68},{68... | collective-permute-start | bytes 122888 | tf_op jit(solution)/shard_map/ppermute | solution.py:37
  164.9 11.0 %copy-start.1 = (bf16[4,3584]{1,0:T(4,128)(2,1)S(1)}, bf16[4,3584]{1,0:T(4,128)(2,1)}, u32[]{:S(2)}) copy-start(bf16[4,3584]{1,0:T(4,128)(2,1)} %hidden.1) | copy-start | bytes 86020
  164.9 11.0 %copy-start.4 = (bf16[3584]{0:T(1024)(128)(2,1)S(1)}, bf16[3584]{0:T(1024)(128)(2,1)}, u32[]{:S(2)}) copy-start(bf16[3584]{0:T(1024)(128)(2,1)} %param.11) | copy-start | bytes 21508
  164.9 11.0 %all-to-all-start.6 = ((f32[8,2,1408]{2,1,0:T(2,128)}), f32[8,2,1408]{2,1,0:T(2,128)S(1)}, u32[]{:S(2)}, u32[]{:S(2)}) async-start(f32[8,2,1408]{2,1,0:T(2,128)} %shard_map.116), calls=%async_computation.6 | async-start | bytes 180224 | tf_op jit(solution)/shard_map/all_to_all | solution.py:33

commit v4 on v3

--- a/solution.py
+++ b/solution.py
@@ -20,7 +20,9 @@
 SMEM = pl.BlockSpec(memory_space=pltpu.SMEM)
 ANY = pl.BlockSpec(memory_space=pl.ANY)
 MIB = 2**20
-BIG = 52
+NORM = 8
+LOGITS = 8
+BIG = 16
 shape = jax.ShapeDtypeStruct
 
 
@@ -99,51 +101,34 @@
 
 
 def logits_kernel(
-    plane, t_own, t_other, s_own, s_other,
-    t_logits, s_logits, logs, student_rows,
-    t_rows, s_rows, t_heads, s_heads, t_out, s_out, sems, out_sems,
+    plane, t_heads, s_heads, t_logits, s_logits, logs, student_rows, t_out, s_out, sems
 ):
     nx = plane.shape[0]
-    qt = t_rows.shape[1] // nx
-    qs = s_rows.shape[1] // nx
-    rows = t_own.shape[0]
-    parts = []
-    for k in range(nx):
-        at = slice(k * qt, (k + 1) * qt)
-        parts.append(
-            [
-                (plane.at[k, :, 0:qt], t_rows.at[:, at]),
-                (t_own.at[:, at], t_heads.at[0:rows, at]),
-                (t_other.at[:, at], t_heads.at[rows:, at]),
-            ]
+    nc, rows, dt = t_heads.shape
+    qt = dt // nx
+    qs = s_heads.shape[2] // nx
+    back = [
+        pltpu.make_async_copy(
+            plane.at[k, :, qt:], student_rows.at[:, k * qs : (k + 1) * qs], sems.at[k]
         )
-    parts.append(
-        [(plane.at[k, :, qt:], s_rows.at[:, k * qs : (k + 1) * qs]) for k in range(nx)]
-        + [(s_own, s_heads.at[0:rows]), (s_other, s_heads.at[rows:])]
-    )
-    copies, number = ([], 0)
-    for part in parts:
-        copies.append([])
-        for source, target in part:
-            copies[-1].append(pltpu.make_async_copy(source, target, sems.at[number]))
-            copies[-1][-1].start()
-            number += 1
-    total = 0.0
-    for k in range(nx):
-        for copy in copies[k]:
-            copy.wait()
-        at = slice(k * qt, (k + 1) * qt)
-        total += dot(t_heads[:, at], t_rows[:, at], 1, 1)
-    t_out[...] = total
-    back = [pltpu.make_async_copy(t_out, t_logits, out_sems.at[0])]
-    back[0].start()
-    for copy in copies[nx]:
-        copy.wait()
-    back.append(pltpu.make_async_copy(s_rows, student_rows, out_sems.at[1]))
-    back[1].start()
-    s_out[...] = dot(s_heads[...], s_rows[...], 1, 1)
-    back.append(pltpu.make_async_copy(s_out, s_logits, out_sems.at[2]))
-    back[2].start()
+        for k in range(nx)
+    ]
+    back.append(pltpu.make_async_copy(t_out, t_logits, sems.at[nx]))
+    back.append(pltpu.make_async_copy(s_out, s_logits, sems.at[nx + 1]))
+    for copy in back[:nx]:
+        copy.start()
+    for n in range(nc):
+        total = 0.0
+        for k in range(nx):
+            total += dot(t_heads[n, :, k * qt : (k + 1) * qt], plane[k, :, 0:qt], 1, 1)
+        t_out[n * rows : (n + 1) * rows] = total
+    back[nx].start()
+    for n in range(nc):
+        total = 0.0
+        for k in range(nx):
+            total += dot(s_heads[n, :, k * qs : (k + 1) * qs], plane[k, :, qt:], 1, 1)
+        s_out[n * rows : (n + 1) * rows] = total
+    back[nx + 1].start()
     t_log = column_log(t_out[...])
     s_log = column_log(s_out[...])
     for k in range(logs.shape[0]):
@@ -162,15 +147,14 @@
 
 
 def terms_kernel(
-    place, got, label, cot, t_logits, s_logits, student_rows, s_own, s_other,
+    place, got, label, cot, t_logits, s_logits, student_rows, s_heads_at,
     slope, sent, common, t_in, s_in, s_rows, s_heads, sems,
 ):
-    rows = s_own.shape[0]
+    rows = s_heads_at.shape[1]
     pairs = (
         (t_logits, t_in),
         (s_logits, s_in),
-        (s_own, s_heads.at[0:rows]),
-        (s_other, s_heads.at[rows:]),
+        (s_heads_at, s_heads),
         (student_rows, s_rows),
     )
     copies = [pltpu.make_async_copy(a, b, sems.at[k]) for k, (a, b) in enumerate(pairs)]
@@ -203,7 +187,8 @@
     slopes = slope[...]
     for x in range(nx):
         at = slice(x * qs, (x + 1) * qs)
-        terms = dot(slopes, s_heads[:, at], 0, 0)
+        terms = dot(slopes[:rows], s_heads[0, :, at], 0, 0)
+        terms += dot(slopes[rows:], s_heads[1, :, at], 0, 0)
         gain = jnp.sum(terms * s_rows[:, at].astype(f32), axis=0, keepdims=True)
         high = gain.astype(bf16).astype(f32)
         tail = jnp.where(line == 14, loss_high, jnp.where(line == 15, loss_terms - loss_high, 0.0))
@@ -293,14 +278,14 @@
     def start_of(core):
         return (((ix * nc + core) * nz + iz) * ny + iy) * rows
 
-    place = jnp.stack([ix, ic, start_of(ic), start_of(1 - ic)])
+    place = jnp.stack([ix, ic, start_of(0), start_of(1)])
     t_gain, s_gain = (g.reshape(-1, 128) for g in (teacher_gain, student_gain))
     pieces = called(
         norm_kernel,
         [SMEM] + [ANY] * 4,
         VMEM,
         shape((nz, half, qt + qs), bf16),
-        BIG,
+        NORM,
         [
             pltpu.VMEM((own, dt), bf16),
             pltpu.VMEM((own, ds), bf16),
@@ -313,24 +298,23 @@
         ],
     )(place, teacher_hidden, student_hidden, t_gain, s_gain)
 
-    pieces, teacher_head, student_head = lax.optimization_barrier(
-        (pieces, teacher_head, student_head)
-    )
-    teacher_other, student_other = (swapped(teacher_head), swapped(student_head))
-
     def of_tokens(a):
         mine = lax.dynamic_index_in_dim(a.reshape(nz, ny, nc, half), ic, 2, keepdims=False)
         return mine.transpose(1, 0, 2).reshape(1, tokens)
 
+    pieces, labels, cotangent = lax.optimization_barrier((pieces, labels, cotangent))
+    label, cot = (of_tokens(labels), of_tokens(cotangent))
+    t_heads, s_heads = (lax.all_gather(a, C) for a in (teacher_head, student_head))
+
     line = exchanged(pieces, Z).reshape(held, qt + qs)
-    line, teacher_other, student_other, label, cot = lax.optimization_barrier(
-        (line, teacher_other, student_other, of_tokens(labels), of_tokens(cotangent))
+    line, label, cot, t_heads, s_heads = lax.optimization_barrier(
+        (line, label, cot, t_heads, s_heads)
     )
     plane = to_all(line, PLANE).reshape(nx, tokens, qt + qs)
 
     t_logits, s_logits, logs, student_rows = called(
         logits_kernel,
-        [ANY] * 5,
+        [VMEM] * 3,
         [ANY, ANY, VMEM, ANY],
         [
             shape((2 * rows, tokens), f32),
@@ -338,25 +322,20 @@
             shape((nx * ny, 2, tokens), f32),
             shape((tokens, ds), bf16),
         ],
-        BIG,
-        [
-            pltpu.VMEM((tokens, dt), bf16),
-            pltpu.VMEM((tokens, ds), bf16),
-            pltpu.VMEM((2 * rows, dt), bf16),
-            pltpu.VMEM((2 * rows, ds), bf16),
+        LOGITS,
+        [
             pltpu.VMEM((2 * rows, tokens), f32),
             pltpu.VMEM((2 * rows, tokens), f32),
-            pltpu.SemaphoreType.DMA((4 * nx + 2,)),
-            pltpu.SemaphoreType.DMA((3,)),
-        ],
-    )(plane, teacher_head, teacher_other, student_head, student_other)
+            pltpu.SemaphoreType.DMA((nx + 2,)),
+        ],
+    )(plane, t_heads, s_heads)
     logs = exchanged(logs, PLANE)
     logs = called(merge_kernel, [VMEM], VMEM, shape((nz, 2, tokens), f32), 4)(logs)
     logs = exchanged(logs, Z)
 
     slope, sent, common = called(
         terms_kernel,
-        [SMEM] + [VMEM] * 3 + [ANY] * 5,
+        [SMEM] + [VMEM] * 3 + [ANY] * 4,
         [VMEM] * 3,
         [
             shape((2 * rows, tokens), bf16),
@@ -368,18 +347,19 @@
             pltpu.VMEM((2 * rows, tokens), f32),
             pltpu.VMEM((2 * rows, tokens), f32),
             pltpu.VMEM((tokens, ds), bf16),
-            pltpu.VMEM((2 * rows, ds), bf16),
-            pltpu.SemaphoreType.DMA((5,)),
-        ],
-    )(place, logs, label, cot, t_logits, s_logits, student_rows, student_head, student_other)
+            pltpu.VMEM((nc, rows, ds), bf16),
+            pltpu.SemaphoreType.DMA((4,)),
+        ],
+    )(place, logs, label, cot, t_logits, s_logits, student_rows, s_heads)
     got = exchanged(sent.reshape(nx * ny, held, qs + 128), PLANE)
+    got = called(repack_kernel, [VMEM], VMEM, shape((nz, half, qs + 512), f32), 8)(got)
     got, student_rows, slope = lax.optimization_barrier((got, student_rows, slope))
-    got = called(repack_kernel, [VMEM], VMEM, shape((nz, half, qs + 512), f32), 8)(got)
     got = exchanged(got, Z)
 
+    mine = lax.dynamic_slice_in_dim(slope, ic * rows, rows, 0)
+    others = lax.dynamic_slice_in_dim(slope, (1 - ic) * rows, rows, 0)
     head_grad = (
-        dot(slope[:rows], student_rows, 1, 0)
-        + dot(swapped(slope[rows:]), swapped(student_rows), 1, 0)
+        dot(mine, student_rows, 1, 0) + dot(swapped(others), swapped(student_rows), 1, 0)
     ).astype(bf16)
 
     got = called(share_kernel, [VMEM] * 2, VMEM, shape((nx * nc, half, qs + 512), f32), 4)(

time: 178 us -> 209 us (1.17)
  waiting for transfers between devices: 22.4 us -> 53.5 us
  between operations: 0.81 us -> 14.3 us
  Pallas kernels: 15.2 us -> 9.74 us
  local copies, waits for them, and re-layouts: 6.36 us -> 2.02 us
  starting transfers between devices: 39.6 us -> 35.3 us
    all_gather x0 -> x2, waiting for transfers between devices: none -> 28.5 us  [on_device(): lax.all_gather(a, C)]
    ppermute x4 -> x2, starting transfers between devices: 20.6 us -> 10.1 us  [swapped(): return lax.ppermute(x, C, [(0, 1), (1, 0)])]
    all_to_all x3, starting transfers between devices: 19.1 us -> 25.2 us  [exchanged(): return lax.all_to_all(x, axes, 0, 0, tiled=True)]
    pallas_call x2, Pallas kernels: 11.1 us -> 5.53 us  [the longest x1 2.98 us: on_device(): called(logits_kernel, [VMEM] * 3, [ANY, ANY, VMEM, ANY], [shape((2 * rows...]
    unnamed x14 -> x16, local copies, waits for them, and re-layouts: 3.02 us -> 0.03 us
  transfers between devices with their start and end apart: 7 -> 7, of which waited for: 3 -> 4; matrix products, arithmetic and copies ran while one was open for 4% -> 2% of each run, Pallas kernels for 1% -> 1%
where the time goes in v4:
time: 209 us
  blocking collectives  90.8 us (43%)
  waiting for transfers between devices  53.5 us (26%)
  starting transfers between devices  35.3 us (17%)
  between operations  14.3 us (7%)
  Pallas kernels  9.74 us (5%)
  matrix products  3.07 us (1%)
    all_to_all x4, blocking collectives, exchanged(): return lax.all_to_all(x, axes, 0, 0, tiled=True)  90.8 us
    all_gather x2, waiting for transfers between devices, on_device(): lax.all_gather(a, C)  28.5 us
    all_to_all x3, starting transfers between devices, exchanged(): return lax.all_to_all(x, axes, 0, 0, tiled=True)  25.2 us
    all_to_all x3, waiting for transfers between devices, exchanged(): return lax.all_to_all(x, axes, 0, 0, tiled=True)  23.6 us
    ppermute x2, starting transfers between devices, swapped(): return lax.ppermute(x, C, [(0, 1), (1, 0)])  10.1 us
  transfers between devices with their start and end apart: 7, of which 4 were waited for; matrix products, arithmetic and copies ran while one was open for 2% of the time, Pallas kernels for 1%

profile of v4, /device:TPU:1, one launch (start us, length us, event | category | flops | bytes accessed | tf_op | source)
XLA Modules:
  0.0 208.8 jit_solution(7707628920522994629)
XLA Ops:
  7.2 0.0 copy-start.4
  7.2 0.0 copy-start.5
  7.2 0.0 copy-start.3
  7.2 0.0 copy-start.2
  7.2 0.0 copy-start.6
  7.2 0.0 copy-start.7
  7.2 0.0 all-gather.7.cloned.1.call-start
  7.3 0.7 all-gather.7.cloned.1.call-update
  8.0 0.0 all-gather.5.cloned.1.call-start
  8.0 0.7 all-gather.5.cloned.1.call-update
  8.7 0.1 pad_add_fusion.place
  8.8 0.0 copy-done.4
  8.8 0.0 copy-done.5
  8.8 0.0 copy-done.3
  8.8 0.0 copy-done.2
  8.8 1.8 shard_map.111
  10.6 15.8 %all-to-all-start = ((bf16[16,2,2944]{2,1,0:T(2,128)(2,1)}), bf16[16,2,2944]{2,1,0:T(2,128)(2,1)S(1)}, u32[]{:S(2)}, u32[]{:S(2)}) async-start(bf16[16,2,2944]{2,1,0:T(2,128)(2,1)} %shard_map.111), calls=%async_computation | async-start | bytes 376832 | tf_op jit(solution)/shard_map/all_to_all | solution.py:35
  26.4 0.0 copy-done.6
  26.4 0.2 reshape.45
  26.6 0.1 copy.14
  26.7 0.1 copy.15
  26.8 0.1 reshape.46.label
  27.0 0.0 copy-done.7
  27.0 0.2 reshape.47
  27.2 0.1 copy.16
  27.3 0.1 copy.17
  27.4 0.1 reshape.48.cot
  27.5 11.3 %all-to-all-done = bf16[16,2,2944]{2,1,0:T(2,128)(2,1)S(1)} async-done(((bf16[16,2,2944]{2,1,0:T(2,128)(2,1)}), bf16[16,2,2944]{2,1,0:T(2,128)(2,1)S(1)}, u32[]{:S(2)}, u32[]{:S(2)}) %all-to-all-start) | async-done | bytes 188448 | tf_op jit(solution)/shard_map/all_to_all | solution.py:35
  38.8 0.1 reshape.44
  38.9 0.0 all-gather.7.cloned.1.call-done
  38.9 28.5 %all-gather.5.cloned.1.call-done = bf16[320,8192]{1,0:T(8,128)(2,1)} async-done(((bf16[160,8192]{1,0:T(8,128)(2,1)}), bf16[320,8192]{1,0:T(8,128)(2,1)}) %all-gather.5.cloned.1.call-update) | async-done | bytes 5242896 | tf_op jit(solution)/shard_map/all_gather | solution.py:307
  67.4 0.0 copy-start.1
  67.4 0.2 broadcast_in_dim.2
  67.6 0.0 copy-start
  67.6 42.7 %all_to_all.35 = bf16[16,32,2944]{2,1,0:T(8,128)(2,1)S(1)} all-to-all(bf16[16,32,2944]{2,1,0:T(8,128)(2,1)S(1)} %broadcast_in_dim.2), channel_id=1, replica_groups=mesh['section_0'=4,'section_1'=2,'dp_0'=16,'dp_1'=4] {'section_0','dp_1'}, dimensions={0} | all-to-all | bytes 6029312 | tf_op jit(solution)/shard_map/all_to_all | solution.py:35
  110.4 0.0 copy-done.1
  110.4 0.0 copy-done
  110.4 3.0 %shard_map.112 = (f32[320,128]{1,0:T(8,128)S(1)}, f32[320,128]{1,0:T(8,128)S(1)}, f32[16,2,128]{2,1,0:T(2,128)S(1)}, bf16[128,3584]{1,0:T(8,128)(2,1)S(1)}) custom-call(bf16[4,128,2944]{2,1,0:T(8,128)(2,1)S(1)} %bitcast.21, bf16[2,160,8192]{2,1,0:T(8,128)(2,1)S(1)} %bitcast.24, bf16[2,160,3584]{2,1,0:T(8,128)(2,1)S(1)} %bitcast.22), custom_call_target="tpu_custom_call" | custom-call | tf_op jit(solution)/shard_map/pallas_call | solution.py:315
  113.4 10.0 %all_to_all.36.got = f32[16,2,128]{2,1,0:T(2,128)S(1)} all-to-all(f32[16,2,128]{2,1,0:T(2,128)S(1)} %get-tuple-element.33), channel_id=1, replica_groups=mesh['section_0'=4,'section_1'=2,'dp_0'=16,'dp_1'=4] {'section_0','dp_1'}, dimensions={0} | all-to-all | bytes 32768 | tf_op jit(solution)/shard_map/all_to_all | solution.py:35
  123.5 23.2 %all_to_all.37.got = f32[16,2,128]{2,1,0:T(2,128)S(1)} all-to-all(f32[16,2,128]{2,1,0:T(2,128)S(1)} %shard_map.113), channel_id=1, replica_groups=mesh['section_0'=4,'section_1'=2,'dp_0'=16,'dp_1'=4] {'dp_0'}, dimensions={0} | all-to-all | bytes 32768 | tf_op jit(solution)/shard_map/all_to_all | solution.py:35
  146.7 2.5 %shard_map.114 = (bf16[320,128]{1,0:T(8,128)(2,1)S(1)}, bf16[4,4,32,1024]{3,2,1,0:T(8,128)(2,1)S(1)}, f32[1,128]{1,0:T(1,128)S(1)}) custom-call(s32[4]{0:T(128)S(1)} %pad_add_fusion.place, f32[16,2,128]{2,1,0:T(2,128)S(1)} %all_to_all.37.got, s32[1,128]{1,0:T(1,128)S(1)} %reshape.46.label, f32[1,128]{1,0:T(1,128)S(1)} %reshape.48.cot, ...), custom_call_target="tpu_custom_call" | custom-call | tf_op jit(solution)/shard_map/pallas_call | solution.py:336
  149.2 14.8 %all_to_all.38.got = bf16[16,32,1024]{2,1,0:T(8,128)(2,1)S(1)} all-to-all(bf16[16,32,1024]{2,1,0:T(8,128)(2,1)S(1)} %bitcast.25), channel_id=1, replica_groups=mesh['section_0'=4,'section_1'=2,'dp_0'=16,'dp_1'=4] {'section_0','dp_1'}, dimensions={0} | all-to-all | bytes 2097152 | tf_op jit(solution)/shard_map/all_to_all | solution.py:35
  164.1 0.8 shard_map.115
  164.9 8.1 %collective-permute-start.1 = (bf16[128,3584]{1,0:T(8,128)(2,1)S(1)}, bf16[128,3584]{1,0:T(8,128)(2,1)}, u32[]{:S(2)}, u32[]{:S(2)}) collective-permute-start(bf16[128,3584]{1,0:T(8,128)(2,1)S(1)} %get-tuple-element.44.student_rows), channel_id=1, source_target_pairs={{0,64},{64,0},{1,65},{65,1},{2,66},{66,2},{3,67},{67,3},{4,68},{68... | collective-permute-start | bytes 2752520 | tf_op jit(solution)/shard_map/ppermute | solution.py:39
  173.0 3.5 %all-to-all-start.5 = ((f32[16,2,1408]{2,1,0:T(2,128)}), f32[16,2,1408]{2,1,0:T(2,128)S(1)}, u32[]{:S(2)}, u32[]{:S(2)}) async-start(f32[16,2,1408]{2,1,0:T(2,128)} %shard_map.115), calls=%async_computation.5 | async-start | bytes 360448 | tf_op jit(solution)/shard_map/all_to_all | solution.py:35
  176.6 0.6 constant_dynamic-slice_fusion
  177.2 1.9 collective-permute-start
  179.1 0.4 fusion.1
  179.6 10.0 %all-to-all-done.5.got = f32[16,2,1408]{2,1,0:T(2,128)S(1)} async-done(((f32[16,2,1408]{2,1,0:T(2,128)}), f32[16,2,1408]{2,1,0:T(2,128)S(1)}, u32[]{:S(2)}, u32[]{:S(2)}) %all-to-all-start.5) | async-done | bytes 180256 | tf_op jit(solution)/shard_map/all_to_all | solution.py:35
  189.6 0.7 shard_map.116
  190.3 5.9 %all-to-all-start.6 = ((f32[8,2,1408]{2,1,0:T(2,128)}), f32[8,2,1408]{2,1,0:T(2,128)S(1)}, u32[]{:S(2)}, u32[]{:S(2)}) async-start(f32[8,2,1408]{2,1,0:T(2,128)} %shard_map.116), calls=%async_computation.6 | async-start | bytes 180224 | tf_op jit(solution)/shard_map/all_to_all | solution.py:35
  196.2 0.0 collective-permute-done
  196.2 0.0 collective-permute-done.1
  196.2 2.6 %fusion = bf16[160,3584]{1,0:T(8,128)(2,1)} fusion(f32[160,3584]{1,0:T(8,128)S(1)} %fusion.1, bf16[160,128]{1,0:T(8,128)(2,1)S(1)} %collective-permute-done, bf16[128,3584]{1,0:T(8,128)(2,1)} %collective-permute-done.1), kind=kOutput, calls=%fused_computation.1 | convolution fusion | flops 147947520 | bytes 4399104 | tf_op jit(solution)/shard_map/dot_general | solution.py:43
  198.8 2.3 %all-to-all-done.6.got = f32[8,2,1408]{2,1,0:T(2,128)S(1)} async-done(((f32[8,2,1408]{2,1,0:T(2,128)}), f32[8,2,1408]{2,1,0:T(2,128)S(1)}, u32[]{:S(2)}, u32[]{:S(2)}) %all-to-all-start.6) | async-done | bytes 90144 | tf_op jit(solution)/shard_map/all_to_all | solution.py:35
  201.1 0.9 shard_map.117
  (3 shorter events, 0.1 us)
Async XLA Ops:
  7.2 1.6 copy-start.4
  7.2 1.6 copy-start.5
  7.2 1.6 copy-start.3
  7.2 1.6 copy-start.2
  7.2 19.2 %copy-start.6 = (s32[256]{0:T(256)S(1)}, s32[256]{0:T(256)}, u32[]{:S(2)}) copy-start(s32[256]{0:T(256)} %param.14) | copy-start | bytes 3076
  7.2 19.8 %copy-start.7 = (f32[256]{0:T(256)S(1)}, f32[256]{0:T(256)}, u32[]{:S(2)}) copy-start(f32[256]{0:T(256)} %param.15) | copy-start | bytes 3076
  7.2 31.7 %all-gather.7.cloned.1.call-start = ((), (), s32[]{:S(2)}) async-start(), calls=%async_computation.8 | async-start | bytes 3440640 | tf_op jit(solution)/shard_map/all_gather | solution.py:307
  8.0 59.4 %all-gather.5.cloned.1.call-start = ((), (), s32[]{:S(2)}) async-start(), calls=%async_computation.7 | async-start | bytes 7864320 | tf_op jit(solution)/shard_map/all_gather | solution.py:307
  10.6 28.2 %all-to-all-start = ((bf16[16,2,2944]{2,1,0:T(2,128)(2,1)}), bf16[16,2,2944]{2,1,0:T(2,128)(2,1)S(1)}, u32[]{:S(2)}, u32[]{:S(2)}) async-start(bf16[16,2,2944]{2,1,0:T(2,128)(2,1)} %shard_map.111), calls=%async_computation | async-start | bytes 376832 | tf_op jit(solution)/shard_map/all_to_all | solution.py:35
  67.4 43.0 %copy-start.1 = (bf16[320,8192]{1,0:T(8,128)(2,1)S(1)}, bf16[320,8192]{1,0:T(8,128)(2,1)}, u32[]{:S(2)}) copy-start(bf16[320,8192]{1,0:T(8,128)(2,1)} %all-gather.5.cloned.1.call-done) | copy-start | bytes 15728644
  67.6 42.8 %copy-start = (bf16[320,3584]{1,0:T(8,128)(2,1)S(1)}, bf16[320,3584]{1,0:T(8,128)(2,1)}, u32[]{:S(2)}) copy-start(bf16[320,3584]{1,0:T(8,128)(2,1)} %all-gather.7.cloned.1.call-done) | copy-start | bytes 6881284
  164.9 31.3 %collective-permute-start.1 = (bf16[128,3584]{1,0:T(8,128)(2,1)S(1)}, bf16[128,3584]{1,0:T(8,128)(2,1)}, u32[]{:S(2)}, u32[]{:S(2)}) collective-permute-start(bf16[128,3584]{1,0:T(8,128)(2,1)S(1)} %get-tuple-element.44.student_rows), channel_id=1, source_target_pairs={{0,64},{64,0},{1,65},{65,1},{2,66},{66,2},{3,67},{67,3},{4,68},{68... | collective-permute-start | bytes 2752520 | tf_op jit(solution)/shard_map/ppermute | solution.py:39
  173.0 16.6 %all-to-all-start.5 = ((f32[16,2,1408]{2,1,0:T(2,128)}), f32[16,2,1408]{2,1,0:T(2,128)S(1)}, u32[]{:S(2)}, u32[]{:S(2)}) async-start(f32[16,2,1408]{2,1,0:T(2,128)} %shard_map.115), calls=%async_computation.5 | async-start | bytes 360448 | tf_op jit(solution)/shard_map/all_to_all | solution.py:35
  177.2 19.0 %collective-permute-start = (bf16[160,128]{1,0:T(8,128)(2,1)}, bf16[160,128]{1,0:T(8,128)(2,1)S(1)}, u32[]{:S(2)}, u32[]{:S(2)}) collective-permute-start(bf16[160,128]{1,0:T(8,128)(2,1)} %constant_dynamic-slice_fusion), channel_id=1, source_target_pairs={{0,64},{64,0},{1,65},{65,1},{2,66},{66,2},{3,67},{67,3},{4,68},{68... | collective-permute-start | bytes 122888 | tf_op jit(solution)/shard_map/ppermute | solution.py:39
  190.3 10.9 %all-to-all-start.6 = ((f32[8,2,1408]{2,1,0:T(2,128)}), f32[8,2,1408]{2,1,0:T(2,128)S(1)}, u32[]{:S(2)}, u32[]{:S(2)}) async-start(f32[8,2,1408]{2,1,0:T(2,128)} %shard_map.116), calls=%async_computation.6 | async-start | bytes 180224 | tf_op jit(solution)/shard_map/all_to_all | solution.py:35
Sparse Core Ops, SparseCore 0:
  10.1 28.0 all-gather.6
  40.4 27.0 all-gather.4

commit v5 on v4

--- a/solution.py
+++ b/solution.py
@@ -20,7 +20,7 @@
 SMEM = pl.BlockSpec(memory_space=pltpu.SMEM)
 ANY = pl.BlockSpec(memory_space=pl.ANY)
 MIB = 2**20
-NORM = 8
+NORM = 63
 LOGITS = 8
 BIG = 16
 shape = jax.ShapeDtypeStruct
@@ -101,12 +101,12 @@
 
 
 def logits_kernel(
-    plane, t_heads, s_heads, t_logits, s_logits, logs, student_rows, t_out, s_out, sems
+    plane, t_own, t_other, s_own, s_other, t_logits, s_logits, logs, student_rows, t_out, s_out, sems
 ):
     nx = plane.shape[0]
-    nc, rows, dt = t_heads.shape
+    rows, dt = t_own.shape
     qt = dt // nx
-    qs = s_heads.shape[2] // nx
+    qs = s_own.shape[1] // nx
     back = [
         pltpu.make_async_copy(
             plane.at[k, :, qt:], student_rows.at[:, k * qs : (k + 1) * qs], sems.at[k]
@@ -117,16 +117,16 @@
     back.append(pltpu.make_async_copy(s_out, s_logits, sems.at[nx + 1]))
     for copy in back[:nx]:
         copy.start()
-    for n in range(nc):
+    for n, head in enumerate((t_own, t_other)):
         total = 0.0
         for k in range(nx):
-            total += dot(t_heads[n, :, k * qt : (k + 1) * qt], plane[k, :, 0:qt], 1, 1)
+            total += dot(head[:, k * qt : (k + 1) * qt], plane[k, :, 0:qt], 1, 1)
         t_out[n * rows : (n + 1) * rows] = total
     back[nx].start()
-    for n in range(nc):
+    for n, head in enumerate((s_own, s_other)):
         total = 0.0
         for k in range(nx):
-            total += dot(s_heads[n, :, k * qs : (k + 1) * qs], plane[k, :, qt:], 1, 1)
+            total += dot(head[:, k * qs : (k + 1) * qs], plane[k, :, qt:], 1, 1)
         s_out[n * rows : (n + 1) * rows] = total
     back[nx + 1].start()
     t_log = column_log(t_out[...])
@@ -147,14 +147,15 @@
 
 
 def terms_kernel(
-    place, got, label, cot, t_logits, s_logits, student_rows, s_heads_at,
+    place, got, label, cot, t_logits, s_logits, student_rows, s_own, s_other,
     slope, sent, common, t_in, s_in, s_rows, s_heads, sems,
 ):
-    rows = s_heads_at.shape[1]
+    rows = s_own.shape[0]
     pairs = (
         (t_logits, t_in),
         (s_logits, s_in),
-        (s_heads_at, s_heads),
+        (s_own, s_heads.at[0]),
+        (s_other, s_heads.at[1]),
         (student_rows, s_rows),
     )
     copies = [pltpu.make_async_copy(a, b, sems.at[k]) for k, (a, b) in enumerate(pairs)]
@@ -278,7 +279,7 @@
     def start_of(core):
         return (((ix * nc + core) * nz + iz) * ny + iy) * rows
 
-    place = jnp.stack([ix, ic, start_of(0), start_of(1)])
+    place = jnp.stack([ix, ic, start_of(ic), start_of(1 - ic)])
     t_gain, s_gain = (g.reshape(-1, 128) for g in (teacher_gain, student_gain))
     pieces = called(
         norm_kernel,
@@ -304,17 +305,20 @@
 
     pieces, labels, cotangent = lax.optimization_barrier((pieces, labels, cotangent))
     label, cot = (of_tokens(labels), of_tokens(cotangent))
-    t_heads, s_heads = (lax.all_gather(a, C) for a in (teacher_head, student_head))
+    pieces, teacher_head, student_head = lax.optimization_barrier(
+        (pieces, teacher_head, student_head)
+    )
+    teacher_other, student_other = (swapped(teacher_head), swapped(student_head))
 
     line = exchanged(pieces, Z).reshape(held, qt + qs)
-    line, label, cot, t_heads, s_heads = lax.optimization_barrier(
-        (line, label, cot, t_heads, s_heads)
+    line, label, cot, teacher_other, student_other = lax.optimization_barrier(
+        (line, label, cot, teacher_other, student_other)
     )
     plane = to_all(line, PLANE).reshape(nx, tokens, qt + qs)
 
     t_logits, s_logits, logs, student_rows = called(
         logits_kernel,
-        [VMEM] * 3,
+        [VMEM] * 5,
         [ANY, ANY, VMEM, ANY],
         [
             shape((2 * rows, tokens), f32),
@@ -328,14 +332,14 @@
             pltpu.VMEM((2 * rows, tokens), f32),
             pltpu.SemaphoreType.DMA((nx + 2,)),
         ],
-    )(plane, t_heads, s_heads)
+    )(plane, teacher_head, teacher_other, student_head, student_other)
     logs = exchanged(logs, PLANE)
     logs = called(merge_kernel, [VMEM], VMEM, shape((nz, 2, tokens), f32), 4)(logs)
     logs = exchanged(logs, Z)
 
     slope, sent, common = called(
         terms_kernel,
-        [SMEM] + [VMEM] * 3 + [ANY] * 4,
+        [SMEM] + [VMEM] * 3 + [ANY] * 5,
         [VMEM] * 3,
         [
             shape((2 * rows, tokens), bf16),
@@ -348,18 +352,18 @@
             pltpu.VMEM((2 * rows, tokens), f32),
             pltpu.VMEM((tokens, ds), bf16),
             pltpu.VMEM((nc, rows, ds), bf16),
-            pltpu.SemaphoreType.DMA((4,)),
+            pltpu.SemaphoreType.DMA((5,)),
         ],
-    )(place, logs, label, cot, t_logits, s_logits, student_rows, s_heads)
+    )(place, logs, label, cot, t_logits, s_logits, student_rows, student_head, student_other)
     got = exchanged(sent.reshape(nx * ny, held, qs + 128), PLANE)
     got = called(repack_kernel, [VMEM], VMEM, shape((nz, half, qs + 512), f32), 8)(got)
-    got, student_rows, slope = lax.optimization_barrier((got, student_rows, slope))
+    got, slope = lax.optimization_barrier((got, slope))
     got = exchanged(got, Z)
-
-    mine = lax.dynamic_slice_in_dim(slope, ic * rows, rows, 0)
-    others = lax.dynamic_slice_in_dim(slope, (1 - ic) * rows, rows, 0)
+    slope_other, student_rows = lax.optimization_barrier((slope[rows:], student_rows))
+
     head_grad = (
-        dot(mine, student_rows, 1, 0) + dot(swapped(others), swapped(student_rows), 1, 0)
+        dot(slope[:rows], student_rows, 1, 0)
+        + dot(swapped(slope_other), swapped(student_rows), 1, 0)
     ).astype(bf16)
 
     got = called(share_kernel, [VMEM] * 2, VMEM, shape((nx * nc, half, qs + 512), f32), 4)(

time: 209 us -> 172 us (0.82)
  waiting for transfers between devices: 53.5 us -> 21.1 us
  between operations: 14.3 us -> 0.81 us
  starting transfers between devices: 35.3 us -> 39.7 us
  Pallas kernels: 9.74 us -> 12.3 us
  blocking collectives: 90.8 us -> 88.7 us
    all_gather x2 -> x0, waiting for transfers between devices: 28.5 us -> none  [on_device(): lax.all_gather(a, C)]
    ppermute x2 -> x4, starting transfers between devices: 10.1 us -> 20.5 us  [swapped(): return lax.ppermute(x, C, [(0, 1), (1, 0)])]
    all_to_all x3, starting transfers between devices: 25.2 us -> 19.1 us  [exchanged(): return lax.all_to_all(x, axes, 0, 0, tiled=True)]
    all_to_all x3, waiting for transfers between devices: 23.6 us -> 21.1 us  [exchanged(): return lax.all_to_all(x, axes, 0, 0, tiled=True)]
    all_to_all x4, blocking collectives: 90.8 us -> 88.7 us  [exchanged(): return lax.all_to_all(x, axes, 0, 0, tiled=True)]
  transfers between devices with their start and end apart: 7 -> 7, of which waited for: 4 -> 3; matrix products, arithmetic and copies ran while one was open for 2% -> 4% of each run, Pallas kernels for 1% -> 0%
where the time goes in v5:
time: 172 us; the launch traced here: 171 us
  blocking collectives  88.7 us (52%)
  starting transfers between devices  39.7 us (23%)
  waiting for transfers between devices  21.1 us (12%)
  Pallas kernels  12.3 us (7%)
  matrix products  4.95 us (3%)
  local copies, waits for them, and re-layouts  2.75 us (2%)
    all_to_all x4, blocking collectives, exchanged(): return lax.all_to_all(x, axes, 0, 0, tiled=True)  88.7 us
    all_to_all x3, waiting for transfers between devices, exchanged(): return lax.all_to_all(x, axes, 0, 0, tiled=True)  21.1 us
    ppermute x4, starting transfers between devices, swapped(): return lax.ppermute(x, C, [(0, 1), (1, 0)])  20.5 us
    all_to_all x3, starting transfers between devices, exchanged(): return lax.all_to_all(x, axes, 0, 0, tiled=True)  19.1 us
    dot_general x2, matrix products, dot(): lax.dot_general(a, b, (((along_a,), (along_b,)), ((), ())), preferred_ele...  4.95 us
    pallas_call x1, Pallas kernels, on_device(): called(logits_kernel, [VMEM] * 5, [ANY, ANY, VMEM, ANY], [shape((2 * rows...  4.72 us
  transfers between devices with their start and end apart: 7, of which 3 were waited for; matrix products, arithmetic and copies ran while one was open for 4% of the time, Pallas kernels for 0%

profile of v5, /device:TPU:1, one launch (start us, length us, event | category | flops | bytes accessed | tf_op | source)
XLA Modules:
  0.0 171.0 jit_solution(8518507411725165590)
XLA Ops:
  0.6 0.6 pad_add_fusion.place
  1.3 2.6 %shard_map.111 = bf16[16,2,2944]{2,1,0:T(2,128)(2,1)} custom-call(s32[4]{0:T(128)} %pad_add_fusion.place, bf16[4,8192]{1,0:T(4,128)(2,1)} %teacher_at.1, bf16[4,3584]{1,0:T(4,128)(2,1)} %hidden.1, bf16[64,128]{1,0:T(8,128)(2,1)} %bitcast.23, bf16[28,128]{1,0:T(8,128)(2,1)} %bitcast.21), custom_call_target="tpu_custom_call" | custom-call | tf_op jit(solution)/shard_map/pallas_call | solution.py:284
  3.9 8.8 %collective-permute-start = (bf16[160,8192]{1,0:T(8,128)(2,1)}, bf16[160,8192]{1,0:T(8,128)(2,1)}, u32[]{:S(2)}, u32[]{:S(2)}) collective-permute-start(bf16[160,8192]{1,0:T(8,128)(2,1)} %t_own), channel_id=1, source_target_pairs={{0,64},{64,0},{1,65},{65,1},{2,66},{66,2},{3,67},{67,3},{4,68},{68... | collective-permute-start | bytes 7864328 | tf_op jit(solution)/shard_map/ppermute | solution.py:39
  12.7 1.9 %collective-permute-start.1 = (bf16[160,3584]{1,0:T(8,128)(2,1)}, bf16[160,3584]{1,0:T(8,128)(2,1)S(1)}, u32[]{:S(2)}, u32[]{:S(2)}) collective-permute-start(bf16[160,3584]{1,0:T(8,128)(2,1)} %s_own.1), channel_id=1, source_target_pairs={{0,64},{64,0},{1,65},{65,1},{2,66},{66,2},{3,67},{67,3},{4,68},{68... | collective-permute-start | bytes 3440648 | tf_op jit(solution)/shard_map/ppermute | solution.py:39
  14.6 9.6 %all-to-all-start = ((bf16[16,2,2944]{2,1,0:T(2,128)(2,1)}), bf16[16,2,2944]{2,1,0:T(2,128)(2,1)S(1)}, u32[]{:S(2)}, u32[]{:S(2)}) async-start(bf16[16,2,2944]{2,1,0:T(2,128)(2,1)} %shard_map.111), calls=%async_computation | async-start | bytes 376832 | tf_op jit(solution)/shard_map/all_to_all | solution.py:35
  24.2 0.8 reshape.45
  25.1 0.1 copy.14
  25.2 0.1 copy.15
  25.3 0.1 reshape.46.label
  25.4 0.8 reshape.47
  26.3 0.1 copy.16
  26.4 0.1 copy.17
  26.5 0.1 reshape.48.cot
  26.7 10.0 %all-to-all-done = bf16[16,2,2944]{2,1,0:T(2,128)(2,1)S(1)} async-done(((bf16[16,2,2944]{2,1,0:T(2,128)(2,1)}), bf16[16,2,2944]{2,1,0:T(2,128)(2,1)S(1)}, u32[]{:S(2)}, u32[]{:S(2)}) %all-to-all-start) | async-done | bytes 188448 | tf_op jit(solution)/shard_map/all_to_all | solution.py:35
  36.7 0.1 reshape.44
  36.8 0.0 collective-permute-done.1.s_other
  36.8 0.0 collective-permute-done.t_other
  36.8 0.2 broadcast_in_dim.2
  37.0 0.0 copy-start
  37.0 0.0 copy-start.1
  37.0 39.2 %all_to_all.35 = bf16[16,32,2944]{2,1,0:T(8,128)(2,1)S(1)} all-to-all(bf16[16,32,2944]{2,1,0:T(8,128)(2,1)S(1)} %broadcast_in_dim.2), channel_id=1, replica_groups=mesh['section_0'=4,'section_1'=2,'dp_0'=16,'dp_1'=4] {'section_0','dp_1'}, dimensions={0} | all-to-all | bytes 6029312 | tf_op jit(solution)/shard_map/all_to_all | solution.py:35
  76.2 0.0 copy-done
  76.2 0.0 copy-done.1
  76.2 0.0 copy-start.4
  76.2 4.7 %shard_map.112 = (f32[320,128]{1,0:T(8,128)S(1)}, f32[320,128]{1,0:T(8,128)S(1)}, f32[16,2,128]{2,1,0:T(2,128)S(1)}, bf16[128,3584]{1,0:T(8,128)(2,1)S(1)}) custom-call(bf16[4,128,2944]{2,1,0:T(8,128)(2,1)S(1)} %bitcast.19, bf16[160,8192]{1,0:T(8,128)(2,1)S(1)} %copy-done.1, bf16[160,8192]{1,0:T(8,128)(2,1)} %collective-permute-done.t_other, ...), custom_call_target="tpu_custom_call" | custom-call | tf_op jit(solution)/shard_map/pallas_call | solution.py:319
  81.0 10.5 %all_to_all.36.got = f32[16,2,128]{2,1,0:T(2,128)S(1)} all-to-all(f32[16,2,128]{2,1,0:T(2,128)S(1)} %get-tuple-element.40), channel_id=1, replica_groups=mesh['section_0'=4,'section_1'=2,'dp_0'=16,'dp_1'=4] {'section_0','dp_1'}, dimensions={0} | all-to-all | bytes 32768 | tf_op jit(solution)/shard_map/all_to_all | solution.py:35
  91.5 24.0 %all_to_all.37.got = f32[16,2,128]{2,1,0:T(2,128)S(1)} all-to-all(f32[16,2,128]{2,1,0:T(2,128)S(1)} %shard_map.113), channel_id=1, replica_groups=mesh['section_0'=4,'section_1'=2,'dp_0'=16,'dp_1'=4] {'dp_0'}, dimensions={0} | all-to-all | bytes 32768 | tf_op jit(solution)/shard_map/all_to_all | solution.py:35
  115.5 0.0 copy-done.4
  115.5 2.6 %shard_map.114 = (bf16[320,128]{1,0:T(8,128)(2,1)S(1)}, bf16[4,4,32,1024]{3,2,1,0:T(8,128)(2,1)S(1)}, f32[1,128]{1,0:T(1,128)S(1)}) custom-call(s32[4]{0:T(128)S(1)} %copy-done.4, f32[16,2,128]{2,1,0:T(2,128)S(1)} %all_to_all.37.got, s32[1,128]{1,0:T(1,128)S(1)} %reshape.46.label, f32[1,128]{1,0:T(1,128)S(1)} %reshape.48.cot, ...), custom_call_target="tpu_custom_call" | custom-call | tf_op jit(solution)/shard_map/pallas_call | solution.py:340
  118.1 15.1 %all_to_all.38.got = bf16[16,32,1024]{2,1,0:T(8,128)(2,1)S(1)} all-to-all(bf16[16,32,1024]{2,1,0:T(8,128)(2,1)S(1)} %bitcast.20), channel_id=1, replica_groups=mesh['section_0'=4,'section_1'=2,'dp_0'=16,'dp_1'=4] {'section_0','dp_1'}, dimensions={0} | all-to-all | bytes 2097152 | tf_op jit(solution)/shard_map/all_to_all | solution.py:35
  133.2 0.8 shard_map.115
  134.0 7.9 %collective-permute-start.3 = (bf16[128,3584]{1,0:T(8,128)(2,1)S(1)}, bf16[128,3584]{1,0:T(8,128)(2,1)S(1)}, u32[]{:S(2)}, u32[]{:S(2)}) collective-permute-start(bf16[128,3584]{1,0:T(8,128)(2,1)S(1)} %get-tuple-element.51.student_rows), channel_id=1, source_target_pairs={{0,64},{64,0},{1,65},{65,1},{2,66},{66,2},{3,67},{67,3},{4,68},{68... | collective-permute-start | bytes 2752520 | tf_op jit(solution)/shard_map/ppermute | solution.py:39
  141.9 3.5 %all-to-all-start.5 = ((f32[16,2,1408]{2,1,0:T(2,128)}), f32[16,2,1408]{2,1,0:T(2,128)S(1)}, u32[]{:S(2)}, u32[]{:S(2)}) async-start(f32[16,2,1408]{2,1,0:T(2,128)} %shard_map.115), calls=%async_computation.5 | async-start | bytes 360448 | tf_op jit(solution)/shard_map/all_to_all | solution.py:35
  145.4 1.9 %collective-permute-start.2 = (bf16[160,128]{1,0:T(8,128)(2,1)S(1)}, bf16[160,128]{1,0:T(8,128)(2,1)S(1)}, u32[]{:S(2)}, u32[]{:S(2)}) collective-permute-start(bf16[160,128]{1,0:T(8,128)(2,1)S(1)} %slice.7), channel_id=1, source_target_pairs={{0,64},{64,0},{1,65},{65,1},{2,66},{66,2},{3,67},{67,3},{4,68},{68... | collective-permute-start | bytes 122888 | tf_op jit(solution)/shard_map/ppermute | solution.py:39
  147.4 1.9 %fusion.1 = f32[160,3584]{1,0:T(8,128)} fusion(bf16[128,3584]{1,0:T(8,128)(2,1)S(1)} %get-tuple-element.51.student_rows, bf16[320,128]{1,0:T(8,128)(2,1)S(1)} %get-tuple-element.50), kind=kOutput, calls=%fused_computation.2 | convolution fusion | flops 146800640 | bytes 3252224 | tf_op jit(solution)/shard_map/dot_general | solution.py:43
  149.2 9.2 %all-to-all-done.5.got = f32[16,2,1408]{2,1,0:T(2,128)S(1)} async-done(((f32[16,2,1408]{2,1,0:T(2,128)}), f32[16,2,1408]{2,1,0:T(2,128)S(1)}, u32[]{:S(2)}, u32[]{:S(2)}) %all-to-all-start.5) | async-done | bytes 180256 | tf_op jit(solution)/shard_map/all_to_all | solution.py:35
  158.5 0.6 shard_map.116
  159.1 0.0 copy-start.2
  159.1 0.0 copy-start.3
  159.1 6.0 %all-to-all-start.6 = ((f32[8,2,1408]{2,1,0:T(2,128)}), f32[8,2,1408]{2,1,0:T(2,128)S(1)}, u32[]{:S(2)}, u32[]{:S(2)}) async-start(f32[8,2,1408]{2,1,0:T(2,128)} %shard_map.116), calls=%async_computation.6 | async-start | bytes 180224 | tf_op jit(solution)/shard_map/all_to_all | solution.py:35
  165.1 0.0 collective-permute-done.2
  165.1 0.0 collective-permute-done.3
  165.1 3.1 %fusion = bf16[160,3584]{1,0:T(8,128)(2,1)} fusion(f32[160,3584]{1,0:T(8,128)} %fusion.1, bf16[160,128]{1,0:T(8,128)(2,1)S(1)} %collective-permute-done.2, bf16[128,3584]{1,0:T(8,128)(2,1)S(1)} %collective-permute-done.3), kind=kOutput, calls=%fused_computation.1 | convolution fusion | flops 147947520 | bytes 4399104 | tf_op jit(solution)/shard_map/dot_general | solution.py:43
  168.2 1.9 %all-to-all-done.6.got = f32[8,2,1408]{2,1,0:T(2,128)S(1)} async-done(((f32[8,2,1408]{2,1,0:T(2,128)}), f32[8,2,1408]{2,1,0:T(2,128)S(1)}, u32[]{:S(2)}, u32[]{:S(2)}) %all-to-all-start.6) | async-done | bytes 90144 | tf_op jit(solution)/shard_map/all_to_all | solution.py:35
  170.1 0.0 copy-done.2
  170.1 0.0 copy-done.3
  170.1 0.9 shard_map.117
  (4 shorter events, 0.1 us)
Async XLA Ops:
  3.9 32.9 %collective-permute-start = (bf16[160,8192]{1,0:T(8,128)(2,1)}, bf16[160,8192]{1,0:T(8,128)(2,1)}, u32[]{:S(2)}, u32[]{:S(2)}) collective-permute-start(bf16[160,8192]{1,0:T(8,128)(2,1)} %t_own), channel_id=1, source_target_pairs={{0,64},{64,0},{1,65},{65,1},{2,66},{66,2},{3,67},{67,3},{4,68},{68... | collective-permute-start | bytes 7864328 | tf_op jit(solution)/shard_map/ppermute | solution.py:39
  12.7 24.1 %collective-permute-start.1 = (bf16[160,3584]{1,0:T(8,128)(2,1)}, bf16[160,3584]{1,0:T(8,128)(2,1)S(1)}, u32[]{:S(2)}, u32[]{:S(2)}) collective-permute-start(bf16[160,3584]{1,0:T(8,128)(2,1)} %s_own.1), channel_id=1, source_target_pairs={{0,64},{64,0},{1,65},{65,1},{2,66},{66,2},{3,67},{67,3},{4,68},{68... | collective-permute-start | bytes 3440648 | tf_op jit(solution)/shard_map/ppermute | solution.py:39
  14.6 22.1 %all-to-all-start = ((bf16[16,2,2944]{2,1,0:T(2,128)(2,1)}), bf16[16,2,2944]{2,1,0:T(2,128)(2,1)S(1)}, u32[]{:S(2)}, u32[]{:S(2)}) async-start(bf16[16,2,2944]{2,1,0:T(2,128)(2,1)} %shard_map.111), calls=%async_computation | async-start | bytes 376832 | tf_op jit(solution)/shard_map/all_to_all | solution.py:35
  37.0 39.2 %copy-start = (bf16[160,3584]{1,0:T(8,128)(2,1)S(1)}, bf16[160,3584]{1,0:T(8,128)(2,1)}, u32[]{:S(2)}) copy-start(bf16[160,3584]{1,0:T(8,128)(2,1)} %s_own.1) | copy-start | bytes 3440644
  37.0 39.2 %copy-start.1 = (bf16[160,8192]{1,0:T(8,128)(2,1)S(1)}, bf16[160,8192]{1,0:T(8,128)(2,1)}, u32[]{:S(2)}) copy-start(bf16[160,8192]{1,0:T(8,128)(2,1)} %t_own) | copy-start | bytes 7864324
  76.2 39.3 %copy-start.4 = (s32[4]{0:T(128)S(1)}, s32[4]{0:T(128)}, u32[]{:S(2)}) copy-start(s32[4]{0:T(128)} %pad_add_fusion.place) | copy-start | bytes 52
  134.0 31.2 %collective-permute-start.3 = (bf16[128,3584]{1,0:T(8,128)(2,1)S(1)}, bf16[128,3584]{1,0:T(8,128)(2,1)S(1)}, u32[]{:S(2)}, u32[]{:S(2)}) collective-permute-start(bf16[128,3584]{1,0:T(8,128)(2,1)S(1)} %get-tuple-element.51.student_rows), channel_id=1, source_target_pairs={{0,64},{64,0},{1,65},{65,1},{2,66},{66,2},{3,67},{67,3},{4,68},{68... | collective-permute-start | bytes 2752520 | tf_op jit(solution)/shard_map/ppermute | solution.py:39
  141.9 16.6 %all-to-all-start.5 = ((f32[16,2,1408]{2,1,0:T(2,128)}), f32[16,2,1408]{2,1,0:T(2,128)S(1)}, u32[]{:S(2)}, u32[]{:S(2)}) async-start(f32[16,2,1408]{2,1,0:T(2,128)} %shard_map.115), calls=%async_computation.5 | async-start | bytes 360448 | tf_op jit(solution)/shard_map/all_to_all | solution.py:35
  145.4 19.7 %collective-permute-start.2 = (bf16[160,128]{1,0:T(8,128)(2,1)S(1)}, bf16[160,128]{1,0:T(8,128)(2,1)S(1)}, u32[]{:S(2)}, u32[]{:S(2)}) collective-permute-start(bf16[160,128]{1,0:T(8,128)(2,1)S(1)} %slice.7), channel_id=1, source_target_pairs={{0,64},{64,0},{1,65},{65,1},{2,66},{66,2},{3,67},{67,3},{4,68},{68... | collective-permute-start | bytes 122888 | tf_op jit(solution)/shard_map/ppermute | solution.py:39
  159.1 11.0 %copy-start.2 = (bf16[4,3584]{1,0:T(4,128)(2,1)S(1)}, bf16[4,3584]{1,0:T(4,128)(2,1)}, u32[]{:S(2)}) copy-start(bf16[4,3584]{1,0:T(4,128)(2,1)} %hidden.1) | copy-start | bytes 86020
  159.1 11.0 %copy-start.3 = (bf16[3584]{0:T(1024)(128)(2,1)S(1)}, bf16[3584]{0:T(1024)(128)(2,1)}, u32[]{:S(2)}) copy-start(bf16[3584]{0:T(1024)(128)(2,1)} %param.11) | copy-start | bytes 21508
  159.1 11.0 %all-to-all-start.6 = ((f32[8,2,1408]{2,1,0:T(2,128)}), f32[8,2,1408]{2,1,0:T(2,128)S(1)}, u32[]{:S(2)}, u32[]{:S(2)}) async-start(f32[8,2,1408]{2,1,0:T(2,128)} %shard_map.116), calls=%async_computation.6 | async-start | bytes 180224 | tf_op jit(solution)/shard_map/all_to_all | solution.py:35

commit v6 on v5

--- a/solution.py
+++ b/solution.py
@@ -21,7 +21,7 @@
 ANY = pl.BlockSpec(memory_space=pl.ANY)
 MIB = 2**20
 NORM = 63
-LOGITS = 8
+LOGITS = 10
 BIG = 16
 shape = jax.ShapeDtypeStruct
 
@@ -64,7 +64,7 @@
 
 
 def norm_kernel(
-    place, teacher_at, student_at, t_gain_at, s_gain_at, out,
+    at_x, at_c, teacher_at, student_at, t_gain_at, s_gain_at, out,
     teacher, student, t_gain, s_gain, t_scaled, s_scaled, gains, sems,
 ):
     pairs = (
@@ -76,7 +76,7 @@
     copies = [pltpu.make_async_copy(a, b, sems.at[k]) for k, (a, b) in enumerate(pairs)]
     for copy in copies:
         copy.start()
-    ix, ic = (place[0], place[1])
+    ix, ic = (at_x[0], at_c[0])
     half = out.shape[1]
     at = 0
     for n, (hidden, gain, scaled) in enumerate(
@@ -101,12 +101,15 @@
 
 
 def logits_kernel(
-    plane, t_own, t_other, s_own, s_other, t_logits, s_logits, logs, student_rows, t_out, s_out, sems
+    plane, t_own, s_own, s_other, t_other_at, t_logits, s_logits, logs, student_rows,
+    t_other, t_out, s_out, sems,
 ):
     nx = plane.shape[0]
     rows, dt = t_own.shape
     qt = dt // nx
     qs = s_own.shape[1] // nx
+    late = pltpu.make_async_copy(t_other_at, t_other, sems.at[nx + 2])
+    late.start()
     back = [
         pltpu.make_async_copy(
             plane.at[k, :, qt:], student_rows.at[:, k * qs : (k + 1) * qs], sems.at[k]
@@ -117,18 +120,21 @@
     back.append(pltpu.make_async_copy(s_out, s_logits, sems.at[nx + 1]))
     for copy in back[:nx]:
         copy.start()
-    for n, head in enumerate((t_own, t_other)):
+    for out, n, head, at, width in (
+        (s_out, 0, s_own, qt, qs),
+        (s_out, 1, s_other, qt, qs),
+        (t_out, 0, t_own, 0, qt),
+        (t_out, 1, t_other, 0, qt),
+    ):
+        if head is t_other:
+            back[nx + 1].start()
+            late.wait()
         total = 0.0
         for k in range(nx):
-            total += dot(head[:, k * qt : (k + 1) * qt], plane[k, :, 0:qt], 1, 1)
-        t_out[n * rows : (n + 1) * rows] = total
+            part = plane[k, :, at : at + width]
+            total += dot(head[:, k * width : (k + 1) * width], part, 1, 1)
+        out[n * rows : (n + 1) * rows] = total
     back[nx].start()
-    for n, head in enumerate((s_own, s_other)):
-        total = 0.0
-        for k in range(nx):
-            total += dot(head[:, k * qs : (k + 1) * qs], plane[k, :, qt:], 1, 1)
-        s_out[n * rows : (n + 1) * rows] = total
-    back[nx + 1].start()
     t_log = column_log(t_out[...])
     s_log = column_log(s_out[...])
     for k in range(logs.shape[0]):
@@ -172,7 +178,7 @@
     for k in range(2):
         at = slice(k * rows, (k + 1) * rows)
         s_part, t_part = (s_in[at], t_in[at])
-        entry = lax.broadcasted_iota(jnp.int32, s_part.shape, 0) + place[2 + k]
+        entry = lax.broadcasted_iota(jnp.int32, s_part.shape, 0) + place[k]
         hits = entry == label[...]
         s_prob = jnp.exp(s_part - student_log)
         t_prob = jnp.exp(t_part - teacher_log)
@@ -212,21 +218,29 @@
     tail = total[0:16, qs:]
     lines = [tail[k : k + 1] + tail[7 + k : 8 + k] for k in range(7)]
     lines.append(tail[14:15] + tail[15:16])
-    pairs = [jnp.concatenate([lines[k], lines[4 + k]], axis=0) for k in range(4)]
+    pairs = []
+    for line in lines:
+        high = line.astype(bf16).astype(f32)
+        pairs.append(jnp.concatenate([high, line - high], axis=0).astype(bf16))
     for z in range(nz):
-        out[z, :, 0:qs] = total[z * half : (z + 1) * half, 0:qs]
-        for k in range(4):
+        out[z, :, 0:qs] = total[z * half : (z + 1) * half, 0:qs].astype(bf16)
+        for k in range(8):
             out[z, :, qs + k * 128 : qs + (k + 1) * 128] = pairs[k]
 
 
 def share_kernel(got, common, out):
-    total = got[0]
+    total = got[0].astype(f32)
     for k in range(1, got.shape[0]):
-        total += got[k]
-    width = out.shape[2] - 128
+        total += got[k].astype(f32)
+    qs = out.shape[2] - 512
+    lines = [total[0:1, qs + k * 128 : qs + (k + 1) * 128] for k in range(8)]
+    lines = [x + total[1:2, qs + k * 128 : qs + (k + 1) * 128] for k, x in enumerate(lines)]
+    lines[7] += common[...]
     for k in range(out.shape[0]):
-        out[k] = total
-        out[k, 1:2, width:] = total[1:2, width:] + common[...]
+        out[k, :, 0:qs] = total[:, 0:qs]
+        for n in range(8):
+            at = qs + (n % 4) * 128
+            out[k, n // 4 : n // 4 + 1, at : at + 128] = lines[n]
 
 
 def final_kernel(got, hidden, gain, student_grad, gain_grad, loss, gains):
@@ -279,11 +293,10 @@
     def start_of(core):
         return (((ix * nc + core) * nz + iz) * ny + iy) * rows
 
-    place = jnp.stack([ix, ic, start_of(ic), start_of(1 - ic)])
     t_gain, s_gain = (g.reshape(-1, 128) for g in (teacher_gain, student_gain))
     pieces = called(
         norm_kernel,
-        [SMEM] + [ANY] * 4,
+        [SMEM] * 2 + [ANY] * 4,
         VMEM,
         shape((nz, half, qt + qs), bf16),
         NORM,
@@ -297,13 +310,13 @@
             pltpu.VMEM((dt // 128, 128), f32),
             pltpu.SemaphoreType.DMA((4,)),
         ],
-    )(place, teacher_hidden, student_hidden, t_gain, s_gain)
+    )(ix[None], ic[None], teacher_hidden, student_hidden, t_gain, s_gain)
 
     def of_tokens(a):
         mine = lax.dynamic_index_in_dim(a.reshape(nz, ny, nc, half), ic, 2, keepdims=False)
         return mine.transpose(1, 0, 2).reshape(1, tokens)
 
-    pieces, labels, cotangent = lax.optimization_barrier((pieces, labels, cotangent))
+    pieces, labels, cotangent, ix = lax.optimization_barrier((pieces, labels, cotangent, ix))
     label, cot = (of_tokens(labels), of_tokens(cotangent))
     pieces, teacher_head, student_head = lax.optimization_barrier(
         (pieces, teacher_head, student_head)
@@ -311,14 +324,15 @@
     teacher_other, student_other = (swapped(teacher_head), swapped(student_head))
 
     line = exchanged(pieces, Z).reshape(held, qt + qs)
-    line, label, cot, teacher_other, student_other = lax.optimization_barrier(
-        (line, label, cot, teacher_other, student_other)
+    place = jnp.stack([start_of(ic), start_of(1 - ic)])
+    line, place, label, cot, teacher_other, student_other = lax.optimization_barrier(
+        (line, place, label, cot, teacher_other, student_other)
     )
     plane = to_all(line, PLANE).reshape(nx, tokens, qt + qs)
 
     t_logits, s_logits, logs, student_rows = called(
         logits_kernel,
-        [VMEM] * 5,
+        [VMEM] * 4 + [ANY],
         [ANY, ANY, VMEM, ANY],
         [
             shape((2 * rows, tokens), f32),
@@ -328,11 +342,12 @@
         ],
         LOGITS,
         [
+            pltpu.VMEM((rows, dt), bf16),
             pltpu.VMEM((2 * rows, tokens), f32),
             pltpu.VMEM((2 * rows, tokens), f32),
-            pltpu.SemaphoreType.DMA((nx + 2,)),
+            pltpu.SemaphoreType.DMA((nx + 3,)),
         ],
-    )(plane, teacher_head, teacher_other, student_head, student_other)
+    )(plane, teacher_head, student_head, student_other, teacher_other)
     logs = exchanged(logs, PLANE)
     logs = called(merge_kernel, [VMEM], VMEM, shape((nz, 2, tokens), f32), 4)(logs)
     logs = exchanged(logs, Z)
@@ -356,7 +371,7 @@
         ],
     )(place, logs, label, cot, t_logits, s_logits, student_rows, student_head, student_other)
     got = exchanged(sent.reshape(nx * ny, held, qs + 128), PLANE)
-    got = called(repack_kernel, [VMEM], VMEM, shape((nz, half, qs + 512), f32), 8)(got)
+    got = called(repack_kernel, [VMEM], VMEM, shape((nz, half, qs + 1024), bf16), 8)(got)
     got, slope = lax.optimization_barrier((got, slope))
     got = exchanged(got, Z)
     slope_other, student_rows = lax.optimization_barrier((slope[rows:], student_rows))

time: 172 us -> 168 us (0.977)
  transfers between devices with their start and end apart: 7 -> 7, of which waited for: 3 -> 3; matrix products, arithmetic and copies ran while one was open for 4% -> 5% of each run, Pallas kernels for 0% -> 0%
where the time goes in v6:
time: 168 us; the launch traced here: 167 us
  blocking collectives  88.8 us (53%)
  starting transfers between devices  38.3 us (23%)
  waiting for transfers between devices  20.5 us (12%)
  Pallas kernels  11.2 us (7%)
  matrix products  4.96 us (3%)
  local copies, waits for them, and re-layouts  2.75 us (2%)
    all_to_all x4, blocking collectives, exchanged(): return lax.all_to_all(x, axes, 0, 0, tiled=True)  88.8 us
    ppermute x4, starting transfers between devices, swapped(): return lax.ppermute(x, C, [(0, 1), (1, 0)])  20.5 us
    all_to_all x3, waiting for transfers between devices, exchanged(): return lax.all_to_all(x, axes, 0, 0, tiled=True)  20.4 us
    all_to_all x3, starting transfers between devices, exchanged(): return lax.all_to_all(x, axes, 0, 0, tiled=True)  17.8 us
    dot_general x2, matrix products, dot(): lax.dot_general(a, b, (((along_a,), (along_b,)), ((), ())), preferred_ele...  4.96 us
    pallas_call x1, Pallas kernels, on_device(): called(logits_kernel, [VMEM] * 4 + [ANY], [ANY, ANY, VMEM, ANY], [shape((...  4.31 us
  transfers between devices with their start and end apart: 7, of which 3 were waited for; matrix products, arithmetic and copies ran while one was open for 5% of the time, Pallas kernels for 0%

profile of v6, /device:TPU:1, one launch (start us, length us, event | category | flops | bytes accessed | tf_op | source)
XLA Modules:
  0.0 167.4 jit_solution(4012594392547707589)
XLA Ops:
  0.6 1.9 %shard_map.111 = bf16[16,2,2944]{2,1,0:T(2,128)(2,1)} custom-call(s32[1]{0:T(128)} %bitcast.at_x, s32[1]{0:T(128)} %bitcast.1.at_c, bf16[4,8192]{1,0:T(4,128)(2,1)} %teacher_at.1, bf16[4,3584]{1,0:T(4,128)(2,1)} %hidden.1, bf16[64,128]{1,0:T(8,128)(2,1)} %bitcast.23, bf16[28,128]{1,0:T(8,128)(2,1)} %bitcast.21), custom_call_target="tpu_custom_call" | custom-call | tf_op jit(solution)/shard_map/pallas_call | solution.py:297
  2.6 8.8 %collective-permute-start = (bf16[160,8192]{1,0:T(8,128)(2,1)}, bf16[160,8192]{1,0:T(8,128)(2,1)}, u32[]{:S(2)}, u32[]{:S(2)}) collective-permute-start(bf16[160,8192]{1,0:T(8,128)(2,1)} %t_own), channel_id=1, source_target_pairs={{0,64},{64,0},{1,65},{65,1},{2,66},{66,2},{3,67},{67,3},{4,68},{68... | collective-permute-start | bytes 7864328 | tf_op jit(solution)/shard_map/ppermute | solution.py:39
  11.4 1.9 %collective-permute-start.1 = (bf16[160,3584]{1,0:T(8,128)(2,1)}, bf16[160,3584]{1,0:T(8,128)(2,1)S(1)}, u32[]{:S(2)}, u32[]{:S(2)}) collective-permute-start(bf16[160,3584]{1,0:T(8,128)(2,1)} %s_own.1), channel_id=1, source_target_pairs={{0,64},{64,0},{1,65},{65,1},{2,66},{66,2},{3,67},{67,3},{4,68},{68... | collective-permute-start | bytes 3440648 | tf_op jit(solution)/shard_map/ppermute | solution.py:39
  13.3 9.6 %all-to-all-start = ((bf16[16,2,2944]{2,1,0:T(2,128)(2,1)}), bf16[16,2,2944]{2,1,0:T(2,128)(2,1)S(1)}, u32[]{:S(2)}, u32[]{:S(2)}) async-start(bf16[16,2,2944]{2,1,0:T(2,128)(2,1)} %shard_map.111), calls=%async_computation | async-start | bytes 376832 | tf_op jit(solution)/shard_map/all_to_all | solution.py:35
  22.9 0.8 reshape.45
  23.8 0.1 copy.14
  23.9 0.1 copy.15
  24.0 0.1 reshape.46.label
  24.1 0.8 reshape.47
  25.0 0.1 copy.16
  25.1 0.1 copy.17
  25.2 0.1 reshape.48.cot
  25.4 0.1 pad_add_fusion.place
  25.5 9.9 %all-to-all-done = bf16[16,2,2944]{2,1,0:T(2,128)(2,1)S(1)} async-done(((bf16[16,2,2944]{2,1,0:T(2,128)(2,1)}), bf16[16,2,2944]{2,1,0:T(2,128)(2,1)S(1)}, u32[]{:S(2)}, u32[]{:S(2)}) %all-to-all-start) | async-done | bytes 188448 | tf_op jit(solution)/shard_map/all_to_all | solution.py:35
  35.4 0.1 reshape.44
  35.5 0.0 collective-permute-done.1.s_other
  35.5 0.0 collective-permute-done.t_other_at
  35.5 0.2 broadcast_in_dim.14
  35.7 0.0 copy-start
  35.7 0.0 copy-start.1
  35.7 39.2 %all_to_all.35 = bf16[16,32,2944]{2,1,0:T(8,128)(2,1)S(1)} all-to-all(bf16[16,32,2944]{2,1,0:T(8,128)(2,1)S(1)} %broadcast_in_dim.14), channel_id=1, replica_groups=mesh['section_0'=4,'section_1'=2,'dp_0'=16,'dp_1'=4] {'section_0','dp_1'}, dimensions={0} | all-to-all | bytes 6029312 | tf_op jit(solution)/shard_map/all_to_all | solution.py:35
  74.9 0.0 copy-done
  74.9 0.0 copy-done.1
  74.9 4.3 %shard_map.112 = (f32[320,128]{1,0:T(8,128)S(1)}, f32[320,128]{1,0:T(8,128)S(1)}, f32[16,2,128]{2,1,0:T(2,128)S(1)}, bf16[128,3584]{1,0:T(8,128)(2,1)S(1)}) custom-call(bf16[4,128,2944]{2,1,0:T(8,128)(2,1)S(1)} %bitcast.19, bf16[160,8192]{1,0:T(8,128)(2,1)S(1)} %copy-done.1, bf16[160,3584]{1,0:T(8,128)(2,1)S(1)} %copy-done, ...), custom_call_target="tpu_custom_call" | custom-call | tf_op jit(solution)/shard_map/pallas_call | solution.py:333
  79.3 10.5 %all_to_all.36.got = f32[16,2,128]{2,1,0:T(2,128)S(1)} all-to-all(f32[16,2,128]{2,1,0:T(2,128)S(1)} %get-tuple-element.44), channel_id=1, replica_groups=mesh['section_0'=4,'section_1'=2,'dp_0'=16,'dp_1'=4] {'section_0','dp_1'}, dimensions={0} | all-to-all | bytes 32768 | tf_op jit(solution)/shard_map/all_to_all | solution.py:35
  89.8 24.0 %all_to_all.37.got = f32[16,2,128]{2,1,0:T(2,128)S(1)} all-to-all(f32[16,2,128]{2,1,0:T(2,128)S(1)} %shard_map.113), channel_id=1, replica_groups=mesh['section_0'=4,'section_1'=2,'dp_0'=16,'dp_1'=4] {'dp_0'}, dimensions={0} | all-to-all | bytes 32768 | tf_op jit(solution)/shard_map/all_to_all | solution.py:35
  113.8 2.6 %shard_map.114 = (bf16[320,128]{1,0:T(8,128)(2,1)S(1)}, bf16[4,4,32,1024]{3,2,1,0:T(8,128)(2,1)S(1)}, f32[1,128]{1,0:T(1,128)S(1)}) custom-call(s32[2]{0:T(128)S(1)} %pad_add_fusion.place, f32[16,2,128]{2,1,0:T(2,128)S(1)} %all_to_all.37.got, s32[1,128]{1,0:T(1,128)S(1)} %reshape.46.label, f32[1,128]{1,0:T(1,128)S(1)} %reshape.48.cot, ...), custom_call_target="tpu_custom_call" | custom-call | tf_op jit(solution)/shard_map/pallas_call | solution.py:355
  116.3 15.1 %all_to_all.38.got = bf16[16,32,1024]{2,1,0:T(8,128)(2,1)S(1)} all-to-all(bf16[16,32,1024]{2,1,0:T(8,128)(2,1)S(1)} %bitcast.20), channel_id=1, replica_groups=mesh['section_0'=4,'section_1'=2,'dp_0'=16,'dp_1'=4] {'section_0','dp_1'}, dimensions={0} | all-to-all | bytes 2097152 | tf_op jit(solution)/shard_map/all_to_all | solution.py:35
  131.4 0.8 shard_map.115
  132.3 7.9 %collective-permute-start.3 = (bf16[128,3584]{1,0:T(8,128)(2,1)S(1)}, bf16[128,3584]{1,0:T(8,128)(2,1)S(1)}, u32[]{:S(2)}, u32[]{:S(2)}) collective-permute-start(bf16[128,3584]{1,0:T(8,128)(2,1)S(1)} %get-tuple-element.55.student_rows), channel_id=1, source_target_pairs={{0,64},{64,0},{1,65},{65,1},{2,66},{66,2},{3,67},{67,3},{4,68},{68... | collective-permute-start | bytes 2752520 | tf_op jit(solution)/shard_map/ppermute | solution.py:39
  140.2 3.5 %all-to-all-start.5 = ((bf16[16,2,1920]{2,1,0:T(2,128)(2,1)}), bf16[16,2,1920]{2,1,0:T(2,128)(2,1)S(1)}, u32[]{:S(2)}, u32[]{:S(2)}) async-start(bf16[16,2,1920]{2,1,0:T(2,128)(2,1)} %shard_map.115), calls=%async_computation.5 | async-start | bytes 245760 | tf_op jit(solution)/shard_map/all_to_all | solution.py:35
  143.7 1.9 %collective-permute-start.2 = (bf16[160,128]{1,0:T(8,128)(2,1)S(1)}, bf16[160,128]{1,0:T(8,128)(2,1)S(1)}, u32[]{:S(2)}, u32[]{:S(2)}) collective-permute-start(bf16[160,128]{1,0:T(8,128)(2,1)S(1)} %slice.7), channel_id=1, source_target_pairs={{0,64},{64,0},{1,65},{65,1},{2,66},{66,2},{3,67},{67,3},{4,68},{68... | collective-permute-start | bytes 122888 | tf_op jit(solution)/shard_map/ppermute | solution.py:39
  145.6 1.9 %fusion.1 = f32[160,3584]{1,0:T(8,128)} fusion(bf16[128,3584]{1,0:T(8,128)(2,1)S(1)} %get-tuple-element.55.student_rows, bf16[320,128]{1,0:T(8,128)(2,1)S(1)} %get-tuple-element.54), kind=kOutput, calls=%fused_computation.2 | convolution fusion | flops 146800640 | bytes 3252224 | tf_op jit(solution)/shard_map/dot_general | solution.py:43
  147.5 8.7 %all-to-all-done.5.got = bf16[16,2,1920]{2,1,0:T(2,128)(2,1)S(1)} async-done(((bf16[16,2,1920]{2,1,0:T(2,128)(2,1)}), bf16[16,2,1920]{2,1,0:T(2,128)(2,1)S(1)}, u32[]{:S(2)}, u32[]{:S(2)}) %all-to-all-start.5) | async-done | bytes 122912 | tf_op jit(solution)/shard_map/all_to_all | solution.py:35
  156.2 0.7 shard_map.116
  156.8 0.0 copy-start.2
  156.8 0.0 copy-start.3
  156.8 4.7 %all-to-all-start.6 = ((f32[8,2,1408]{2,1,0:T(2,128)}), f32[8,2,1408]{2,1,0:T(2,128)S(1)}, u32[]{:S(2)}, u32[]{:S(2)}) async-start(f32[8,2,1408]{2,1,0:T(2,128)} %shard_map.116), calls=%async_computation.6 | async-start | bytes 180224 | tf_op jit(solution)/shard_map/all_to_all | solution.py:35
  161.5 0.0 collective-permute-done.2
  161.6 0.0 collective-permute-done.3
  161.6 3.1 %fusion = bf16[160,3584]{1,0:T(8,128)(2,1)} fusion(f32[160,3584]{1,0:T(8,128)} %fusion.1, bf16[160,128]{1,0:T(8,128)(2,1)S(1)} %collective-permute-done.2, bf16[128,3584]{1,0:T(8,128)(2,1)S(1)} %collective-permute-done.3), kind=kOutput, calls=%fused_computation.1 | convolution fusion | flops 147947520 | bytes 4399104 | tf_op jit(solution)/shard_map/dot_general | solution.py:43
  164.7 1.8 %all-to-all-done.6.got = f32[8,2,1408]{2,1,0:T(2,128)S(1)} async-done(((f32[8,2,1408]{2,1,0:T(2,128)}), f32[8,2,1408]{2,1,0:T(2,128)S(1)}, u32[]{:S(2)}, u32[]{:S(2)}) %all-to-all-start.6) | async-done | bytes 90144 | tf_op jit(solution)/shard_map/all_to_all | solution.py:35
  166.5 0.0 copy-done.2
  166.5 0.0 copy-done.3
  166.5 0.9 shard_map.117
  (4 shorter events, 0.1 us)
Async XLA Ops:
  2.6 32.9 %collective-permute-start = (bf16[160,8192]{1,0:T(8,128)(2,1)}, bf16[160,8192]{1,0:T(8,128)(2,1)}, u32[]{:S(2)}, u32[]{:S(2)}) collective-permute-start(bf16[160,8192]{1,0:T(8,128)(2,1)} %t_own), channel_id=1, source_target_pairs={{0,64},{64,0},{1,65},{65,1},{2,66},{66,2},{3,67},{67,3},{4,68},{68... | collective-permute-start | bytes 7864328 | tf_op jit(solution)/shard_map/ppermute | solution.py:39
  11.4 24.1 %collective-permute-start.1 = (bf16[160,3584]{1,0:T(8,128)(2,1)}, bf16[160,3584]{1,0:T(8,128)(2,1)S(1)}, u32[]{:S(2)}, u32[]{:S(2)}) collective-permute-start(bf16[160,3584]{1,0:T(8,128)(2,1)} %s_own.1), channel_id=1, source_target_pairs={{0,64},{64,0},{1,65},{65,1},{2,66},{66,2},{3,67},{67,3},{4,68},{68... | collective-permute-start | bytes 3440648 | tf_op jit(solution)/shard_map/ppermute | solution.py:39
  13.3 22.1 %all-to-all-start = ((bf16[16,2,2944]{2,1,0:T(2,128)(2,1)}), bf16[16,2,2944]{2,1,0:T(2,128)(2,1)S(1)}, u32[]{:S(2)}, u32[]{:S(2)}) async-start(bf16[16,2,2944]{2,1,0:T(2,128)(2,1)} %shard_map.111), calls=%async_computation | async-start | bytes 376832 | tf_op jit(solution)/shard_map/all_to_all | solution.py:35
  35.7 39.2 %copy-start = (bf16[160,3584]{1,0:T(8,128)(2,1)S(1)}, bf16[160,3584]{1,0:T(8,128)(2,1)}, u32[]{:S(2)}) copy-start(bf16[160,3584]{1,0:T(8,128)(2,1)} %s_own.1) | copy-start | bytes 3440644
  35.7 39.2 %copy-start.1 = (bf16[160,8192]{1,0:T(8,128)(2,1)S(1)}, bf16[160,8192]{1,0:T(8,128)(2,1)}, u32[]{:S(2)}) copy-start(bf16[160,8192]{1,0:T(8,128)(2,1)} %t_own) | copy-start | bytes 7864324
  132.3 29.3 %collective-permute-start.3 = (bf16[128,3584]{1,0:T(8,128)(2,1)S(1)}, bf16[128,3584]{1,0:T(8,128)(2,1)S(1)}, u32[]{:S(2)}, u32[]{:S(2)}) collective-permute-start(bf16[128,3584]{1,0:T(8,128)(2,1)S(1)} %get-tuple-element.55.student_rows), channel_id=1, source_target_pairs={{0,64},{64,0},{1,65},{65,1},{2,66},{66,2},{3,67},{67,3},{4,68},{68... | collective-permute-start | bytes 2752520 | tf_op jit(solution)/shard_map/ppermute | solution.py:39
  140.2 16.0 %all-to-all-start.5 = ((bf16[16,2,1920]{2,1,0:T(2,128)(2,1)}), bf16[16,2,1920]{2,1,0:T(2,128)(2,1)S(1)}, u32[]{:S(2)}, u32[]{:S(2)}) async-start(bf16[16,2,1920]{2,1,0:T(2,128)(2,1)} %shard_map.115), calls=%async_computation.5 | async-start | bytes 245760 | tf_op jit(solution)/shard_map/all_to_all | solution.py:35
  143.7 17.8 %collective-permute-start.2 = (bf16[160,128]{1,0:T(8,128)(2,1)S(1)}, bf16[160,128]{1,0:T(8,128)(2,1)S(1)}, u32[]{:S(2)}, u32[]{:S(2)}) collective-permute-start(bf16[160,128]{1,0:T(8,128)(2,1)S(1)} %slice.7), channel_id=1, source_target_pairs={{0,64},{64,0},{1,65},{65,1},{2,66},{66,2},{3,67},{67,3},{4,68},{68... | collective-permute-start | bytes 122888 | tf_op jit(solution)/shard_map/ppermute | solution.py:39
  156.8 9.7 %copy-start.2 = (bf16[4,3584]{1,0:T(4,128)(2,1)S(1)}, bf16[4,3584]{1,0:T(4,128)(2,1)}, u32[]{:S(2)}) copy-start(bf16[4,3584]{1,0:T(4,128)(2,1)} %hidden.1) | copy-start | bytes 86020
  156.8 9.7 %copy-start.3 = (bf16[3584]{0:T(1024)(128)(2,1)S(1)}, bf16[3584]{0:T(1024)(128)(2,1)}, u32[]{:S(2)}) copy-start(bf16[3584]{0:T(1024)(128)(2,1)} %param.11) | copy-start | bytes 21508
  156.8 9.7 %all-to-all-start.6 = ((f32[8,2,1408]{2,1,0:T(2,128)}), f32[8,2,1408]{2,1,0:T(2,128)S(1)}, u32[]{:S(2)}, u32[]{:S(2)}) async-start(f32[8,2,1408]{2,1,0:T(2,128)} %shard_map.116), calls=%async_computation.6 | async-start | bytes 180224 | tf_op jit(solution)/shard_map/all_to_all | solution.py:35

commit v7 on v6

--- a/solution.py
+++ b/solution.py
@@ -101,42 +101,46 @@
 
 
 def logits_kernel(
-    plane, t_own, s_own, s_other, t_other_at, t_logits, s_logits, logs, student_rows,
-    t_other, t_out, s_out, sems,
+    plane, t_own, s_own, s_other, t_other_at,
+    t_logits, s_logits, logs, student_rows, early_rows, late_rows, t_other, sems,
 ):
-    nx = plane.shape[0]
+    nx, tokens, _ = plane.shape
     rows, dt = t_own.shape
     qt = dt // nx
     qs = s_own.shape[1] // nx
-    late = pltpu.make_async_copy(t_other_at, t_other, sems.at[nx + 2])
+    late = pltpu.make_async_copy(t_other_at, t_other, sems.at[0])
     late.start()
-    back = [
-        pltpu.make_async_copy(
-            plane.at[k, :, qt:], student_rows.at[:, k * qs : (k + 1) * qs], sems.at[k]
-        )
-        for k in range(nx)
-    ]
-    back.append(pltpu.make_async_copy(t_out, t_logits, sems.at[nx]))
-    back.append(pltpu.make_async_copy(s_out, s_logits, sems.at[nx + 1]))
-    for copy in back[:nx]:
-        copy.start()
+    back = []
+    for k in range(nx):
+        at = slice(k * qs, (k + 1) * qs)
+        for n, (target, first, last) in enumerate(
+            (
+                (student_rows, 0, tokens),
+                (early_rows, 0, tokens // 2),
+                (late_rows, tokens // 2, tokens),
+            )
+        ):
+            back.append(
+                pltpu.make_async_copy(
+                    plane.at[k, first:last, qt:], target.at[:, at], sems.at[1 + 3 * k + n]
+                )
+            )
+            back[-1].start()
     for out, n, head, at, width in (
-        (s_out, 0, s_own, qt, qs),
-        (s_out, 1, s_other, qt, qs),
-        (t_out, 0, t_own, 0, qt),
-        (t_out, 1, t_other, 0, qt),
+        (s_logits, 0, s_own, qt, qs),
+        (s_logits, 1, s_other, qt, qs),
+        (t_logits, 0, t_own, 0, qt),
+        (t_logits, 1, t_other, 0, qt),
     ):
         if head is t_other:
-            back[nx + 1].start()
             late.wait()
         total = 0.0
         for k in range(nx):
             part = plane[k, :, at : at + width]
             total += dot(head[:, k * width : (k + 1) * width], part, 1, 1)
         out[n * rows : (n + 1) * rows] = total
-    back[nx].start()
-    t_log = column_log(t_out[...])
-    s_log = column_log(s_out[...])
+    t_log = column_log(t_logits[...])
+    s_log = column_log(s_logits[...])
     for k in range(logs.shape[0]):
         logs[k, 0:1] = t_log
         logs[k, 1:2] = s_log
@@ -153,17 +157,11 @@
 
 
 def terms_kernel(
-    place, got, label, cot, t_logits, s_logits, student_rows, s_own, s_other,
-    slope, sent, common, t_in, s_in, s_rows, s_heads, sems,
+    place, got, label, cot, t_logits, s_logits, s_rows_at, s_own, s_other,
+    slope, sent, common, s_rows, s_heads, sems,
 ):
     rows = s_own.shape[0]
-    pairs = (
-        (t_logits, t_in),
-        (s_logits, s_in),
-        (s_own, s_heads.at[0]),
-        (s_other, s_heads.at[1]),
-        (student_rows, s_rows),
-    )
+    pairs = ((s_own, s_heads.at[0]), (s_other, s_heads.at[1]), (s_rows_at, s_rows))
     copies = [pltpu.make_async_copy(a, b, sems.at[k]) for k, (a, b) in enumerate(pairs)]
     for copy in copies:
         copy.start()
@@ -173,11 +171,9 @@
     student_log = column_log(got[:, 1, :])
     common[...] = (1.0 + ce_weight) * student_log - teacher_log
     loss_terms = 0.0
-    copies[0].wait()
-    copies[1].wait()
     for k in range(2):
         at = slice(k * rows, (k + 1) * rows)
-        s_part, t_part = (s_in[at], t_in[at])
+        s_part, t_part = (s_logits[at], t_logits[at])
         entry = lax.broadcasted_iota(jnp.int32, s_part.shape, 0) + place[k]
         hits = entry == label[...]
         s_prob = jnp.exp(s_part - student_log)
@@ -187,7 +183,7 @@
         slope[at] = value.astype(bf16)
         lost = t_prob * (t_part - s_part) - ce_weight * jnp.where(hits, s_part, 0.0)
         loss_terms += jnp.sum(lost, axis=0, keepdims=True)
-    for copy in copies[2:]:
+    for copy in copies:
         copy.wait()
     line = lax.broadcasted_iota(jnp.int32, (16, 128), 0)
     loss_high = loss_terms.astype(bf16).astype(f32)
@@ -330,22 +326,22 @@
     )
     plane = to_all(line, PLANE).reshape(nx, tokens, qt + qs)
 
-    t_logits, s_logits, logs, student_rows = called(
+    t_logits, s_logits, logs, student_rows, early_rows, late_rows = called(
         logits_kernel,
         [VMEM] * 4 + [ANY],
-        [ANY, ANY, VMEM, ANY],
+        [VMEM] * 3 + [ANY] * 3,
         [
             shape((2 * rows, tokens), f32),
             shape((2 * rows, tokens), f32),
             shape((nx * ny, 2, tokens), f32),
             shape((tokens, ds), bf16),
+            shape((tokens // 2, ds), bf16),
+            shape((tokens // 2, ds), bf16),
         ],
         LOGITS,
         [
             pltpu.VMEM((rows, dt), bf16),
-            pltpu.VMEM((2 * rows, tokens), f32),
-            pltpu.VMEM((2 * rows, tokens), f32),
-            pltpu.SemaphoreType.DMA((nx + 3,)),
+            pltpu.SemaphoreType.DMA((1 + 3 * nx,)),
         ],
     )(plane, teacher_head, student_head, student_other, teacher_other)
     logs = exchanged(logs, PLANE)
@@ -354,7 +350,7 @@
 
     slope, sent, common = called(
         terms_kernel,
-        [SMEM] + [VMEM] * 3 + [ANY] * 5,
+        [SMEM] + [VMEM] * 5 + [ANY] * 3,
         [VMEM] * 3,
         [
             shape((2 * rows, tokens), bf16),
@@ -363,22 +359,23 @@
         ],
         BIG,
         [
-            pltpu.VMEM((2 * rows, tokens), f32),
-            pltpu.VMEM((2 * rows, tokens), f32),
             pltpu.VMEM((tokens, ds), bf16),
             pltpu.VMEM((nc, rows, ds), bf16),
-            pltpu.SemaphoreType.DMA((5,)),
+            pltpu.SemaphoreType.DMA((3,)),
         ],
     )(place, logs, label, cot, t_logits, s_logits, student_rows, student_head, student_other)
     got = exchanged(sent.reshape(nx * ny, held, qs + 128), PLANE)
     got = called(repack_kernel, [VMEM], VMEM, shape((nz, half, qs + 1024), bf16), 8)(got)
     got, slope = lax.optimization_barrier((got, slope))
     got = exchanged(got, Z)
-    slope_other, student_rows = lax.optimization_barrier((slope[rows:], student_rows))
+    slope_other, early_rows, late_rows = lax.optimization_barrier(
+        (slope[rows:], early_rows, late_rows)
+    )
+    rows_other = jnp.concatenate([swapped(early_rows), swapped(late_rows)])
 
     head_grad = (
         dot(slope[:rows], student_rows, 1, 0)
-        + dot(swapped(slope_other), swapped(student_rows), 1, 0)
+        + dot(swapped(slope_other), rows_other, 1, 0)
     ).astype(bf16)
 
     got = called(share_kernel, [VMEM] * 2, VMEM, shape((nx * nc, half, qs + 512), f32), 4)(

time: 168 us -> 165 us (0.982)
  waiting for transfers between devices: 20.5 us -> 11.8 us
  starting transfers between devices: 38.3 us -> 44.3 us
    all_to_all x3, waiting for transfers between devices: 20.4 us -> 11.8 us  [exchanged(): return lax.all_to_all(x, axes, 0, 0, tiled=True)]
    all_to_all x3, starting transfers between devices: 17.8 us -> 21.3 us  [exchanged(): return lax.all_to_all(x, axes, 0, 0, tiled=True)]
    ppermute x4 -> x5, starting transfers between devices: 20.5 us -> 23 us  [swapped(): return lax.ppermute(x, C, [(0, 1), (1, 0)])]
  transfers between devices with their start and end apart: 7 -> 8, of which waited for: 3 -> 2; matrix products, arithmetic and copies ran while one was open for 5% -> 5% of each run, Pallas kernels for 0% -> 0%
where the time goes in v7:
time: 165 us; the launch traced here: 164 us
  blocking collectives  88.8 us (54%)
  starting transfers between devices  44.3 us (27%)
  waiting for transfers between devices  11.8 us (7%)
  Pallas kernels  10.5 us (6%)
  matrix products  4.95 us (3%)
  local copies, waits for them, and re-layouts  2.75 us (2%)
    all_to_all x4, blocking collectives, exchanged(): return lax.all_to_all(x, axes, 0, 0, tiled=True)  88.8 us
    ppermute x5, starting transfers between devices, swapped(): return lax.ppermute(x, C, [(0, 1), (1, 0)])  23 us
    all_to_all x3, starting transfers between devices, exchanged(): return lax.all_to_all(x, axes, 0, 0, tiled=True)  21.3 us
    all_to_all x3, waiting for transfers between devices, exchanged(): return lax.all_to_all(x, axes, 0, 0, tiled=True)  11.8 us
    dot_general x2, matrix products, dot(): lax.dot_general(a, b, (((along_a,), (along_b,)), ((), ())), preferred_ele...  4.95 us
    pallas_call x1, Pallas kernels, on_device(): called(logits_kernel, [VMEM] * 4 + [ANY], [VMEM] * 3 + [ANY] * 3, [shape(...  4.1 us
  transfers between devices with their start and end apart: 8, of which 2 were waited for; matrix products, arithmetic and copies ran while one was open for 5% of the time, Pallas kernels for 0%

profile of v7, /device:TPU:1, one launch (start us, length us, event | category | flops | bytes accessed | tf_op | source)
XLA Modules:
  0.0 164.0 jit_solution(7884762303480536623)
XLA Ops:
  0.6 1.9 %shard_map.111 = bf16[16,2,2944]{2,1,0:T(2,128)(2,1)} custom-call(s32[1]{0:T(128)} %bitcast.at_x, s32[1]{0:T(128)} %bitcast.1.at_c, bf16[4,8192]{1,0:T(4,128)(2,1)} %teacher_at.1, bf16[4,3584]{1,0:T(4,128)(2,1)} %hidden.1, bf16[64,128]{1,0:T(8,128)(2,1)} %bitcast.22, bf16[28,128]{1,0:T(8,128)(2,1)} %bitcast.20), custom_call_target="tpu_custom_call" | custom-call | tf_op jit(solution)/shard_map/pallas_call | solution.py:293
  2.6 8.8 %collective-permute-start = (bf16[160,8192]{1,0:T(8,128)(2,1)}, bf16[160,8192]{1,0:T(8,128)(2,1)}, u32[]{:S(2)}, u32[]{:S(2)}) collective-permute-start(bf16[160,8192]{1,0:T(8,128)(2,1)} %t_own), channel_id=1, source_target_pairs={{0,64},{64,0},{1,65},{65,1},{2,66},{66,2},{3,67},{67,3},{4,68},{68... | collective-permute-start | bytes 7864328 | tf_op jit(solution)/shard_map/ppermute | solution.py:39
  11.4 1.9 %collective-permute-start.1 = (bf16[160,3584]{1,0:T(8,128)(2,1)}, bf16[160,3584]{1,0:T(8,128)(2,1)S(1)}, u32[]{:S(2)}, u32[]{:S(2)}) collective-permute-start(bf16[160,3584]{1,0:T(8,128)(2,1)} %s_own.1), channel_id=1, source_target_pairs={{0,64},{64,0},{1,65},{65,1},{2,66},{66,2},{3,67},{67,3},{4,68},{68... | collective-permute-start | bytes 3440648 | tf_op jit(solution)/shard_map/ppermute | solution.py:39
  13.3 9.6 %all-to-all-start = ((bf16[16,2,2944]{2,1,0:T(2,128)(2,1)}), bf16[16,2,2944]{2,1,0:T(2,128)(2,1)S(1)}, u32[]{:S(2)}, u32[]{:S(2)}) async-start(bf16[16,2,2944]{2,1,0:T(2,128)(2,1)} %shard_map.111), calls=%async_computation | async-start | bytes 376832 | tf_op jit(solution)/shard_map/all_to_all | solution.py:35
  22.9 0.8 reshape.45
  23.8 0.1 copy.14
  23.9 0.1 copy.15
  24.0 0.1 reshape.46.label
  24.1 0.8 reshape.47
  25.0 0.1 copy.16
  25.1 0.1 copy.17
  25.2 0.1 reshape.48.cot
  25.4 0.1 pad_add_fusion.place
  25.5 9.9 %all-to-all-done = bf16[16,2,2944]{2,1,0:T(2,128)(2,1)S(1)} async-done(((bf16[16,2,2944]{2,1,0:T(2,128)(2,1)}), bf16[16,2,2944]{2,1,0:T(2,128)(2,1)S(1)}, u32[]{:S(2)}, u32[]{:S(2)}) %all-to-all-start) | async-done | bytes 188448 | tf_op jit(solution)/shard_map/all_to_all | solution.py:35
  35.4 0.1 reshape.44
  35.5 0.0 collective-permute-done.1.s_other
  35.5 0.0 collective-permute-done.t_other_at
  35.5 0.2 broadcast_in_dim.14
  35.7 0.0 copy-start
  35.7 0.0 copy-start.1
  35.7 39.2 %all_to_all.35 = bf16[16,32,2944]{2,1,0:T(8,128)(2,1)S(1)} all-to-all(bf16[16,32,2944]{2,1,0:T(8,128)(2,1)S(1)} %broadcast_in_dim.14), channel_id=1, replica_groups=mesh['section_0'=4,'section_1'=2,'dp_0'=16,'dp_1'=4] {'section_0','dp_1'}, dimensions={0} | all-to-all | bytes 6029312 | tf_op jit(solution)/shard_map/all_to_all | solution.py:35
  74.9 0.0 copy-done
  74.9 0.0 copy-done.1
  74.9 4.1 %shard_map.112 = (f32[320,128]{1,0:T(8,128)S(1)}, f32[320,128]{1,0:T(8,128)S(1)}, f32[16,2,128]{2,1,0:T(2,128)S(1)}, bf16[128,3584]{1,0:T(8,128)(2,1)S(1)}, bf16...) custom-call(bf16[4,128,2944]{2,1,0:T(8,128)(2,1)S(1)} %bitcast.18, bf16[160,8192]{1,0:T(8,128)(2,1)S(1)} %copy-done.1, ...), custom_call_target="tpu_custom_call" | custom-call | tf_op jit(solution)/shard_map/pallas_call | solution.py:329
  79.0 10.5 %all_to_all.36.got = f32[16,2,128]{2,1,0:T(2,128)S(1)} all-to-all(f32[16,2,128]{2,1,0:T(2,128)S(1)} %get-tuple-element.47), channel_id=1, replica_groups=mesh['section_0'=4,'section_1'=2,'dp_0'=16,'dp_1'=4] {'section_0','dp_1'}, dimensions={0} | all-to-all | bytes 32768 | tf_op jit(solution)/shard_map/all_to_all | solution.py:35
  89.6 24.0 %all_to_all.37.got = f32[16,2,128]{2,1,0:T(2,128)S(1)} all-to-all(f32[16,2,128]{2,1,0:T(2,128)S(1)} %shard_map.113), channel_id=1, replica_groups=mesh['section_0'=4,'section_1'=2,'dp_0'=16,'dp_1'=4] {'dp_0'}, dimensions={0} | all-to-all | bytes 32768 | tf_op jit(solution)/shard_map/all_to_all | solution.py:35
  113.6 2.1 %shard_map.114 = (bf16[320,128]{1,0:T(8,128)(2,1)S(1)}, bf16[4,4,32,1024]{3,2,1,0:T(8,128)(2,1)S(1)}, f32[1,128]{1,0:T(1,128)S(1)}) custom-call(s32[2]{0:T(128)S(1)} %pad_add_fusion.place, f32[16,2,128]{2,1,0:T(2,128)S(1)} %all_to_all.37.got, s32[1,128]{1,0:T(1,128)S(1)} %reshape.46.label, f32[1,128]{1,0:T(1,128)S(1)} %reshape.48.cot, ...), custom_call_target="tpu_custom_call" | custom-call | tf_op jit(solution)/shard_map/pallas_call | solution.py:351
  115.7 15.1 %all_to_all.38.got = bf16[16,32,1024]{2,1,0:T(8,128)(2,1)S(1)} all-to-all(bf16[16,32,1024]{2,1,0:T(8,128)(2,1)S(1)} %bitcast.19), channel_id=1, replica_groups=mesh['section_0'=4,'section_1'=2,'dp_0'=16,'dp_1'=4] {'section_0','dp_1'}, dimensions={0} | all-to-all | bytes 2097152 | tf_op jit(solution)/shard_map/all_to_all | solution.py:35
  130.8 0.8 shard_map.115
  131.6 3.5 %all-to-all-start.5 = ((bf16[16,2,1920]{2,1,0:T(2,128)(2,1)}), bf16[16,2,1920]{2,1,0:T(2,128)(2,1)S(1)}, u32[]{:S(2)}, u32[]{:S(2)}) async-start(bf16[16,2,1920]{2,1,0:T(2,128)(2,1)} %shard_map.115), calls=%async_computation.5 | async-start | bytes 245760 | tf_op jit(solution)/shard_map/all_to_all | solution.py:35
  135.1 7.9 %collective-permute-start.3 = (bf16[64,3584]{1,0:T(8,128)(2,1)S(1)}, bf16[64,3584]{1,0:T(8,128)(2,1)S(1)}, u32[]{:S(2)}, u32[]{:S(2)}) collective-permute-start(bf16[64,3584]{1,0:T(8,128)(2,1)S(1)} %get-tuple-element.61), channel_id=1, source_target_pairs={{0,64},{64,0},{1,65},{65,1},{2,66},{66,2},{3,67},{67,3},{4,68},{68... | collective-permute-start | bytes 1376264 | tf_op jit(solution)/shard_map/ppermute | solution.py:39
  143.0 1.9 %collective-permute-start.4 = (bf16[64,3584]{1,0:T(8,128)(2,1)S(1)}, bf16[64,3584]{1,0:T(8,128)(2,1)S(1)}, u32[]{:S(2)}, u32[]{:S(2)}) collective-permute-start(bf16[64,3584]{1,0:T(8,128)(2,1)S(1)} %get-tuple-element.62), channel_id=1, source_target_pairs={{0,64},{64,0},{1,65},{65,1},{2,66},{66,2},{3,67},{67,3},{4,68},{68... | collective-permute-start | bytes 1376264 | tf_op jit(solution)/shard_map/ppermute | solution.py:39
  145.0 2.4 %collective-permute-start.2 = (bf16[160,128]{1,0:T(8,128)(2,1)S(1)}, bf16[160,128]{1,0:T(8,128)(2,1)S(1)}, u32[]{:S(2)}, u32[]{:S(2)}) collective-permute-start(bf16[160,128]{1,0:T(8,128)(2,1)S(1)} %slice.7), channel_id=1, source_target_pairs={{0,64},{64,0},{1,65},{65,1},{2,66},{66,2},{3,67},{67,3},{4,68},{68... | collective-permute-start | bytes 122888 | tf_op jit(solution)/shard_map/ppermute | solution.py:39
  147.4 1.8 %fusion.4 = f32[160,3584]{1,0:T(8,128)} fusion(bf16[128,3584]{1,0:T(8,128)(2,1)S(1)} %get-tuple-element.52.s_rows_at, bf16[320,128]{1,0:T(8,128)(2,1)S(1)} %get-tuple-element.57), kind=kOutput, calls=%fused_computation.5 | convolution fusion | flops 146800640 | bytes 3252224 | tf_op jit(solution)/shard_map/dot_general | solution.py:43
  149.2 0.0 all-to-all-done.5.got
  149.2 0.7 shard_map.116
  149.9 0.0 copy-start.2
  149.9 0.0 copy-start.3
  149.9 8.3 %all-to-all-start.6 = ((f32[8,2,1408]{2,1,0:T(2,128)}), f32[8,2,1408]{2,1,0:T(2,128)S(1)}, u32[]{:S(2)}, u32[]{:S(2)}) async-start(f32[8,2,1408]{2,1,0:T(2,128)} %shard_map.116), calls=%async_computation.6 | async-start | bytes 180224 | tf_op jit(solution)/shard_map/all_to_all | solution.py:35
  158.2 0.0 collective-permute-done.2
  158.2 0.0 collective-permute-done.3
  158.2 0.0 collective-permute-done.4
  158.2 3.1 %fusion = bf16[160,3584]{1,0:T(8,128)(2,1)} fusion(f32[160,3584]{1,0:T(8,128)} %fusion.4, bf16[160,128]{1,0:T(8,128)(2,1)S(1)} %collective-permute-done.2, bf16[64,3584]{1,0:T(8,128)(2,1)S(1)} %collective-permute-done.4, bf16[64,3584]{1,0:T(8,128)(2,1)S(1)} %collective-permute-done.3), kind=kOutput, calls=%fused_computation.1 | convolution fusion | flops 149782528 | bytes 4399104 | tf_op jit(solution)/shard_map/dot_general | solution.py:43
  161.3 1.8 %all-to-all-done.6.got = f32[8,2,1408]{2,1,0:T(2,128)S(1)} async-done(((f32[8,2,1408]{2,1,0:T(2,128)}), f32[8,2,1408]{2,1,0:T(2,128)S(1)}, u32[]{:S(2)}, u32[]{:S(2)}) %all-to-all-start.6) | async-done | bytes 90144 | tf_op jit(solution)/shard_map/all_to_all | solution.py:35
  163.1 0.0 copy-done.2
  163.1 0.0 copy-done.3
  163.1 0.9 shard_map.117
  (4 shorter events, 0.1 us)
Async XLA Ops:
  2.6 32.9 %collective-permute-start = (bf16[160,8192]{1,0:T(8,128)(2,1)}, bf16[160,8192]{1,0:T(8,128)(2,1)}, u32[]{:S(2)}, u32[]{:S(2)}) collective-permute-start(bf16[160,8192]{1,0:T(8,128)(2,1)} %t_own), channel_id=1, source_target_pairs={{0,64},{64,0},{1,65},{65,1},{2,66},{66,2},{3,67},{67,3},{4,68},{68... | collective-permute-start | bytes 7864328 | tf_op jit(solution)/shard_map/ppermute | solution.py:39
  11.4 24.1 %collective-permute-start.1 = (bf16[160,3584]{1,0:T(8,128)(2,1)}, bf16[160,3584]{1,0:T(8,128)(2,1)S(1)}, u32[]{:S(2)}, u32[]{:S(2)}) collective-permute-start(bf16[160,3584]{1,0:T(8,128)(2,1)} %s_own.1), channel_id=1, source_target_pairs={{0,64},{64,0},{1,65},{65,1},{2,66},{66,2},{3,67},{67,3},{4,68},{68... | collective-permute-start | bytes 3440648 | tf_op jit(solution)/shard_map/ppermute | solution.py:39
  13.3 22.1 %all-to-all-start = ((bf16[16,2,2944]{2,1,0:T(2,128)(2,1)}), bf16[16,2,2944]{2,1,0:T(2,128)(2,1)S(1)}, u32[]{:S(2)}, u32[]{:S(2)}) async-start(bf16[16,2,2944]{2,1,0:T(2,128)(2,1)} %shard_map.111), calls=%async_computation | async-start | bytes 376832 | tf_op jit(solution)/shard_map/all_to_all | solution.py:35
  35.7 39.2 %copy-start = (bf16[160,3584]{1,0:T(8,128)(2,1)S(1)}, bf16[160,3584]{1,0:T(8,128)(2,1)}, u32[]{:S(2)}) copy-start(bf16[160,3584]{1,0:T(8,128)(2,1)} %s_own.1) | copy-start | bytes 3440644
  35.7 39.2 %copy-start.1 = (bf16[160,8192]{1,0:T(8,128)(2,1)S(1)}, bf16[160,8192]{1,0:T(8,128)(2,1)}, u32[]{:S(2)}) copy-start(bf16[160,8192]{1,0:T(8,128)(2,1)} %t_own) | copy-start | bytes 7864324
  131.6 17.6 %all-to-all-start.5 = ((bf16[16,2,1920]{2,1,0:T(2,128)(2,1)}), bf16[16,2,1920]{2,1,0:T(2,128)(2,1)S(1)}, u32[]{:S(2)}, u32[]{:S(2)}) async-start(bf16[16,2,1920]{2,1,0:T(2,128)(2,1)} %shard_map.115), calls=%async_computation.5 | async-start | bytes 245760 | tf_op jit(solution)/shard_map/all_to_all | solution.py:35
  135.1 23.1 %collective-permute-start.3 = (bf16[64,3584]{1,0:T(8,128)(2,1)S(1)}, bf16[64,3584]{1,0:T(8,128)(2,1)S(1)}, u32[]{:S(2)}, u32[]{:S(2)}) collective-permute-start(bf16[64,3584]{1,0:T(8,128)(2,1)S(1)} %get-tuple-element.61), channel_id=1, source_target_pairs={{0,64},{64,0},{1,65},{65,1},{2,66},{66,2},{3,67},{67,3},{4,68},{68... | collective-permute-start | bytes 1376264 | tf_op jit(solution)/shard_map/ppermute | solution.py:39
  143.0 15.1 %collective-permute-start.4 = (bf16[64,3584]{1,0:T(8,128)(2,1)S(1)}, bf16[64,3584]{1,0:T(8,128)(2,1)S(1)}, u32[]{:S(2)}, u32[]{:S(2)}) collective-permute-start(bf16[64,3584]{1,0:T(8,128)(2,1)S(1)} %get-tuple-element.62), channel_id=1, source_target_pairs={{0,64},{64,0},{1,65},{65,1},{2,66},{66,2},{3,67},{67,3},{4,68},{68... | collective-permute-start | bytes 1376264 | tf_op jit(solution)/shard_map/ppermute | solution.py:39
  145.0 13.2 %collective-permute-start.2 = (bf16[160,128]{1,0:T(8,128)(2,1)S(1)}, bf16[160,128]{1,0:T(8,128)(2,1)S(1)}, u32[]{:S(2)}, u32[]{:S(2)}) collective-permute-start(bf16[160,128]{1,0:T(8,128)(2,1)S(1)} %slice.7), channel_id=1, source_target_pairs={{0,64},{64,0},{1,65},{65,1},{2,66},{66,2},{3,67},{67,3},{4,68},{68... | collective-permute-start | bytes 122888 | tf_op jit(solution)/shard_map/ppermute | solution.py:39
  149.9 13.2 %copy-start.2 = (bf16[4,3584]{1,0:T(4,128)(2,1)S(1)}, bf16[4,3584]{1,0:T(4,128)(2,1)}, u32[]{:S(2)}) copy-start(bf16[4,3584]{1,0:T(4,128)(2,1)} %hidden.1) | copy-start | bytes 86020
  149.9 13.2 %copy-start.3 = (bf16[3584]{0:T(1024)(128)(2,1)S(1)}, bf16[3584]{0:T(1024)(128)(2,1)}, u32[]{:S(2)}) copy-start(bf16[3584]{0:T(1024)(128)(2,1)} %param.11) | copy-start | bytes 21508
  149.9 13.2 %all-to-all-start.6 = ((f32[8,2,1408]{2,1,0:T(2,128)}), f32[8,2,1408]{2,1,0:T(2,128)S(1)}, u32[]{:S(2)}, u32[]{:S(2)}) async-start(f32[8,2,1408]{2,1,0:T(2,128)} %shard_map.116), calls=%async_computation.6 | async-start | bytes 180224 | tf_op jit(solution)/shard_map/all_to_all | solution.py:35

commit v8 on v7

--- a/solution.py
+++ b/solution.py
@@ -21,7 +21,7 @@
 ANY = pl.BlockSpec(memory_space=pl.ANY)
 MIB = 2**20
 NORM = 63
-LOGITS = 10
+LOGITS = 52
 BIG = 16
 shape = jax.ShapeDtypeStruct
 
@@ -101,15 +101,23 @@
 
 
 def logits_kernel(
-    plane, t_own, s_own, s_other, t_other_at,
-    t_logits, s_logits, logs, student_rows, early_rows, late_rows, t_other, sems,
+    plane, s_own_at, s_other_at, t_own_at, t_other_at,
+    t_logits, s_logits, logs, student_rows, early_rows, late_rows,
+    s_own, s_other, t_own, t_other, sems, head_sems,
 ):
     nx, tokens, _ = plane.shape
-    rows, dt = t_own.shape
+    rows, dt = t_own_at.shape
     qt = dt // nx
-    qs = s_own.shape[1] // nx
-    late = pltpu.make_async_copy(t_other_at, t_other, sems.at[0])
-    late.start()
+    qs = s_own_at.shape[1] // nx
+    heads = (
+        (s_own_at, s_own),
+        (s_other_at, s_other),
+        (t_own_at, t_own),
+        (t_other_at, t_other),
+    )
+    heads = [pltpu.make_async_copy(a, b, head_sems.at[k]) for k, (a, b) in enumerate(heads)]
+    for copy in heads:
+        copy.start()
     back = []
     for k in range(nx):
         at = slice(k * qs, (k + 1) * qs)
@@ -126,14 +134,16 @@
                 )
             )
             back[-1].start()
-    for out, n, head, at, width in (
-        (s_logits, 0, s_own, qt, qs),
-        (s_logits, 1, s_other, qt, qs),
-        (t_logits, 0, t_own, 0, qt),
-        (t_logits, 1, t_other, 0, qt),
+    for copy, (out, n, head, at, width) in zip(
+        heads,
+        (
+            (s_logits, 0, s_own, qt, qs),
+            (s_logits, 1, s_other, qt, qs),
+            (t_logits, 0, t_own, 0, qt),
+            (t_logits, 1, t_other, 0, qt),
+        ),
     ):
-        if head is t_other:
-            late.wait()
+        copy.wait()
         total = 0.0
         for k in range(nx):
             part = plane[k, :, at : at + width]
@@ -314,21 +324,17 @@
 
     pieces, labels, cotangent, ix = lax.optimization_barrier((pieces, labels, cotangent, ix))
     label, cot = (of_tokens(labels), of_tokens(cotangent))
-    pieces, teacher_head, student_head = lax.optimization_barrier(
-        (pieces, teacher_head, student_head)
-    )
-    teacher_other, student_other = (swapped(teacher_head), swapped(student_head))
-
     line = exchanged(pieces, Z).reshape(held, qt + qs)
     place = jnp.stack([start_of(ic), start_of(1 - ic)])
-    line, place, label, cot, teacher_other, student_other = lax.optimization_barrier(
-        (line, place, label, cot, teacher_other, student_other)
-    )
+    line, place, label, cot, teacher_head, student_head = lax.optimization_barrier(
+        (line, place, label, cot, teacher_head, student_head)
+    )
+    teacher_other, student_other = (swapped(teacher_head), swapped(student_head))
     plane = to_all(line, PLANE).reshape(nx, tokens, qt + qs)
 
     t_logits, s_logits, logs, student_rows, early_rows, late_rows = called(
         logits_kernel,
-        [VMEM] * 4 + [ANY],
+        [VMEM] + [ANY] * 4,
         [VMEM] * 3 + [ANY] * 3,
         [
             shape((2 * rows, tokens), f32),
@@ -340,10 +346,14 @@
         ],
         LOGITS,
         [
+            pltpu.VMEM((rows, ds), bf16),
+            pltpu.VMEM((rows, ds), bf16),
+            pltpu.VMEM((rows, dt), bf16),
             pltpu.VMEM((rows, dt), bf16),
             pltpu.SemaphoreType.DMA((1 + 3 * nx,)),
+            pltpu.SemaphoreType.DMA((4,)),
         ],
-    )(plane, teacher_head, student_head, student_other, teacher_other)
+    )(plane, student_head, student_other, teacher_head, teacher_other)
     logs = exchanged(logs, PLANE)
     logs = called(merge_kernel, [VMEM], VMEM, shape((nz, 2, tokens), f32), 4)(logs)
     logs = exchanged(logs, Z)

time: 165 us -> 180 us (1.091)
  blocking collectives: 88.8 us -> 53.9 us
  waiting for transfers between devices: 11.8 us -> 44.5 us
  starting transfers between devices: 44.3 us -> 53.4 us
  local copies, waits for them, and re-layouts: 2.75 us -> 6.83 us
  Pallas kernels: 10.5 us -> 14.4 us
    all_to_all x4 -> x3, blocking collectives: 88.8 us -> 53.9 us  [exchanged(): return lax.all_to_all(x, axes, 0, 0, tiled=True)]
    all_to_all x3 -> x4, waiting for transfers between devices: 11.8 us -> 39.5 us  [exchanged(): return lax.all_to_all(x, axes, 0, 0, tiled=True)]
    all_to_all x3 -> x4, starting transfers between devices: 21.3 us -> 32.3 us  [exchanged(): return lax.all_to_all(x, axes, 0, 0, tiled=True)]
    ppermute x5, waiting for transfers between devices: 0.01 us -> 5.07 us  [swapped(): return lax.ppermute(x, C, [(0, 1), (1, 0)])]
    pallas_call x1, Pallas kernels: 4.1 us -> 7.96 us  [on_device(): called(logits_kernel, [VMEM] + [ANY] * 4, [VMEM] * 3 + [ANY] * 3, [shape(...]
    unnamed x8 -> x16, local copies, waits for them, and re-layouts: 0.02 us -> 2.46 us
    ppermute x5, starting transfers between devices: 23 us -> 21.1 us  [swapped(): return lax.ppermute(x, C, [(0, 1), (1, 0)])]
  transfers between devices with their start and end apart: 8 -> 9, of which waited for: 2 -> 6; matrix products, arithmetic and copies ran while one was open for 5% -> 4% of each run, Pallas kernels for 0% -> 0%
where the time goes in v8:
time: 180 us; the launch traced here: 179 us
  blocking collectives  53.9 us (30%)
  starting transfers between devices  53.4 us (30%)
  waiting for transfers between devices  44.5 us (25%)
  Pallas kernels  14.4 us (8%)
  local copies, waits for them, and re-layouts  6.83 us (4%)
  matrix products  4.96 us (3%)
    all_to_all x3, blocking collectives, exchanged(): return lax.all_to_all(x, axes, 0, 0, tiled=True)  53.9 us
    all_to_all x4, waiting for transfers between devices, exchanged(): return lax.all_to_all(x, axes, 0, 0, tiled=True)  39.5 us
    all_to_all x4, starting transfers between devices, exchanged(): return lax.all_to_all(x, axes, 0, 0, tiled=True)  32.3 us
    ppermute x5, starting transfers between devices, swapped(): return lax.ppermute(x, C, [(0, 1), (1, 0)])  21.1 us
    pallas_call x1, Pallas kernels, on_device(): called(logits_kernel, [VMEM] + [ANY] * 4, [VMEM] * 3 + [ANY] * 3, [shape(...  7.96 us
    ppermute x5, waiting for transfers between devices, swapped(): return lax.ppermute(x, C, [(0, 1), (1, 0)])  5.07 us
    dot_general x2, matrix products, dot(): lax.dot_general(a, b, (((along_a,), (along_b,)), ((), ())), preferred_ele...  4.96 us
  transfers between devices with their start and end apart: 9, of which 6 were waited for; matrix products, arithmetic and copies ran while one was open for 4% of the time, Pallas kernels for 0%

profile of v8, /device:TPU:1, one launch (start us, length us, event | category | flops | bytes accessed | tf_op | source)
XLA Modules:
  0.0 178.9 jit_solution(989738608053651717)
XLA Ops:
  0.6 1.9 %shard_map.111 = bf16[16,2,2944]{2,1,0:T(2,128)(2,1)} custom-call(s32[1]{0:T(128)} %bitcast.at_x, s32[1]{0:T(128)} %bitcast.1.at_c, bf16[4,8192]{1,0:T(4,128)(2,1)} %teacher_at.1, bf16[4,3584]{1,0:T(4,128)(2,1)} %hidden.1, bf16[64,128]{1,0:T(8,128)(2,1)} %bitcast.21, bf16[28,128]{1,0:T(8,128)(2,1)} %bitcast.19), custom_call_target="tpu_custom_call" | custom-call | tf_op jit(solution)/shard_map/pallas_call | solution.py:303
  2.6 15.8 %all-to-all-start = ((bf16[16,2,2944]{2,1,0:T(2,128)(2,1)}), bf16[16,2,2944]{2,1,0:T(2,128)(2,1)S(1)}, u32[]{:S(2)}, u32[]{:S(2)}) async-start(bf16[16,2,2944]{2,1,0:T(2,128)(2,1)} %shard_map.111), calls=%async_computation | async-start | bytes 376832 | tf_op jit(solution)/shard_map/all_to_all | solution.py:35
  18.4 0.8 reshape.45
  19.3 0.1 copy.14
  19.4 0.1 copy.15
  19.5 0.1 reshape.46.label
  19.6 0.8 reshape.47
  20.5 0.1 copy.16
  20.6 0.1 copy.17
  20.7 0.1 reshape.48.cot
  20.9 0.1 pad_add_fusion.place
  20.9 9.8 %all-to-all-done = bf16[16,2,2944]{2,1,0:T(2,128)(2,1)S(1)} async-done(((bf16[16,2,2944]{2,1,0:T(2,128)(2,1)}), bf16[16,2,2944]{2,1,0:T(2,128)(2,1)S(1)}, u32[]{:S(2)}, u32[]{:S(2)}) %all-to-all-start) | async-done | bytes 188448 | tf_op jit(solution)/shard_map/all_to_all | solution.py:35
  30.8 0.1 reshape.44
  30.9 1.8 %broadcast_in_dim.14 = bf16[16,32,2944]{2,1,0:T(8,128)(2,1)} broadcast(bf16[32,2944]{1,0:T(8,128)(2,1)S(1)} %reshape.44), dimensions={1,2} | broadcast | bytes 3203072 | tf_op jit(solution)/shard_map/broadcast_in_dim | solution.py:31
  32.7 0.0 copy-start
  32.7 6.9 %all-to-all-start.1 = ((bf16[16,32,2944]{2,1,0:T(8,128)(2,1)}), bf16[16,32,2944]{2,1,0:T(8,128)(2,1)}, u32[]{:S(2)}, u32[]{:S(2)}) async-start(bf16[16,32,2944]{2,1,0:T(8,128)(2,1)} %broadcast_in_dim.14), calls=%async_computation.1 | async-start | bytes 6029312 | tf_op jit(solution)/shard_map/all_to_all | solution.py:35
  39.6 6.9 %collective-permute-start.1 = (bf16[160,8192]{1,0:T(8,128)(2,1)}, bf16[160,8192]{1,0:T(8,128)(2,1)}, u32[]{:S(2)}, u32[]{:S(2)}) collective-permute-start(bf16[160,8192]{1,0:T(8,128)(2,1)} %t_own_at), channel_id=1, source_target_pairs={{0,64},{64,0},{1,65},{65,1},{2,66},{66,2},{3,67},{67,3},{4,68},{68... | collective-permute-start | bytes 7864328 | tf_op jit(solution)/shard_map/ppermute | solution.py:39
  46.5 0.0 copy-done
  46.5 1.9 %collective-permute-start = (bf16[160,3584]{1,0:T(8,128)(2,1)S(1)}, bf16[160,3584]{1,0:T(8,128)(2,1)S(1)}, u32[]{:S(2)}, u32[]{:S(2)}) collective-permute-start(bf16[160,3584]{1,0:T(8,128)(2,1)S(1)} %copy-done), channel_id=1, source_target_pairs={{0,64},{64,0},{1,65},{65,1},{2,66},{66,2},{3,67},{67,3},{4,68},{68... | collective-permute-start | bytes 3440648 | tf_op jit(solution)/shard_map/ppermute | solution.py:39
  48.5 4.2 %collective-permute-done.s_other_at.s_other = bf16[160,3584]{1,0:T(8,128)(2,1)S(1)} collective-permute-done((bf16[160,3584]{1,0:T(8,128)(2,1)S(1)}, bf16[160,3584]{1,0:T(8,128)(2,1)S(1)}, u32[]{:S(2)}, u32[]{:S(2)}) %collective-permute-start) | collective-permute-done | bytes 1146912 | tf_op jit(solution)/shard_map/ppermute | solution.py:39
  52.7 0.0 copy-start.2
  52.7 0.0 collective-permute-done.1.t_other_at
  52.7 20.9 %all-to-all-done.1 = bf16[16,32,2944]{2,1,0:T(8,128)(2,1)} async-done(((bf16[16,32,2944]{2,1,0:T(8,128)(2,1)}), bf16[16,32,2944]{2,1,0:T(8,128)(2,1)}, u32[]{:S(2)}, u32[]{:S(2)}) %all-to-all-start.1) | async-done | bytes 3014688 | tf_op jit(solution)/shard_map/all_to_all | solution.py:35
  73.6 0.0 copy-done.2
  73.6 0.0 copy-start.1
  73.6 8.0 %shard_map.112 = (f32[320,128]{1,0:T(8,128)S(1)}, f32[320,128]{1,0:T(8,128)S(1)}, f32[16,2,128]{2,1,0:T(2,128)S(1)}, bf16[128,3584]{1,0:T(8,128)(2,1)}, bf16[64,...) custom-call(bf16[4,128,2944]{2,1,0:T(8,128)(2,1)} %bitcast.10.plane, bf16[160,3584]{1,0:T(8,128)(2,1)} %s_own, ...), custom_call_target="tpu_custom_call" | custom-call | tf_op jit(solution)/shard_map/pallas_call | solution.py:335
  81.6 14.9 %all_to_all.35.got = f32[16,2,128]{2,1,0:T(2,128)S(1)} all-to-all(f32[16,2,128]{2,1,0:T(2,128)S(1)} %get-tuple-element.41), channel_id=1, replica_groups=mesh['section_0'=4,'section_1'=2,'dp_0'=16,'dp_1'=4] {'section_0','dp_1'}, dimensions={0} | all-to-all | bytes 32768 | tf_op jit(solution)/shard_map/all_to_all | solution.py:35
  96.5 24.1 %all_to_all.36.got = f32[16,2,128]{2,1,0:T(2,128)S(1)} all-to-all(f32[16,2,128]{2,1,0:T(2,128)S(1)} %shard_map.113), channel_id=1, replica_groups=mesh['section_0'=4,'section_1'=2,'dp_0'=16,'dp_1'=4] {'dp_0'}, dimensions={0} | all-to-all | bytes 32768 | tf_op jit(solution)/shard_map/all_to_all | solution.py:35
  120.7 0.0 copy-done.1
  120.7 0.0 copy-start.3
  120.7 1.3 copy-done.3
  121.9 0.0 copy-start.4
  121.9 1.2 copy-done.4
  123.1 2.1 %shard_map.114 = (bf16[320,128]{1,0:T(8,128)(2,1)S(1)}, bf16[4,4,32,1024]{3,2,1,0:T(8,128)(2,1)S(1)}, f32[1,128]{1,0:T(1,128)S(1)}) custom-call(s32[2]{0:T(128)S(1)} %pad_add_fusion.place, f32[16,2,128]{2,1,0:T(2,128)S(1)} %all_to_all.36.got, s32[1,128]{1,0:T(1,128)S(1)} %reshape.46.label, f32[1,128]{1,0:T(1,128)S(1)} %reshape.48.cot, ...), custom_call_target="tpu_custom_call" | custom-call | tf_op jit(solution)/shard_map/pallas_call | solution.py:361
  125.2 14.8 %all_to_all.37.got = bf16[16,32,1024]{2,1,0:T(8,128)(2,1)S(1)} all-to-all(bf16[16,32,1024]{2,1,0:T(8,128)(2,1)S(1)} %bitcast.18), channel_id=1, replica_groups=mesh['section_0'=4,'section_1'=2,'dp_0'=16,'dp_1'=4] {'section_0','dp_1'}, dimensions={0} | all-to-all | bytes 2097152 | tf_op jit(solution)/shard_map/all_to_all | solution.py:35
  140.0 0.0 copy-start.5
  140.1 0.8 shard_map.115
  140.9 7.9 %collective-permute-start.3 = (bf16[64,3584]{1,0:T(8,128)(2,1)S(1)}, bf16[64,3584]{1,0:T(8,128)(2,1)S(1)}, u32[]{:S(2)}, u32[]{:S(2)}) collective-permute-start(bf16[64,3584]{1,0:T(8,128)(2,1)S(1)} %get-tuple-element.55), channel_id=1, source_target_pairs={{0,64},{64,0},{1,65},{65,1},{2,66},{66,2},{3,67},{67,3},{4,68},{68... | collective-permute-start | bytes 1376264 | tf_op jit(solution)/shard_map/ppermute | solution.py:39
  148.8 1.9 %collective-permute-start.4 = (bf16[64,3584]{1,0:T(8,128)(2,1)S(1)}, bf16[64,3584]{1,0:T(8,128)(2,1)S(1)}, u32[]{:S(2)}, u32[]{:S(2)}) collective-permute-start(bf16[64,3584]{1,0:T(8,128)(2,1)S(1)} %get-tuple-element.56), channel_id=1, source_target_pairs={{0,64},{64,0},{1,65},{65,1},{2,66},{66,2},{3,67},{67,3},{4,68},{68... | collective-permute-start | bytes 1376264 | tf_op jit(solution)/shard_map/ppermute | solution.py:39
  150.8 3.5 %all-to-all-start.5 = ((bf16[16,2,1920]{2,1,0:T(2,128)(2,1)}), bf16[16,2,1920]{2,1,0:T(2,128)(2,1)S(1)}, u32[]{:S(2)}, u32[]{:S(2)}) async-start(bf16[16,2,1920]{2,1,0:T(2,128)(2,1)} %shard_map.115), calls=%async_computation.5 | async-start | bytes 245760 | tf_op jit(solution)/shard_map/all_to_all | solution.py:35
  154.3 2.4 %collective-permute-start.2 = (bf16[160,128]{1,0:T(8,128)(2,1)S(1)}, bf16[160,128]{1,0:T(8,128)(2,1)S(1)}, u32[]{:S(2)}, u32[]{:S(2)}) collective-permute-start(bf16[160,128]{1,0:T(8,128)(2,1)S(1)} %slice.7), channel_id=1, source_target_pairs={{0,64},{64,0},{1,65},{65,1},{2,66},{66,2},{3,67},{67,3},{4,68},{68... | collective-permute-start | bytes 122888 | tf_op jit(solution)/shard_map/ppermute | solution.py:39
  156.7 0.8 collective-permute-done.2
  157.5 0.0 collective-permute-done.3
  157.6 0.0 collective-permute-done.4
  157.6 1.9 %fusion.1 = f32[160,3584]{1,0:T(8,128)} fusion(bf16[160,128]{1,0:T(8,128)(2,1)S(1)} %collective-permute-done.2, bf16[64,3584]{1,0:T(8,128)(2,1)S(1)} %collective-permute-done.4, bf16[64,3584]{1,0:T(8,128)(2,1)S(1)} %collective-permute-done.3), kind=kOutput, calls=%fused_computation.2 | convolution fusion | flops 148635648 | bytes 3252224 | tf_op jit(solution)/shard_map/dot_general | solution.py:43
  159.4 6.9 %all-to-all-done.5.got = bf16[16,2,1920]{2,1,0:T(2,128)(2,1)S(1)} async-done(((bf16[16,2,1920]{2,1,0:T(2,128)(2,1)}), bf16[16,2,1920]{2,1,0:T(2,128)(2,1)S(1)}, u32[]{:S(2)}, u32[]{:S(2)}) %all-to-all-start.5) | async-done | bytes 122912 | tf_op jit(solution)/shard_map/all_to_all | solution.py:35
  166.3 0.7 shard_map.116
  166.9 0.0 copy-start.6
  166.9 0.0 copy-start.7
  166.9 6.1 %all-to-all-start.6 = ((f32[8,2,1408]{2,1,0:T(2,128)}), f32[8,2,1408]{2,1,0:T(2,128)S(1)}, u32[]{:S(2)}, u32[]{:S(2)}) async-start(f32[8,2,1408]{2,1,0:T(2,128)} %shard_map.116), calls=%async_computation.6 | async-start | bytes 180224 | tf_op jit(solution)/shard_map/all_to_all | solution.py:35
  173.0 0.0 copy-done.5
  173.0 3.1 %fusion = bf16[160,3584]{1,0:T(8,128)(2,1)} fusion(f32[160,3584]{1,0:T(8,128)} %fusion.1, bf16[128,3584]{1,0:T(8,128)(2,1)S(1)} %copy-done.5, bf16[320,128]{1,0:T(8,128)(2,1)S(1)} %get-tuple-element.51), kind=kOutput, calls=%fused_computation.1 | convolution fusion | flops 147947520 | bytes 4399104 | tf_op jit(solution)/shard_map/dot_general | solution.py:43
  176.1 1.9 %all-to-all-done.6.got = f32[8,2,1408]{2,1,0:T(2,128)S(1)} async-done(((f32[8,2,1408]{2,1,0:T(2,128)}), f32[8,2,1408]{2,1,0:T(2,128)S(1)}, u32[]{:S(2)}, u32[]{:S(2)}) %all-to-all-start.6) | async-done | bytes 90144 | tf_op jit(solution)/shard_map/all_to_all | solution.py:35
  178.0 0.0 copy-done.6
  178.0 0.0 copy-done.7
  178.0 0.9 shard_map.117
  (4 shorter events, 0.1 us)
Async XLA Ops:
  2.6 28.2 %all-to-all-start = ((bf16[16,2,2944]{2,1,0:T(2,128)(2,1)}), bf16[16,2,2944]{2,1,0:T(2,128)(2,1)S(1)}, u32[]{:S(2)}, u32[]{:S(2)}) async-start(bf16[16,2,2944]{2,1,0:T(2,128)(2,1)} %shard_map.111), calls=%async_computation | async-start | bytes 376832 | tf_op jit(solution)/shard_map/all_to_all | solution.py:35
  32.7 13.8 %copy-start = (bf16[160,3584]{1,0:T(8,128)(2,1)S(1)}, bf16[160,3584]{1,0:T(8,128)(2,1)}, u32[]{:S(2)}) copy-start(bf16[160,3584]{1,0:T(8,128)(2,1)} %s_own) | copy-start | bytes 3440644
  32.7 40.9 %all-to-all-start.1 = ((bf16[16,32,2944]{2,1,0:T(8,128)(2,1)}), bf16[16,32,2944]{2,1,0:T(8,128)(2,1)}, u32[]{:S(2)}, u32[]{:S(2)}) async-start(bf16[16,32,2944]{2,1,0:T(8,128)(2,1)} %broadcast_in_dim.14), calls=%async_computation.1 | async-start | bytes 6029312 | tf_op jit(solution)/shard_map/all_to_all | solution.py:35
  39.6 13.1 %collective-permute-start.1 = (bf16[160,8192]{1,0:T(8,128)(2,1)}, bf16[160,8192]{1,0:T(8,128)(2,1)}, u32[]{:S(2)}, u32[]{:S(2)}) collective-permute-start(bf16[160,8192]{1,0:T(8,128)(2,1)} %t_own_at), channel_id=1, source_target_pairs={{0,64},{64,0},{1,65},{65,1},{2,66},{66,2},{3,67},{67,3},{4,68},{68... | collective-permute-start | bytes 7864328 | tf_op jit(solution)/shard_map/ppermute | solution.py:39
  46.5 6.1 %collective-permute-start = (bf16[160,3584]{1,0:T(8,128)(2,1)S(1)}, bf16[160,3584]{1,0:T(8,128)(2,1)S(1)}, u32[]{:S(2)}, u32[]{:S(2)}) collective-permute-start(bf16[160,3584]{1,0:T(8,128)(2,1)S(1)} %copy-done), channel_id=1, source_target_pairs={{0,64},{64,0},{1,65},{65,1},{2,66},{66,2},{3,67},{67,3},{4,68},{68... | collective-permute-start | bytes 3440648 | tf_op jit(solution)/shard_map/ppermute | solution.py:39
  52.7 20.9 %copy-start.2 = (bf16[160,3584]{1,0:T(8,128)(2,1)}, bf16[160,3584]{1,0:T(8,128)(2,1)S(1)}, u32[]{:S(2)}) copy-start(bf16[160,3584]{1,0:T(8,128)(2,1)S(1)} %collective-permute-done.s_other_at.s_other) | copy-start | bytes 3440644
  73.6 47.1 %copy-start.1 = (bf16[160,3584]{1,0:T(8,128)(2,1)S(1)}, bf16[160,3584]{1,0:T(8,128)(2,1)}, u32[]{:S(2)}) copy-start(bf16[160,3584]{1,0:T(8,128)(2,1)} %s_own) | copy-start | bytes 3440644
  120.7 1.3 copy-start.3
  121.9 1.2 copy-start.4
  140.0 33.0 %copy-start.5 = (bf16[128,3584]{1,0:T(8,128)(2,1)S(1)}, bf16[128,3584]{1,0:T(8,128)(2,1)}, u32[]{:S(2)}) copy-start(bf16[128,3584]{1,0:T(8,128)(2,1)} %get-tuple-element.46.s_rows_at) | copy-start | bytes 2752516
  140.9 16.7 %collective-permute-start.3 = (bf16[64,3584]{1,0:T(8,128)(2,1)S(1)}, bf16[64,3584]{1,0:T(8,128)(2,1)S(1)}, u32[]{:S(2)}, u32[]{:S(2)}) collective-permute-start(bf16[64,3584]{1,0:T(8,128)(2,1)S(1)} %get-tuple-element.55), channel_id=1, source_target_pairs={{0,64},{64,0},{1,65},{65,1},{2,66},{66,2},{3,67},{67,3},{4,68},{68... | collective-permute-start | bytes 1376264 | tf_op jit(solution)/shard_map/ppermute | solution.py:39
  148.8 8.7 %collective-permute-start.4 = (bf16[64,3584]{1,0:T(8,128)(2,1)S(1)}, bf16[64,3584]{1,0:T(8,128)(2,1)S(1)}, u32[]{:S(2)}, u32[]{:S(2)}) collective-permute-start(bf16[64,3584]{1,0:T(8,128)(2,1)S(1)} %get-tuple-element.56), channel_id=1, source_target_pairs={{0,64},{64,0},{1,65},{65,1},{2,66},{66,2},{3,67},{67,3},{4,68},{68... | collective-permute-start | bytes 1376264 | tf_op jit(solution)/shard_map/ppermute | solution.py:39
  150.8 15.5 %all-to-all-start.5 = ((bf16[16,2,1920]{2,1,0:T(2,128)(2,1)}), bf16[16,2,1920]{2,1,0:T(2,128)(2,1)S(1)}, u32[]{:S(2)}, u32[]{:S(2)}) async-start(bf16[16,2,1920]{2,1,0:T(2,128)(2,1)} %shard_map.115), calls=%async_computation.5 | async-start | bytes 245760 | tf_op jit(solution)/shard_map/all_to_all | solution.py:35
  154.3 3.3 %collective-permute-start.2 = (bf16[160,128]{1,0:T(8,128)(2,1)S(1)}, bf16[160,128]{1,0:T(8,128)(2,1)S(1)}, u32[]{:S(2)}, u32[]{:S(2)}) collective-permute-start(bf16[160,128]{1,0:T(8,128)(2,1)S(1)} %slice.7), channel_id=1, source_target_pairs={{0,64},{64,0},{1,65},{65,1},{2,66},{66,2},{3,67},{67,3},{4,68},{68... | collective-permute-start | bytes 122888 | tf_op jit(solution)/shard_map/ppermute | solution.py:39
  166.9 11.1 %copy-start.6 = (bf16[4,3584]{1,0:T(4,128)(2,1)S(1)}, bf16[4,3584]{1,0:T(4,128)(2,1)}, u32[]{:S(2)}) copy-start(bf16[4,3584]{1,0:T(4,128)(2,1)} %hidden.1) | copy-start | bytes 86020
  166.9 11.1 %copy-start.7 = (bf16[3584]{0:T(1024)(128)(2,1)S(1)}, bf16[3584]{0:T(1024)(128)(2,1)}, u32[]{:S(2)}) copy-start(bf16[3584]{0:T(1024)(128)(2,1)} %param.11) | copy-start | bytes 21508
  166.9 11.0 %all-to-all-start.6 = ((f32[8,2,1408]{2,1,0:T(2,128)}), f32[8,2,1408]{2,1,0:T(2,128)S(1)}, u32[]{:S(2)}, u32[]{:S(2)}) async-start(f32[8,2,1408]{2,1,0:T(2,128)} %shard_map.116), calls=%async_computation.6 | async-start | bytes 180224 | tf_op jit(solution)/shard_map/all_to_all | solution.py:35

commit v9 on v7

--- a/solution.py
+++ b/solution.py
@@ -102,36 +102,29 @@
 
 def logits_kernel(
     plane, t_own, s_own, s_other, t_other_at,
-    t_logits, s_logits, logs, student_rows, early_rows, late_rows, t_other, sems,
+    t_logits, s_logits, logs, student_rows, t_other, sems,
 ):
-    nx, tokens, _ = plane.shape
+    nx = plane.shape[0]
     rows, dt = t_own.shape
     qt = dt // nx
     qs = s_own.shape[1] // nx
     late = pltpu.make_async_copy(t_other_at, t_other, sems.at[0])
     late.start()
-    back = []
-    for k in range(nx):
-        at = slice(k * qs, (k + 1) * qs)
-        for n, (target, first, last) in enumerate(
-            (
-                (student_rows, 0, tokens),
-                (early_rows, 0, tokens // 2),
-                (late_rows, tokens // 2, tokens),
-            )
-        ):
-            back.append(
-                pltpu.make_async_copy(
-                    plane.at[k, first:last, qt:], target.at[:, at], sems.at[1 + 3 * k + n]
-                )
-            )
-            back[-1].start()
+    back = [
+        pltpu.make_async_copy(
+            plane.at[k, :, qt:], student_rows.at[:, k * qs : (k + 1) * qs], sems.at[1 + k]
+        )
+        for k in range(nx)
+    ]
     for out, n, head, at, width in (
         (s_logits, 0, s_own, qt, qs),
         (s_logits, 1, s_other, qt, qs),
         (t_logits, 0, t_own, 0, qt),
         (t_logits, 1, t_other, 0, qt),
     ):
+        if head is t_own:
+            for copy in back:
+                copy.start()
         if head is t_other:
             late.wait()
         total = 0.0
@@ -326,22 +319,20 @@
     )
     plane = to_all(line, PLANE).reshape(nx, tokens, qt + qs)
 
-    t_logits, s_logits, logs, student_rows, early_rows, late_rows = called(
+    t_logits, s_logits, logs, student_rows = called(
         logits_kernel,
         [VMEM] * 4 + [ANY],
-        [VMEM] * 3 + [ANY] * 3,
+        [VMEM] * 3 + [ANY],
         [
             shape((2 * rows, tokens), f32),
             shape((2 * rows, tokens), f32),
             shape((nx * ny, 2, tokens), f32),
             shape((tokens, ds), bf16),
-            shape((tokens // 2, ds), bf16),
-            shape((tokens // 2, ds), bf16),
         ],
         LOGITS,
         [
             pltpu.VMEM((rows, dt), bf16),
-            pltpu.SemaphoreType.DMA((1 + 3 * nx,)),
+            pltpu.SemaphoreType.DMA((1 + nx,)),
         ],
     )(plane, teacher_head, student_head, student_other, teacher_other)
     logs = exchanged(logs, PLANE)
@@ -368,10 +359,9 @@
     got = called(repack_kernel, [VMEM], VMEM, shape((nz, half, qs + 1024), bf16), 8)(got)
     got, slope = lax.optimization_barrier((got, slope))
     got = exchanged(got, Z)
-    slope_other, early_rows, late_rows = lax.optimization_barrier(
-        (slope[rows:], early_rows, late_rows)
-    )
-    rows_other = jnp.concatenate([swapped(early_rows), swapped(late_rows)])
+    slope_other, student_rows = lax.optimization_barrier((slope[rows:], student_rows))
+    cut = tokens // 2
+    rows_other = jnp.concatenate([swapped(student_rows[:cut]), swapped(student_rows[cut:])])
 
     head_grad = (
         dot(slope[:rows], student_rows, 1, 0)

time: 165 us -> 165 us (level)
  no operation moved by 1% of the time
where the time goes in v9:
time: 165 us; the launch traced here: 164 us
  blocking collectives  88.8 us (54%)
  starting transfers between devices  44.2 us (27%)
  waiting for transfers between devices  11.8 us (7%)
  Pallas kernels  10.5 us (6%)
  matrix products  4.95 us (3%)
  local copies, waits for them, and re-layouts  2.81 us (2%)
    all_to_all x4, blocking collectives, exchanged(): return lax.all_to_all(x, axes, 0, 0, tiled=True)  88.8 us
    ppermute x5, starting transfers between devices, swapped(): return lax.ppermute(x, C, [(0, 1), (1, 0)])  23 us
    all_to_all x3, starting transfers between devices, exchanged(): return lax.all_to_all(x, axes, 0, 0, tiled=True)  21.2 us
    all_to_all x3, waiting for transfers between devices, exchanged(): return lax.all_to_all(x, axes, 0, 0, tiled=True)  11.8 us
    dot_general x2, matrix products, dot(): lax.dot_general(a, b, (((along_a,), (along_b,)), ((), ())), preferred_ele...  4.95 us
    pallas_call x1, Pallas kernels, on_device(): called(logits_kernel, [VMEM] * 4 + [ANY], [VMEM] * 3 + [ANY], [shape((2 *...  4.03 us
  transfers between devices with their start and end apart: 8, of which 2 were waited for; matrix products, arithmetic and copies ran while one was open for 5% of the time, Pallas kernels for 0%

profile of v9, /device:TPU:1, one launch (start us, length us, event | category | flops | bytes accessed | tf_op | source)
XLA Modules:
  0.0 163.9 jit_solution(4315191087878912802)
XLA Ops:
  0.6 1.9 %shard_map.111 = bf16[16,2,2944]{2,1,0:T(2,128)(2,1)} custom-call(s32[1]{0:T(128)} %bitcast.at_x, s32[1]{0:T(128)} %bitcast.1.at_c, bf16[4,8192]{1,0:T(4,128)(2,1)} %teacher_at.1, bf16[4,3584]{1,0:T(4,128)(2,1)} %hidden.1, bf16[64,128]{1,0:T(8,128)(2,1)} %bitcast.22, bf16[28,128]{1,0:T(8,128)(2,1)} %bitcast.20), custom_call_target="tpu_custom_call" | custom-call | tf_op jit(solution)/shard_map/pallas_call | solution.py:286
  2.6 8.8 %collective-permute-start = (bf16[160,8192]{1,0:T(8,128)(2,1)}, bf16[160,8192]{1,0:T(8,128)(2,1)}, u32[]{:S(2)}, u32[]{:S(2)}) collective-permute-start(bf16[160,8192]{1,0:T(8,128)(2,1)} %t_own), channel_id=1, source_target_pairs={{0,64},{64,0},{1,65},{65,1},{2,66},{66,2},{3,67},{67,3},{4,68},{68... | collective-permute-start | bytes 7864328 | tf_op jit(solution)/shard_map/ppermute | solution.py:39
  11.4 1.9 %collective-permute-start.1 = (bf16[160,3584]{1,0:T(8,128)(2,1)}, bf16[160,3584]{1,0:T(8,128)(2,1)S(1)}, u32[]{:S(2)}, u32[]{:S(2)}) collective-permute-start(bf16[160,3584]{1,0:T(8,128)(2,1)} %s_own.1), channel_id=1, source_target_pairs={{0,64},{64,0},{1,65},{65,1},{2,66},{66,2},{3,67},{67,3},{4,68},{68... | collective-permute-start | bytes 3440648 | tf_op jit(solution)/shard_map/ppermute | solution.py:39
  13.3 9.6 %all-to-all-start = ((bf16[16,2,2944]{2,1,0:T(2,128)(2,1)}), bf16[16,2,2944]{2,1,0:T(2,128)(2,1)S(1)}, u32[]{:S(2)}, u32[]{:S(2)}) async-start(bf16[16,2,2944]{2,1,0:T(2,128)(2,1)} %shard_map.111), calls=%async_computation | async-start | bytes 376832 | tf_op jit(solution)/shard_map/all_to_all | solution.py:35
  22.9 0.8 reshape.45
  23.8 0.1 copy.14
  23.9 0.1 copy.15
  24.0 0.1 reshape.46.label
  24.1 0.8 reshape.47
  25.0 0.1 copy.16
  25.1 0.1 copy.17
  25.2 0.1 reshape.48.cot
  25.4 0.1 pad_add_fusion.place
  25.5 9.9 %all-to-all-done = bf16[16,2,2944]{2,1,0:T(2,128)(2,1)S(1)} async-done(((bf16[16,2,2944]{2,1,0:T(2,128)(2,1)}), bf16[16,2,2944]{2,1,0:T(2,128)(2,1)S(1)}, u32[]{:S(2)}, u32[]{:S(2)}) %all-to-all-start) | async-done | bytes 188448 | tf_op jit(solution)/shard_map/all_to_all | solution.py:35
  35.4 0.1 reshape.44
  35.5 0.0 collective-permute-done.1.s_other
  35.5 0.0 collective-permute-done.t_other_at
  35.5 0.2 broadcast_in_dim.14
  35.7 0.0 copy-start
  35.7 0.0 copy-start.1
  35.7 39.2 %all_to_all.35 = bf16[16,32,2944]{2,1,0:T(8,128)(2,1)S(1)} all-to-all(bf16[16,32,2944]{2,1,0:T(8,128)(2,1)S(1)} %broadcast_in_dim.14), channel_id=1, replica_groups=mesh['section_0'=4,'section_1'=2,'dp_0'=16,'dp_1'=4] {'section_0','dp_1'}, dimensions={0} | all-to-all | bytes 6029312 | tf_op jit(solution)/shard_map/all_to_all | solution.py:35
  74.9 0.0 copy-done
  74.9 0.0 copy-done.1
  74.9 4.0 %shard_map.112 = (f32[320,128]{1,0:T(8,128)S(1)}, f32[320,128]{1,0:T(8,128)S(1)}, f32[16,2,128]{2,1,0:T(2,128)S(1)}, bf16[128,3584]{1,0:T(8,128)(2,1)S(1)}) custom-call(bf16[4,128,2944]{2,1,0:T(8,128)(2,1)S(1)} %bitcast.18, bf16[160,8192]{1,0:T(8,128)(2,1)S(1)} %copy-done.1, bf16[160,3584]{1,0:T(8,128)(2,1)S(1)} %copy-done, ...), custom_call_target="tpu_custom_call" | custom-call | tf_op jit(solution)/shard_map/pallas_call | solution.py:322
  79.0 10.5 %all_to_all.36.got = f32[16,2,128]{2,1,0:T(2,128)S(1)} all-to-all(f32[16,2,128]{2,1,0:T(2,128)S(1)} %get-tuple-element.44), channel_id=1, replica_groups=mesh['section_0'=4,'section_1'=2,'dp_0'=16,'dp_1'=4] {'section_0','dp_1'}, dimensions={0} | all-to-all | bytes 32768 | tf_op jit(solution)/shard_map/all_to_all | solution.py:35
  89.5 24.0 %all_to_all.37.got = f32[16,2,128]{2,1,0:T(2,128)S(1)} all-to-all(f32[16,2,128]{2,1,0:T(2,128)S(1)} %shard_map.113), channel_id=1, replica_groups=mesh['section_0'=4,'section_1'=2,'dp_0'=16,'dp_1'=4] {'dp_0'}, dimensions={0} | all-to-all | bytes 32768 | tf_op jit(solution)/shard_map/all_to_all | solution.py:35
  113.5 2.1 %shard_map.114 = (bf16[320,128]{1,0:T(8,128)(2,1)S(1)}, bf16[4,4,32,1024]{3,2,1,0:T(8,128)(2,1)S(1)}, f32[1,128]{1,0:T(1,128)S(1)}) custom-call(s32[2]{0:T(128)S(1)} %pad_add_fusion.place, f32[16,2,128]{2,1,0:T(2,128)S(1)} %all_to_all.37.got, s32[1,128]{1,0:T(1,128)S(1)} %reshape.46.label, f32[1,128]{1,0:T(1,128)S(1)} %reshape.48.cot, ...), custom_call_target="tpu_custom_call" | custom-call | tf_op jit(solution)/shard_map/pallas_call | solution.py:342
  115.6 15.1 %all_to_all.38.got = bf16[16,32,1024]{2,1,0:T(8,128)(2,1)S(1)} all-to-all(bf16[16,32,1024]{2,1,0:T(8,128)(2,1)S(1)} %bitcast.19), channel_id=1, replica_groups=mesh['section_0'=4,'section_1'=2,'dp_0'=16,'dp_1'=4] {'section_0','dp_1'}, dimensions={0} | all-to-all | bytes 2097152 | tf_op jit(solution)/shard_map/all_to_all | solution.py:35
  130.7 0.8 shard_map.115
  131.5 3.5 %all-to-all-start.5 = ((bf16[16,2,1920]{2,1,0:T(2,128)(2,1)}), bf16[16,2,1920]{2,1,0:T(2,128)(2,1)S(1)}, u32[]{:S(2)}, u32[]{:S(2)}) async-start(bf16[16,2,1920]{2,1,0:T(2,128)(2,1)} %shard_map.115), calls=%async_computation.5 | async-start | bytes 245760 | tf_op jit(solution)/shard_map/all_to_all | solution.py:35
  135.0 0.1 fusion.7
  135.1 7.9 %collective-permute-start.3 = (bf16[64,3584]{1,0:T(8,128)(2,1)S(1)}, bf16[64,3584]{1,0:T(8,128)(2,1)S(1)}, u32[]{:S(2)}, u32[]{:S(2)}) collective-permute-start(bf16[64,3584]{1,0:T(8,128)(2,1)S(1)} %get-tuple-element.62), channel_id=1, source_target_pairs={{0,64},{64,0},{1,65},{65,1},{2,66},{66,2},{3,67},{67,3},{4,68},{68... | collective-permute-start | bytes 1376264 | tf_op jit(solution)/shard_map/ppermute | solution.py:39
  143.0 1.9 %collective-permute-start.4 = (bf16[64,3584]{1,0:T(8,128)(2,1)S(1)}, bf16[64,3584]{1,0:T(8,128)(2,1)S(1)}, u32[]{:S(2)}, u32[]{:S(2)}) collective-permute-start(bf16[64,3584]{1,0:T(8,128)(2,1)S(1)} %get-tuple-element.63), channel_id=1, source_target_pairs={{0,64},{64,0},{1,65},{65,1},{2,66},{66,2},{3,67},{67,3},{4,68},{68... | collective-permute-start | bytes 1376264 | tf_op jit(solution)/shard_map/ppermute | solution.py:39
  145.0 2.4 %collective-permute-start.2 = (bf16[160,128]{1,0:T(8,128)(2,1)S(1)}, bf16[160,128]{1,0:T(8,128)(2,1)S(1)}, u32[]{:S(2)}, u32[]{:S(2)}) collective-permute-start(bf16[160,128]{1,0:T(8,128)(2,1)S(1)} %slice.13), channel_id=1, source_target_pairs={{0,64},{64,0},{1,65},{65,1},{2,66},{66,2},{3,67},{67,3},{4,68},{68... | collective-permute-start | bytes 122888 | tf_op jit(solution)/shard_map/ppermute | solution.py:39
  147.4 1.9 %fusion.4 = f32[160,3584]{1,0:T(8,128)} fusion(bf16[128,3584]{1,0:T(8,128)(2,1)S(1)} %get-tuple-element.55.s_rows_at, bf16[320,128]{1,0:T(8,128)(2,1)S(1)} %get-tuple-element.54), kind=kOutput, calls=%fused_computation.5 | convolution fusion | flops 146800640 | bytes 3252224 | tf_op jit(solution)/shard_map/dot_general | solution.py:43
  149.2 0.0 all-to-all-done.5.got
  149.2 0.7 shard_map.116
  149.9 0.0 copy-start.2
  149.9 0.0 copy-start.3
  149.9 8.2 %all-to-all-start.6 = ((f32[8,2,1408]{2,1,0:T(2,128)}), f32[8,2,1408]{2,1,0:T(2,128)S(1)}, u32[]{:S(2)}, u32[]{:S(2)}) async-start(f32[8,2,1408]{2,1,0:T(2,128)} %shard_map.116), calls=%async_computation.6 | async-start | bytes 180224 | tf_op jit(solution)/shard_map/all_to_all | solution.py:35
  158.1 0.0 collective-permute-done.2
  158.1 0.0 collective-permute-done.3
  158.1 0.0 collective-permute-done.4
  158.1 3.1 %fusion = bf16[160,3584]{1,0:T(8,128)(2,1)} fusion(f32[160,3584]{1,0:T(8,128)} %fusion.4, bf16[160,128]{1,0:T(8,128)(2,1)S(1)} %collective-permute-done.2, bf16[64,3584]{1,0:T(8,128)(2,1)S(1)} %collective-permute-done.4, bf16[64,3584]{1,0:T(8,128)(2,1)S(1)} %collective-permute-done.3), kind=kOutput, calls=%fused_computation.1 | convolution fusion | flops 149782528 | bytes 4399104 | tf_op jit(solution)/shard_map/dot_general | solution.py:43
  161.2 1.8 %all-to-all-done.6.got = f32[8,2,1408]{2,1,0:T(2,128)S(1)} async-done(((f32[8,2,1408]{2,1,0:T(2,128)}), f32[8,2,1408]{2,1,0:T(2,128)S(1)}, u32[]{:S(2)}, u32[]{:S(2)}) %all-to-all-start.6) | async-done | bytes 90144 | tf_op jit(solution)/shard_map/all_to_all | solution.py:35
  163.1 0.0 copy-done.2
  163.1 0.0 copy-done.3
  163.1 0.9 shard_map.117
  (4 shorter events, 0.1 us)
Async XLA Ops:
  2.6 32.9 %collective-permute-start = (bf16[160,8192]{1,0:T(8,128)(2,1)}, bf16[160,8192]{1,0:T(8,128)(2,1)}, u32[]{:S(2)}, u32[]{:S(2)}) collective-permute-start(bf16[160,8192]{1,0:T(8,128)(2,1)} %t_own), channel_id=1, source_target_pairs={{0,64},{64,0},{1,65},{65,1},{2,66},{66,2},{3,67},{67,3},{4,68},{68... | collective-permute-start | bytes 7864328 | tf_op jit(solution)/shard_map/ppermute | solution.py:39
  11.4 24.1 %collective-permute-start.1 = (bf16[160,3584]{1,0:T(8,128)(2,1)}, bf16[160,3584]{1,0:T(8,128)(2,1)S(1)}, u32[]{:S(2)}, u32[]{:S(2)}) collective-permute-start(bf16[160,3584]{1,0:T(8,128)(2,1)} %s_own.1), channel_id=1, source_target_pairs={{0,64},{64,0},{1,65},{65,1},{2,66},{66,2},{3,67},{67,3},{4,68},{68... | collective-permute-start | bytes 3440648 | tf_op jit(solution)/shard_map/ppermute | solution.py:39
  13.3 22.1 %all-to-all-start = ((bf16[16,2,2944]{2,1,0:T(2,128)(2,1)}), bf16[16,2,2944]{2,1,0:T(2,128)(2,1)S(1)}, u32[]{:S(2)}, u32[]{:S(2)}) async-start(bf16[16,2,2944]{2,1,0:T(2,128)(2,1)} %shard_map.111), calls=%async_computation | async-start | bytes 376832 | tf_op jit(solution)/shard_map/all_to_all | solution.py:35
  35.7 39.2 %copy-start = (bf16[160,3584]{1,0:T(8,128)(2,1)S(1)}, bf16[160,3584]{1,0:T(8,128)(2,1)}, u32[]{:S(2)}) copy-start(bf16[160,3584]{1,0:T(8,128)(2,1)} %s_own.1) | copy-start | bytes 3440644
  35.7 39.2 %copy-start.1 = (bf16[160,8192]{1,0:T(8,128)(2,1)S(1)}, bf16[160,8192]{1,0:T(8,128)(2,1)}, u32[]{:S(2)}) copy-start(bf16[160,8192]{1,0:T(8,128)(2,1)} %t_own) | copy-start | bytes 7864324
  131.5 17.7 %all-to-all-start.5 = ((bf16[16,2,1920]{2,1,0:T(2,128)(2,1)}), bf16[16,2,1920]{2,1,0:T(2,128)(2,1)S(1)}, u32[]{:S(2)}, u32[]{:S(2)}) async-start(bf16[16,2,1920]{2,1,0:T(2,128)(2,1)} %shard_map.115), calls=%async_computation.5 | async-start | bytes 245760 | tf_op jit(solution)/shard_map/all_to_all | solution.py:35
  135.1 23.0 %collective-permute-start.3 = (bf16[64,3584]{1,0:T(8,128)(2,1)S(1)}, bf16[64,3584]{1,0:T(8,128)(2,1)S(1)}, u32[]{:S(2)}, u32[]{:S(2)}) collective-permute-start(bf16[64,3584]{1,0:T(8,128)(2,1)S(1)} %get-tuple-element.62), channel_id=1, source_target_pairs={{0,64},{64,0},{1,65},{65,1},{2,66},{66,2},{3,67},{67,3},{4,68},{68... | collective-permute-start | bytes 1376264 | tf_op jit(solution)/shard_map/ppermute | solution.py:39
  143.0 15.1 %collective-permute-start.4 = (bf16[64,3584]{1,0:T(8,128)(2,1)S(1)}, bf16[64,3584]{1,0:T(8,128)(2,1)S(1)}, u32[]{:S(2)}, u32[]{:S(2)}) collective-permute-start(bf16[64,3584]{1,0:T(8,128)(2,1)S(1)} %get-tuple-element.63), channel_id=1, source_target_pairs={{0,64},{64,0},{1,65},{65,1},{2,66},{66,2},{3,67},{67,3},{4,68},{68... | collective-permute-start | bytes 1376264 | tf_op jit(solution)/shard_map/ppermute | solution.py:39
  145.0 13.1 %collective-permute-start.2 = (bf16[160,128]{1,0:T(8,128)(2,1)S(1)}, bf16[160,128]{1,0:T(8,128)(2,1)S(1)}, u32[]{:S(2)}, u32[]{:S(2)}) collective-permute-start(bf16[160,128]{1,0:T(8,128)(2,1)S(1)} %slice.13), channel_id=1, source_target_pairs={{0,64},{64,0},{1,65},{65,1},{2,66},{66,2},{3,67},{67,3},{4,68},{68... | collective-permute-start | bytes 122888 | tf_op jit(solution)/shard_map/ppermute | solution.py:39
  149.9 13.2 %copy-start.2 = (bf16[4,3584]{1,0:T(4,128)(2,1)S(1)}, bf16[4,3584]{1,0:T(4,128)(2,1)}, u32[]{:S(2)}) copy-start(bf16[4,3584]{1,0:T(4,128)(2,1)} %hidden.1) | copy-start | bytes 86020
  149.9 13.2 %copy-start.3 = (bf16[3584]{0:T(1024)(128)(2,1)S(1)}, bf16[3584]{0:T(1024)(128)(2,1)}, u32[]{:S(2)}) copy-start(bf16[3584]{0:T(1024)(128)(2,1)} %param.11) | copy-start | bytes 21508
  149.9 13.2 %all-to-all-start.6 = ((f32[8,2,1408]{2,1,0:T(2,128)}), f32[8,2,1408]{2,1,0:T(2,128)S(1)}, u32[]{:S(2)}, u32[]{:S(2)}) async-start(f32[8,2,1408]{2,1,0:T(2,128)} %shard_map.116), calls=%async_computation.6 | async-start | bytes 180224 | tf_op jit(solution)/shard_map/all_to_all | solution.py:35
